TPU v7x, 32 devices: a whole 2x2x4 slice. The times are simulated.
32 devices in a mesh: groups: 2 (over y), chan: 4 (over z), img: 4 (over x, core).
Axes of the slice: x: 2, y: 2, z: 4, core: 2. Of those that a mesh axis runs over, the one named last changes fastest.
Arguments:
- features: bfloat16 [8, 16, 16, 2048], P(('groups', 'img'), None, None, 'chan'), parts along dimension 0, may hold values from -6 to 6
- kernel_one: bfloat16 [3, 3, 2048, 2048], P(None, None, 'img', 'chan'), may hold values from -0.046875 to 0.046875
- kernel_two: bfloat16 [3, 3, 2048, 2048], P(None, None, 'img', 'chan'), may hold values from -0.046875 to 0.046875
Outputs:
- second_out: bfloat16 [8, 16, 16, 2048], P(('groups', 'img'), None, None, 'chan'), parts along dimension 0
There are 2 independent parts, one for each index of `groups`. A program takes and returns all parts, laid end to end along the dimension named above; an argument that names none is the same for every part. Nothing has to cross between parts.
All inputs are finite; a program needn't handle non-finite values.
Results may differ from a plain program's by a relative error of at most 0.005.
Values may be sent and summed in bfloat16 or wider, within the bound.
No kernel may reach another device: no remote copies, remote signals or barrier semaphores. Data moves between devices by JAX's collectives and lax.ppermute only.
A program may use at most 64 MiB of HBM per device.

v0:
```python
import jax
import jax.numpy as jnp
from jax import lax
from jax.sharding import PartitionSpec as P


def pad_frames(active):
    return jnp.pad(active, ((0, 0), (1, 1), (1, 1), (0, 0)))


def conv_padded(padded, kernel):
    frame_count = padded.shape[0]
    height = padded.shape[1] - 2
    breadth = padded.shape[2] - 2
    summed = jnp.zeros((frame_count * height * breadth, kernel.shape[3]), jnp.float32)
    for offset_y in range(3):
        for offset_x in range(3):
            window = padded[:, offset_y : offset_y + height, offset_x : offset_x + breadth, :]
            window = window.reshape(frame_count * height * breadth, padded.shape[3])
            summed = summed + jnp.dot(
                window, kernel[offset_y, offset_x], preferred_element_type=jnp.float32
            )
    return summed.reshape(frame_count, height, breadth, kernel.shape[3])


def apply_layer(active, kernel):
    whole = lax.all_gather(active, "chan", axis=3, tiled=True)
    swapped = lax.all_to_all(whole, "img", split_axis=3, concat_axis=0, tiled=True)
    padded = pad_frames(swapped)
    return lax.psum_scatter(conv_padded(padded, kernel), "img", scatter_dimension=0, tiled=True)


def shards(features, kernel_one, kernel_two):
    first = apply_layer(features, kernel_one)
    hidden = jax.nn.silu(first).astype(jnp.bfloat16)
    return apply_layer(hidden, kernel_two).astype(jnp.bfloat16)


def solution(mesh):
    placed = (
        P(("groups", "img"), None, None, "chan"),
        P(None, None, "img", "chan"),
        P(None, None, "img", "chan"),
    )
    return jax.shard_map(
        shards,
        mesh=mesh,
        in_specs=placed,
        out_specs=P(("groups", "img"), None, None, "chan"),
        check_vma=False,
    )
```

profile of v0, /device:TPU:0, one launch (start us, length us, event | category | flops | bytes accessed | tf_op | source)
XLA Modules:
  0.0 292.1 jit_solution(17055327093405086871)
XLA Ops:
  6.5 0.0 all-gather.3.cloned.1.call-start
  6.5 0.7 all-gather.3.cloned.1.call-update
  7.3 0.0 reduce-scatter.3.cloned.1.call-start
  7.3 32.3 %all-gather.3.cloned.1.call-done = bf16[1,16,16,2048]{3,2,1,0:T(8,128)(2,1)} async-done(((bf16[1,16,16,512]{3,2,1,0:T(8,128)(2,1)}), bf16[1,16,16,2048]{3,2,1,0:T(8,128)(2,1)}) %all-gather.3.cloned.1.call-update) | async-done | bytes 1048592 | tf_op jit(solution)/shard_map/all_gather | solution.py:27
  39.6 9.6 %copy.44 = bf16[1,16,16,2048]{2,1,0,3:T(8,128)(2,1)} copy(bf16[1,16,16,2048]{3,2,1,0:T(8,128)(2,1)} %all-gather.3.cloned.1.call-done) | data formatting | bytes 2097152 | tf_op jit(solution)/shard_map/all_gather | solution.py:27
  49.2 10.2 %reshape.82 = bf16[4,2,65536]{2,1,0:T(2,128)(2,1)S(1)} reshape(bf16[2048,1,16,16]{3,2,1,0:T(8,128)(2,1)} %bitcast.104) | data formatting | bytes 2097152
  59.4 17.0 %all_to_all.36 = bf16[4,2,65536]{2,1,0:T(2,128)(2,1)S(1)} all-to-all(bf16[4,2,65536]{2,1,0:T(2,128)(2,1)S(1)} %reshape.82), channel_id=1, replica_groups=mesh['groups'=2,'chan'=4,'img'=4] {'img'}, dimensions={0} | all-to-all | bytes 2097152 | tf_op jit(solution)/shard_map/all_to_all | solution.py:28
  76.4 7.1 %reshape.83 = bf16[2048,1,16,16]{3,2,1,0:T(8,128)(2,1)} reshape(bf16[4,2,65536]{2,1,0:T(2,128)(2,1)S(1)} %all_to_all.36) | data formatting | bytes 2097152
  83.6 9.0 %copy.66 = bf16[1,16,16,4,512]{4,3,2,1,0:T(4,128)(2,1)S(1)} copy(bf16[1,16,16,4,512]{2,1,4,3,0:T(8,128)(2,1)} %bitcast.105) | data formatting | bytes 2097152 | tf_op jit(solution)/shard_map/all_to_all | solution.py:28
  92.6 0.2 copy.50
  92.8 4.1 %pad_slice_fusion.8 = (bf16[4,16,16,512]{3,0,2,1:T(4,128)(2,1)S(1)}, bf16[4,16,16,512]{3,0,2,1:T(4,128)(2,1)S(1)}, bf16[4,16,16,512]{3,0,2,1:T(4,128)(2,1)S(1)},...) fusion(bf16[4,16,16,512]{3,0,2,1:T(4,128)(2,1)S(1)} %bitcast.109), kind=kLoop, calls=%fused_computation.63 | loop fusion | bytes 9437184 | tf_op jit(solution)/shard_map/slice | solution.py:18
  97.0 0.2 copy.54
  97.2 0.2 copy.47
  97.5 1.8 fusion.24
  99.2 1.7 fusion.30
  101.0 0.2 copy.48
  101.2 1.7 fusion.28
  102.9 0.2 copy.49
  103.2 1.7 fusion.26
  104.9 0.2 copy.51
  105.2 1.7 fusion.22
  106.9 0.2 copy.52
  107.2 1.7 fusion.20
  108.9 0.2 copy.53
  109.1 1.7 fusion.18
  110.9 0.2 copy.46
  111.1 1.7 fusion.32
  112.9 3.6 %add_add_fusion.1 = f32[1024,512]{1,0:T(8,128)} fusion(f32[1024,512]{1,0:T(8,128)S(1)} %fusion.18, f32[1024,512]{1,0:T(8,128)S(1)} %fusion.20, f32[1024,512]{1,0:T(8,128)S(1)} %fusion.22, f32[1024,512]{1,0:T(8,128)S(1)} %fusion.24, f32[1024,512]{1,0:T(8,128)S(1)} %fusion.26, f32[1024,512]{1,0:T(8,128)S(1)} %fusion.28, f32[1024,512]{1,0:T(8,128)S(1)} %fusion.32, ...), kind=kOutput, calls=%fused_computation.1 | convolution fusion | flops 541065216 | bytes 20447232 | tf_op jit(solution)/shard_map/dot_general | solution.py:20
  116.4 0.0 reduce-scatter.3.cloned.1.call-update
  116.5 0.0 all-gather.5.cloned.1.call-start
  116.5 30.1 %reduce-scatter.3.cloned.1.call-done = f32[1,16,16,512]{3,2,1,0:T(8,128)} async-done(((f32[4,16,16,512]{3,2,1,0:T(8,128)}), f32[1,16,16,512]{3,2,1,0:T(8,128)}) %reduce-scatter.3.cloned.1.call-update) | async-done | bytes 524304 | tf_op jit(solution)/shard_map/reduce_scatter | solution.py:30
  146.6 1.9 multiply_convert_fusion
  148.5 0.0 all-gather.5.cloned.1.call-update
  148.5 0.0 reduce-scatter.5.cloned.1.call-start
  148.6 28.0 %all-gather.5.cloned.1.call-done = bf16[1,16,16,2048]{3,2,1,0:T(8,128)(2,1)} async-done(((bf16[1,16,16,512]{3,2,1,0:T(8,128)(2,1)}), bf16[1,16,16,2048]{3,2,1,0:T(8,128)(2,1)}) %all-gather.5.cloned.1.call-update) | async-done | bytes 1048592 | tf_op jit(solution)/shard_map/all_gather | solution.py:27
  176.6 9.6 %copy.55 = bf16[1,16,16,2048]{2,1,0,3:T(8,128)(2,1)} copy(bf16[1,16,16,2048]{3,2,1,0:T(8,128)(2,1)} %all-gather.5.cloned.1.call-done) | data formatting | bytes 2097152 | tf_op jit(solution)/shard_map/all_gather | solution.py:27
  186.2 10.2 %reshape.84 = bf16[4,2,65536]{2,1,0:T(2,128)(2,1)S(1)} reshape(bf16[2048,1,16,16]{3,2,1,0:T(8,128)(2,1)} %bitcast.106) | data formatting | bytes 2097152
  196.5 17.1 %all_to_all.37 = bf16[4,2,65536]{2,1,0:T(2,128)(2,1)S(1)} all-to-all(bf16[4,2,65536]{2,1,0:T(2,128)(2,1)S(1)} %reshape.84), channel_id=1, replica_groups=mesh['groups'=2,'chan'=4,'img'=4] {'img'}, dimensions={0} | all-to-all | bytes 2097152 | tf_op jit(solution)/shard_map/all_to_all | solution.py:28
  213.6 7.1 %reshape.85 = bf16[2048,1,16,16]{3,2,1,0:T(8,128)(2,1)} reshape(bf16[4,2,65536]{2,1,0:T(2,128)(2,1)S(1)} %all_to_all.37) | data formatting | bytes 2097152
  220.7 9.0 %copy.67 = bf16[1,16,16,4,512]{4,3,2,1,0:T(4,128)(2,1)S(1)} copy(bf16[1,16,16,4,512]{2,1,4,3,0:T(8,128)(2,1)} %bitcast.107) | data formatting | bytes 2097152 | tf_op jit(solution)/shard_map/all_to_all | solution.py:28
  229.7 0.2 copy.61
  230.0 4.1 %pad_slice_fusion = (bf16[4,16,16,512]{3,0,2,1:T(4,128)(2,1)S(1)}, bf16[4,16,16,512]{3,0,2,1:T(4,128)(2,1)S(1)}, bf16[4,16,16,512]{3,0,2,1:T(4,128)(2,1)S(1)}, b...) fusion(bf16[4,16,16,512]{3,0,2,1:T(4,128)(2,1)S(1)} %bitcast.111), kind=kLoop, calls=%fused_computation.55 | loop fusion | bytes 9437184 | tf_op jit(solution)/shard_map/slice | solution.py:18
  234.1 0.2 copy.65
  234.3 0.2 copy.58
  234.6 1.7 fusion.7
  236.3 1.8 fusion.13
  238.1 0.2 copy.59
  238.3 1.8 fusion.11
  240.1 0.2 copy.60
  240.3 1.7 fusion.9
  242.1 0.2 copy.62
  242.3 1.7 fusion.5
  244.0 0.2 copy.63
  244.3 1.7 fusion.3
  246.0 0.2 copy.64
  246.3 1.7 fusion.1
  248.0 0.2 copy.57
  248.3 1.7 fusion.15
  250.0 3.6 %add_add_fusion = f32[1024,512]{1,0:T(8,128)} fusion(f32[1024,512]{1,0:T(8,128)S(1)} %fusion.1, f32[1024,512]{1,0:T(8,128)S(1)} %fusion.3, f32[1024,512]{1,0:T(8,128)S(1)} %fusion.5, f32[1024,512]{1,0:T(8,128)S(1)} %fusion.7, f32[1024,512]{1,0:T(8,128)S(1)} %fusion.9, f32[1024,512]{1,0:T(8,128)S(1)} %fusion.11, f32[1024,512]{1,0:T(8,128)S(1)} %fusion.15, ...), kind=kOutput, calls=%fused_computation | convolution fusion | flops 541065216 | bytes 20447232 | tf_op jit(solution)/shard_map/dot_general | solution.py:20
  253.6 0.0 reduce-scatter.5.cloned.1.call-update
  253.6 30.2 %reduce-scatter.5.cloned.1.call-done = f32[1,16,16,512]{3,2,1,0:T(8,128)} async-done(((f32[4,16,16,512]{3,2,1,0:T(8,128)}), f32[1,16,16,512]{3,2,1,0:T(8,128)}) %reduce-scatter.5.cloned.1.call-update) | async-done | bytes 524304 | tf_op jit(solution)/shard_map/reduce_scatter | solution.py:30
  283.8 1.8 convert_element_type.10
Async XLA Ops:
  6.5 33.1 %all-gather.3.cloned.1.call-start = ((), (), s32[]{:S(2)}) async-start(), calls=%async_computation.4 | async-start | bytes 1310720 | tf_op jit(solution)/shard_map/all_gather | solution.py:27
  7.3 139.4 %reduce-scatter.3.cloned.1.call-start = ((), (), s32[]{:S(2)}) async-start(), calls=%async_computation.5 | async-start | bytes 2621440 | tf_op jit(solution)/shard_map/reduce_scatter | solution.py:30
  116.5 60.1 %all-gather.5.cloned.1.call-start = ((), (), s32[]{:S(2)}) async-start(), calls=%async_computation.6 | async-start | bytes 1310720 | tf_op jit(solution)/shard_map/all_gather | solution.py:27
  148.5 135.2 %reduce-scatter.5.cloned.1.call-start = ((), (), s32[]{:S(2)}) async-start(), calls=%async_computation.7 | async-start | bytes 2621440 | tf_op jit(solution)/shard_map/reduce_scatter | solution.py:30
Sparse Core Ops, SparseCore 0:
  8.9 30.6 all-gather.2
  116.6 29.9 reduce-scatter.2
  148.6 27.9 all-gather.4
  253.7 29.9 reduce-scatter.4
where the time goes:
time: 294 us; the launch traced here: 292 us
  waiting for transfers between devices  121 us (41%)
  local copies, waits for them, and re-layouts  84.4 us (29%)
  matrix products  35 us (12%)
  blocking collectives  34.1 us (12%)
  between operations  13.4 us (5%)
  other arithmetic  3.67 us (1%)
    all_gather x2, waiting for transfers between devices, apply_layer(): whole = lax.all_gather(active, 'chan', axis=3, tiled=True)  60.3 us
    reduce_scatter x2, waiting for transfers between devices, apply_layer(): lax.psum_scatter(conv_padded(padded, kernel), 'img', scatter_dimension=0,...  60.3 us
    dot_general x18, matrix products, conv_padded(): jnp.dot(window, kernel[offset_y, offset_x], preferred_element_type=jnp.fl...  35 us
    unnamed x4, local copies, waits for them, and re-layouts  34.7 us
    all_to_all x2, blocking collectives, apply_layer(): lax.all_to_all(whole, 'img', split_axis=3, concat_axis=0, tiled=True)  34.1 us
    all_gather x2, local copies, waits for them, and re-layouts, apply_layer(): whole = lax.all_gather(active, 'chan', axis=3, tiled=True)  19.3 us
    all_to_all x4, local copies, waits for them, and re-layouts, apply_layer(): lax.all_to_all(whole, 'img', split_axis=3, concat_axis=0, tiled=True)  18.5 us
    slice x18, local copies, waits for them, and re-layouts, conv_padded(): padded[:, offset_y:offset_y + height, offset_x:offset_x + breadth, :]  12 us
  transfers between devices with their start and end apart: 4, of which 4 were waited for; matrix products, arithmetic and copies ran while one was open for 0% of the time, Pallas kernels for 0%

commit v1 on v0

v1 whole, which is shorter than its diff:
```python
import functools

import jax
import jax.numpy as jnp
from jax import lax
from jax.experimental import pallas as pl
from jax.experimental.pallas import tpu as pltpu
from jax.sharding import PartitionSpec as P

VMEM = pl.BlockSpec(memory_space=pltpu.VMEM)
F32, BF16 = jnp.float32, jnp.bfloat16


class Plan:
    def __init__(self, mesh, features, kernel):
        self.levels = mesh.shape["chan"]
        self.cols = mesh.shape["img"]
        self.ratio = self.levels // self.cols
        self.height, self.width = features.shape[1], features.shape[2]
        self.pixels = self.height * self.width
        self.piece = features.shape[3]
        self.c_in, self.c_out = kernel.shape[2], kernel.shape[3]
        self.share = self.pixels // self.cols
        self.bits = self.cols.bit_length() - 1

    def spread_pairs(self, d, e):
        pairs = []
        for k in range(self.levels):
            for f in range(self.cols):
                level = (f - d) % self.cols * self.ratio + (k % self.ratio - e) % self.ratio
                pairs.append((k * self.cols + f, level * self.cols + k // self.ratio))
        return pairs

    def swap(self, x, bit):
        return lax.ppermute(x, "img", [(i, i ^ (1 << bit)) for i in range(self.cols)])

    def spread(self, x):
        return [
            lax.ppermute(x, ("chan", "img"), self.spread_pairs(d, e))
            for d in range(self.cols)
            for e in range(self.ratio)
        ]

    def call(self, body, inputs, outputs, scratch=(), flops=0):
        moved = sum(x.size * x.dtype.itemsize for x in inputs)
        return pl.pallas_call(
            body,
            in_specs=[VMEM] * len(inputs),
            out_specs=[VMEM] * len(outputs),
            out_shape=[jax.ShapeDtypeStruct(*o) for o in outputs],
            scratch_shapes=list(scratch),
            cost_estimate=pl.CostEstimate(flops=flops, bytes_accessed=moved, transcendentals=0),
            compiler_params=pltpu.CompilerParams(vmem_limit_bytes=24 * 2**20),
        )(*inputs)


def place(plan, rows, frame, row_at, lane_at, wide):
    x = rows.astype(F32)
    column = lax.broadcasted_iota(jnp.int32, x.shape, 0) % plan.width
    left = jnp.where(column == 0, 0.0, pltpu.roll(x, 1, 0))
    right = jnp.where(column == plan.width - 1, 0.0, pltpu.roll(x, x.shape[0] - 1, 0))
    for b, moved in enumerate((left, x, right)):
        lanes = b * plan.c_in + lane_at
        if not isinstance(lanes, int):
            lanes = pl.multiple_of(lanes, 128)
        wide[frame, pl.ds(row_at, x.shape[0]), pl.ds(lanes, plan.piece)] = moved.astype(BF16)


def clear_edges(plan, frames, wide):
    zero = jnp.zeros((plan.width, wide.shape[2]), BF16)
    for f in range(frames):
        wide[f, 0 : plan.width, :] = zero
        wide[f, plan.width + plan.pixels :, :] = zero


def where_am_i(plan):
    level, col = lax.axis_index("chan"), lax.axis_index("img")
    return level // plan.ratio, level % plan.ratio, col


def first_row(plan, col):
    at, size = 0, plan.pixels
    for bit in range(plan.bits):
        size //= 2
        at = at + (col // 2**bit) % 2 * size
    return at


def conv_one_body(plan, frames, *refs):
    pieces = refs[: frames * plan.ratio]
    kernel, keep, send, wide = refs[frames * plan.ratio :]
    turn, lane, col = where_am_i(plan)
    clear_edges(plan, frames, wide)
    for f in range(frames):
        for e in range(plan.ratio):
            lane_at = (lane + e) % plan.ratio * plan.piece if plan.ratio > 1 else 0
            place(plan, pieces[f * plan.ratio + e][0], f, plan.width, lane_at, wide)
    half = plan.pixels // 2
    mine = col % 2 * half
    starts = (mine, half - mine)
    summed = None
    for a in range(3):
        parts = []
        for start in starts:
            rows = pl.ds(pl.multiple_of(start + a * plan.width, 16), half)
            parts.append(wide[:, rows, :].reshape(frames * half, 3 * plan.c_in))
        term = jnp.dot(
            jnp.concatenate(parts, axis=0),
            kernel[a].reshape(3 * plan.c_in, plan.c_out),
            preferred_element_type=F32,
        )
        summed = term if summed is None else summed + term
    keep[...] = summed[: frames * half].reshape(keep.shape)
    send[...] = summed[frames * half :].astype(BF16).reshape(send.shape)


def conv_one(plan, pieces, kernel):
    frames = len(pieces) // plan.ratio
    half = (frames, plan.pixels // 2, plan.c_out)
    return plan.call(
        functools.partial(conv_one_body, plan, frames),
        [*pieces, kernel],
        [(half, F32), (half, BF16)],
        [pltpu.VMEM((frames, plan.pixels + 2 * plan.width, 3 * plan.c_in), BF16)],
        18 * frames * plan.pixels * plan.c_in * plan.c_out,
    )


def halve_body(plan, bit, kept, came, keep, send):
    half = keep.shape[1]
    col = lax.axis_index("img")
    mine = (col // 2**bit) % 2 * half
    a = pl.ds(pl.multiple_of(mine, 16), half)
    b = pl.ds(pl.multiple_of(half - mine, 16), half)
    send[...] = (kept[:, b, :] + came[:, b, :].astype(F32)).astype(BF16)
    keep[...] = kept[:, a, :] + came[:, a, :].astype(F32)


def silu_body(kept, came, hidden):
    v = kept[...] + came[...].astype(F32)
    hidden[...] = (v / (1.0 + jnp.exp(-v))).astype(BF16)


def sum_one(plan, keep, send):
    for bit in range(1, plan.bits):
        came = plan.swap(send, bit - 1)
        half = (keep.shape[0], keep.shape[1] // 2, keep.shape[2])
        keep, send = plan.call(
            functools.partial(halve_body, plan, bit), [keep, came], [(half, F32), (half, BF16)]
        )
    came = plan.swap(send, plan.bits - 1)
    return plan.call(silu_body, [keep, came], [(keep.shape, BF16)])[0]


def conv_two_body(plan, frames, *refs):
    count = plan.cols * plan.ratio
    pieces = refs[:count]
    kernel, keep, send, wide = refs[count:]
    turn, lane, col = where_am_i(plan)
    clear_edges(plan, frames, wide)
    for d in range(plan.cols):
        row_at = pl.multiple_of(plan.width + first_row(plan, (turn + d) % plan.cols), 16)
        for e in range(plan.ratio):
            lane_at = (lane + e) % plan.ratio * plan.piece if plan.ratio > 1 else 0
            for f in range(frames):
                place(plan, pieces[d * plan.ratio + e][f], f, row_at, lane_at, wide)
    summed = None
    for a in range(3):
        rows = wide[:, a * plan.width : a * plan.width + plan.pixels, :]
        term = jnp.dot(
            rows.reshape(frames * plan.pixels, 3 * plan.c_in),
            kernel[a].reshape(3 * plan.c_in, plan.c_out),
            preferred_element_type=F32,
        )
        summed = term if summed is None else summed + term
    for f in range(frames):
        part = summed[f * plan.pixels : (f + 1) * plan.pixels]
        if f % 2 == 0:
            keep[f // 2] = part
        else:
            send[f // 2] = part.astype(BF16)


def conv_two(plan, pieces, kernel):
    frames = pieces[0].shape[0]
    half = (frames // 2, plan.pixels, plan.c_out)
    return plan.call(
        functools.partial(conv_two_body, plan, frames),
        [*pieces, kernel],
        [(half, F32), (half, BF16)],
        [pltpu.VMEM((frames, plan.pixels + 2 * plan.width, 3 * plan.c_in), BF16)],
        18 * frames * plan.pixels * plan.c_in * plan.c_out,
    )


def merge_body(plan, bit, count, *refs):
    kept, came = refs[:count], refs[count : 2 * count]
    outs = refs[2 * count :]
    kept = [(r, t) for r in kept for t in range(r.shape[0])]
    came = [(r, t) for r in came for t in range(r.shape[0])]
    col = lax.axis_index("img")
    low = (col // 2**bit) % 2 == 0
    for n, (ref, t) in enumerate(kept):
        before, behind = came[n - 1], came[n]
        got = jnp.where(low, before[0][before[1]].astype(F32), behind[0][behind[1]].astype(F32))
        total = ref[t] + got
        out = outs[n % 2]
        out[n // 2] = total.astype(out.dtype)


def sum_two(plan, parts):
    keeps, sends = [k for k, _ in parts], [s for _, s in parts]
    for bit in range(plan.bits):
        cames = [plan.swap(s, bit) for s in sends]
        count = sum(k.shape[0] for k in keeps)
        if count == 1:
            return plan.call(
                functools.partial(merge_body, plan, bit, 1),
                [*keeps, *cames],
                [((1, plan.pixels, plan.c_out), BF16)],
            )[0]
        half = (count // 2, plan.pixels, plan.c_out)
        keep, send = plan.call(
            functools.partial(merge_body, plan, bit, len(keeps)),
            [*keeps, *cames],
            [(half, F32), (half, BF16)],
        )
        keeps, sends = [keep], [send]


def shards(mesh, batches, features, kernel_one, kernel_two):
    plan = Plan(mesh, features, kernel_one)
    block = features.reshape(1, plan.pixels, plan.piece)
    pieces = plan.spread(block)
    size = plan.cols // batches
    parts = []
    for n in range(batches):
        own = pieces[n * size * plan.ratio : (n + 1) * size * plan.ratio]
        keep, send = conv_one(plan, own, kernel_one)
        hidden = sum_one(plan, keep, send)
        parts.append(conv_two(plan, plan.spread(hidden), kernel_two))
    return sum_two(plan, parts).reshape(features.shape)


def solution(mesh):
    placed = (
        P(("groups", "img"), None, None, "chan"),
        P(None, None, "img", "chan"),
        P(None, None, "img", "chan"),
    )
    return jax.shard_map(
        functools.partial(shards, mesh, 2),
        mesh=mesh,
        in_specs=placed,
        out_specs=P(("groups", "img"), None, None, "chan"),
        check_vma=False,
    )
```

time: 294 us -> 82.4 us (0.28)
  waiting for transfers between devices: 121 us -> 18.1 us
  local copies, waits for them, and re-layouts: 84.4 us -> 2.35 us
  starting transfers between devices: 0.12 us -> 49.1 us
  matrix products: 35 us -> 0 us
  blocking collectives: 34.1 us -> 0 us
  between operations: 13.4 us -> 0.16 us
  Pallas kernels: 0 us -> 12.4 us
  other arithmetic: 3.67 us -> 0.01 us
    all_gather x2 -> x0, waiting for transfers between devices: 60.3 us -> none  [apply_layer(): whole = lax.all_gather(active, 'chan', axis=3, tiled=True)]
    reduce_scatter x2 -> x0, waiting for transfers between devices: 60.3 us -> none  [apply_layer(): lax.psum_scatter(conv_padded(padded, kernel), 'img', scatter_dimension=0,...]
    ppermute x0 -> x19, starting transfers between devices: none -> 49.1 us  [the longest x7 25.3 us: swap(): return lax.ppermute(x, 'img', [(i, i ^ 1 << bit) for i in range(self.cols)])]
    dot_general x18 -> x0, matrix products: 35 us -> none  [conv_padded(): jnp.dot(window, kernel[offset_y, offset_x], preferred_element_type=jnp.fl...]
    all_to_all x2 -> x0, blocking collectives: 34.1 us -> none  [apply_layer(): lax.all_to_all(whole, 'img', split_axis=3, concat_axis=0, tiled=True)]
    unnamed x4 -> x8, local copies, waits for them, and re-layouts: 34.7 us -> 2.35 us
    all_gather x2 -> x0, local copies, waits for them, and re-layouts: 19.3 us -> none  [apply_layer(): whole = lax.all_gather(active, 'chan', axis=3, tiled=True)]
    all_to_all x4 -> x0, local copies, waits for them, and re-layouts: 18.5 us -> none  [apply_layer(): lax.all_to_all(whole, 'img', split_axis=3, concat_axis=0, tiled=True)]
  transfers between devices with their start and end apart: 4 -> 19, of which waited for: 4 -> 5; matrix products, arithmetic and copies ran while one was open for 0% -> 0% of each run, Pallas kernels for 0% -> 14%
where the time goes in v1:
time: 82.4 us; the launch traced here: 82.2 us
  starting transfers between devices  49.1 us (60%)
  waiting for transfers between devices  18.1 us (22%)
  Pallas kernels  12.4 us (15%)
  local copies, waits for them, and re-layouts  2.35 us (3%)
    ppermute x7, starting transfers between devices, swap(): return lax.ppermute(x, 'img', [(i, i ^ 1 << bit) for i in range(self.cols)])  25.3 us
    ppermute x12, starting transfers between devices, spread(): lax.ppermute(x, ('chan', 'img'), self.spread_pairs(d, e))  23.8 us
    pallas_call x10, Pallas kernels, call(): pl.pallas_call(body, in_specs=[VMEM] * len(inputs), out_specs=[VMEM] * le...  12.4 us
    ppermute x7, waiting for transfers between devices, swap(): return lax.ppermute(x, 'img', [(i, i ^ 1 << bit) for i in range(self.cols)])  10.9 us
    ppermute x12, waiting for transfers between devices, spread(): lax.ppermute(x, ('chan', 'img'), self.spread_pairs(d, e))  7.25 us
    unnamed x8, local copies, waits for them, and re-layouts  2.35 us
  transfers between devices with their start and end apart: 19, of which 5 were waited for; matrix products, arithmetic and copies ran while one was open for 0% of the time, Pallas kernels for 14%

profile of v1, /device:TPU:0, one launch (start us, length us, event | category | flops | bytes accessed | tf_op | source)
XLA Modules:
  0.0 82.2 jit_solution(4489305538775603420)
XLA Ops:
  0.0 3.0 %collective-permute-start.9 = (bf16[1,256,512]{2,1,0:T(8,128)(2,1)}, bf16[1,256,512]{2,1,0:T(8,128)(2,1)S(1)}, u32[]{:S(2)}, u32[]{:S(2)}) collective-permute-start(bf16[1,256,512]{2,1,0:T(8,128)(2,1)} %bitcast.4), channel_id=1, source_target_pairs={{0,4},{1,8},{2,12},{3,0},{4,5},{5,9},{6,13},{7,1},{8,6},{9,10},{10... | collective-permute-start | bytes 786440 | tf_op jit(solution)/shard_map/ppermute | solution.py:39
  3.0 2.4 %collective-permute-start.8 = (bf16[1,256,512]{2,1,0:T(8,128)(2,1)}, bf16[1,256,512]{2,1,0:T(8,128)(2,1)S(1)}, u32[]{:S(2)}, u32[]{:S(2)}) collective-permute-start(bf16[1,256,512]{2,1,0:T(8,128)(2,1)} %bitcast.5), channel_id=1, source_target_pairs={{0,8},{1,12},{2,0},{3,4},{4,9},{5,13},{6,1},{7,5},{8,10},{9,14},{1... | collective-permute-start | bytes 786440 | tf_op jit(solution)/shard_map/ppermute | solution.py:39
  5.4 1.1 %collective-permute-start.1 = (bf16[1,256,512]{2,1,0:T(8,128)(2,1)}, bf16[1,256,512]{2,1,0:T(8,128)(2,1)S(1)}, u32[]{:S(2)}, u32[]{:S(2)}) collective-permute-start(bf16[1,256,512]{2,1,0:T(8,128)(2,1)} %bitcast.6), channel_id=1, source_target_pairs={{0,12},{1,0},{2,4},{3,8},{4,13},{5,1},{6,5},{7,9},{8,14},{9,2},{10... | collective-permute-start | bytes 786440 | tf_op jit(solution)/shard_map/ppermute | solution.py:39
  6.5 1.6 %collective-permute-start = (bf16[1,256,512]{2,1,0:T(8,128)(2,1)}, bf16[1,256,512]{2,1,0:T(8,128)(2,1)S(1)}, u32[]{:S(2)}, u32[]{:S(2)}) collective-permute-start(bf16[1,256,512]{2,1,0:T(8,128)(2,1)} %bitcast.7), channel_id=1, source_target_pairs={{0,0},{1,4},{2,8},{3,12},{4,1},{5,5},{6,9},{7,13},{8,2},{9,6},{10,... | collective-permute-start | bytes 786440 | tf_op jit(solution)/shard_map/ppermute | solution.py:39
  8.1 1.6 %collective-permute-done.9.refs_1_ = bf16[1,256,512]{2,1,0:T(8,128)(2,1)S(1)} collective-permute-done((bf16[1,256,512]{2,1,0:T(8,128)(2,1)}, bf16[1,256,512]{2,1,0:T(8,128)(2,1)S(1)}, u32[]{:S(2)}, u32[]{:S(2)}) %collective-permute-start.9) | collective-permute-done | bytes 262176 | tf_op jit(solution)/shard_map/ppermute | solution.py:39
  9.7 5.6 %collective-permute-done.8.refs_0_ = bf16[1,256,512]{2,1,0:T(8,128)(2,1)S(1)} collective-permute-done((bf16[1,256,512]{2,1,0:T(8,128)(2,1)}, bf16[1,256,512]{2,1,0:T(8,128)(2,1)S(1)}, u32[]{:S(2)}, u32[]{:S(2)}) %collective-permute-start.8) | collective-permute-done | bytes 262176 | tf_op jit(solution)/shard_map/ppermute | solution.py:39
  15.3 0.0 copy-start
  15.3 2.3 %copy-done = bf16[3,3,512,512]{3,2,1,0:T(8,128)(2,1)S(1)} copy-done((bf16[3,3,512,512]{3,2,1,0:T(8,128)(2,1)S(1)}, bf16[3,3,512,512]{3,2,1,0:T(8,128)(2,1)}, u32[]{:S(2)}) %copy-start) | copy-done | bytes 4718616
  17.6 0.0 copy-start.1
  17.6 2.7 %shard_map.41 = (f32[2,128,512]{2,1,0:T(8,128)S(1)}, bf16[2,128,512]{2,1,0:T(8,128)(2,1)S(1)}) custom-call(bf16[1,256,512]{2,1,0:T(8,128)(2,1)S(1)} %collective-permute-done.8.refs_0_, bf16[1,256,512]{2,1,0:T(8,128)(2,1)S(1)} %collective-permute-done.9.refs_1_, bf16[3,3,512,512]{3,2,1,0:T(8,128)(2,1)S(1)} %copy-done), custom_call_target="tpu_custom_call" | custom-call | flops 2415919104 | bytes 5242880 | tf_op jit(solution)/shard_map/pallas_call | solution.py:46
  20.4 0.0 slice-start
  20.4 0.0 slice-start.1
  20.4 1.2 %collective-permute-start.10 = (bf16[2,128,512]{2,1,0:T(8,128)(2,1)S(1)}, bf16[2,128,512]{2,1,0:T(8,128)(2,1)S(1)}, u32[]{:S(2)}, u32[]{:S(2)}) collective-permute-start(bf16[2,128,512]{2,1,0:T(8,128)(2,1)S(1)} %get-tuple-element.25), channel_id=1, source_target_pairs={{0,1},{1,0},{2,3},{3,2},{4,5},{5,4},{6,7},{7,6},{8,9},{9,8},{10,11... | collective-permute-start | bytes 786440 | tf_op jit(solution)/shard_map/ppermute | solution.py:35
  21.6 0.0 collective-permute-done.1.refs_1_
  21.6 0.0 collective-permute-done.refs_0_
  21.6 0.0 copy-done.1
  21.6 2.7 %shard_map.37 = (f32[2,128,512]{2,1,0:T(8,128)S(1)}, bf16[2,128,512]{2,1,0:T(8,128)(2,1)S(1)}) custom-call(bf16[1,256,512]{2,1,0:T(8,128)(2,1)S(1)} %collective-permute-done.refs_0_, bf16[1,256,512]{2,1,0:T(8,128)(2,1)S(1)} %collective-permute-done.1.refs_1_, bf16[3,3,512,512]{3,2,1,0:T(8,128)(2,1)S(1)} %copy-done.1), custom_call_target="tpu_custom_call" | custom-call | flops 2415919104 | bytes 5242880 | tf_op jit(solution)/shard_map/pallas_call | solution.py:46
  24.4 0.1 collective-permute-start.2
  24.5 0.0 collective-permute-done.10.came
  24.5 0.1 shard_map.42
  24.5 8.6 %collective-permute-start.11 = (bf16[2,64,512]{2,1,0:T(8,128)(2,1)S(1)}, bf16[2,64,512]{2,1,0:T(8,128)(2,1)S(1)}, u32[]{:S(2)}, u32[]{:S(2)}) collective-permute-start(bf16[2,64,512]{2,1,0:T(8,128)(2,1)S(1)} %get-tuple-element.27), channel_id=1, source_target_pairs={{0,2},{1,3},{2,0},{3,1},{4,6},{5,7},{6,4},{7,5},{8,10},{9,11},{10,... | collective-permute-start | bytes 393224 | tf_op jit(solution)/shard_map/ppermute | solution.py:35
  33.1 0.0 collective-permute-done.2.came
  33.2 1.1 %collective-permute-start.3 = (bf16[2,64,512]{2,1,0:T(8,128)(2,1)S(1)}, bf16[2,64,512]{2,1,0:T(8,128)(2,1)S(1)}, u32[]{:S(2)}, u32[]{:S(2)}) collective-permute-start(bf16[2,64,512]{2,1,0:T(8,128)(2,1)S(1)} %get-tuple-element.22), channel_id=1, source_target_pairs={{0,2},{1,3},{2,0},{3,1},{4,6},{5,7},{6,4},{7,5},{8,10},{9,11},{10,... | collective-permute-start | bytes 393224 | tf_op jit(solution)/shard_map/ppermute | solution.py:35
  34.3 3.1 %collective-permute-done.11.came = bf16[2,64,512]{2,1,0:T(8,128)(2,1)S(1)} collective-permute-done((bf16[2,64,512]{2,1,0:T(8,128)(2,1)S(1)}, bf16[2,64,512]{2,1,0:T(8,128)(2,1)S(1)}, u32[]{:S(2)}, u32[]{:S(2)}) %collective-permute-start.11) | collective-permute-done | bytes 131104 | tf_op jit(solution)/shard_map/ppermute | solution.py:35
  37.4 0.1 shard_map.43
  37.5 5.1 %collective-permute-start.15 = (bf16[2,64,512]{2,1,0:T(8,128)(2,1)S(1)}, bf16[2,64,512]{2,1,0:T(8,128)(2,1)S(1)}, u32[]{:S(2)}, u32[]{:S(2)}) collective-permute-start(bf16[2,64,512]{2,1,0:T(8,128)(2,1)S(1)} %shard_map.43), channel_id=1, source_target_pairs={{0,4},{1,8},{2,12},{3,0},{4,5},{5,9},{6,13},{7,1},{8,6},{9,10},{10... | collective-permute-start | bytes 393224 | tf_op jit(solution)/shard_map/ppermute | solution.py:39
  42.6 3.0 %collective-permute-start.14 = (bf16[2,64,512]{2,1,0:T(8,128)(2,1)S(1)}, bf16[2,64,512]{2,1,0:T(8,128)(2,1)S(1)}, u32[]{:S(2)}, u32[]{:S(2)}) collective-permute-start(bf16[2,64,512]{2,1,0:T(8,128)(2,1)S(1)} %shard_map.43), channel_id=1, source_target_pairs={{0,8},{1,12},{2,0},{3,4},{4,9},{5,13},{6,1},{7,5},{8,10},{9,14},{1... | collective-permute-start | bytes 393224 | tf_op jit(solution)/shard_map/ppermute | solution.py:39
  45.6 0.0 collective-permute-start.13
  45.6 0.7 collective-permute-start.12
  46.3 0.0 collective-permute-done.3.came
  46.3 0.1 shard_map.39
  46.4 3.4 %collective-permute-start.7 = (bf16[2,64,512]{2,1,0:T(8,128)(2,1)S(1)}, bf16[2,64,512]{2,1,0:T(8,128)(2,1)S(1)}, u32[]{:S(2)}, u32[]{:S(2)}) collective-permute-start(bf16[2,64,512]{2,1,0:T(8,128)(2,1)S(1)} %shard_map.39), channel_id=1, source_target_pairs={{0,4},{1,8},{2,12},{3,0},{4,5},{5,9},{6,13},{7,1},{8,6},{9,10},{10... | collective-permute-start | bytes 393224 | tf_op jit(solution)/shard_map/ppermute | solution.py:39
  49.8 0.0 collective-permute-done.15.refs_3_
  49.8 1.9 %collective-permute-start.6 = (bf16[2,64,512]{2,1,0:T(8,128)(2,1)S(1)}, bf16[2,64,512]{2,1,0:T(8,128)(2,1)S(1)}, u32[]{:S(2)}, u32[]{:S(2)}) collective-permute-start(bf16[2,64,512]{2,1,0:T(8,128)(2,1)S(1)} %shard_map.39), channel_id=1, source_target_pairs={{0,8},{1,12},{2,0},{3,4},{4,9},{5,13},{6,1},{7,5},{8,10},{9,14},{1... | collective-permute-start | bytes 393224 | tf_op jit(solution)/shard_map/ppermute | solution.py:39
  51.7 0.0 collective-permute-done.14.refs_2_
  51.7 0.9 %collective-permute-start.5 = (bf16[2,64,512]{2,1,0:T(8,128)(2,1)S(1)}, bf16[2,64,512]{2,1,0:T(8,128)(2,1)S(1)}, u32[]{:S(2)}, u32[]{:S(2)}) collective-permute-start(bf16[2,64,512]{2,1,0:T(8,128)(2,1)S(1)} %shard_map.39), channel_id=1, source_target_pairs={{0,12},{1,0},{2,4},{3,8},{4,13},{5,1},{6,5},{7,9},{8,14},{9,2},{10... | collective-permute-start | bytes 393224 | tf_op jit(solution)/shard_map/ppermute | solution.py:39
  52.7 0.0 collective-permute-done.13.refs_1_
  52.7 0.7 collective-permute-start.4
  53.3 0.0 collective-permute-done.12.refs_0_
  53.4 0.0 slice-done
  53.4 0.0 slice-done.1
  53.4 2.9 %shard_map.44 = (f32[1,256,512]{2,1,0:T(8,128)S(1)}, bf16[1,256,512]{2,1,0:T(8,128)(2,1)S(1)}) custom-call(bf16[2,64,512]{2,1,0:T(8,128)(2,1)S(1)} %collective-permute-done.12.refs_0_, bf16[2,64,512]{2,1,0:T(8,128)(2,1)S(1)} %collective-permute-done.13.refs_1_, bf16[2,64,512]{2,1,0:T(8,128)(2,1)S(1)} %collective-permute-done.14.refs_2_, ...), custom_call_target="tpu_custom_call" | custom-call | flops 2415919104 | bytes 5242880 | tf_op jit(solution)/shard_map/pallas_call | solution.py:46
  56.3 9.1 %collective-permute-start.17 = (bf16[1,256,512]{2,1,0:T(8,128)(2,1)S(1)}, bf16[1,256,512]{2,1,0:T(8,128)(2,1)S(1)}, u32[]{:S(2)}, u32[]{:S(2)}) collective-permute-start(bf16[1,256,512]{2,1,0:T(8,128)(2,1)S(1)} %get-tuple-element.30), channel_id=1, source_target_pairs={{0,1},{1,0},{2,3},{3,2},{4,5},{5,4},{6,7},{7,6},{8,9},{9,8},{10,11... | collective-permute-start | bytes 786440 | tf_op jit(solution)/shard_map/ppermute | solution.py:35
  65.3 0.0 collective-permute-done.7.refs_3_
  65.4 0.0 collective-permute-done.6.refs_2_
  65.4 0.0 collective-permute-done.5.refs_1_
  65.4 0.0 collective-permute-done.4.refs_0_
  65.4 2.9 %shard_map.40 = (f32[1,256,512]{2,1,0:T(8,128)S(1)}, bf16[1,256,512]{2,1,0:T(8,128)(2,1)S(1)}) custom-call(bf16[2,64,512]{2,1,0:T(8,128)(2,1)S(1)} %collective-permute-done.4.refs_0_, bf16[2,64,512]{2,1,0:T(8,128)(2,1)S(1)} %collective-permute-done.5.refs_1_, bf16[2,64,512]{2,1,0:T(8,128)(2,1)S(1)} %collective-permute-done.6.refs_2_, ...), custom_call_target="tpu_custom_call" | custom-call | flops 2415919104 | bytes 5242880 | tf_op jit(solution)/shard_map/pallas_call | solution.py:46
  68.3 0.8 collective-permute-start.16
  69.1 0.0 collective-permute-done.17.refs_3_
  69.1 1.2 %collective-permute-done.16.refs_2_ = bf16[1,256,512]{2,1,0:T(8,128)(2,1)S(1)} collective-permute-done((bf16[1,256,512]{2,1,0:T(8,128)(2,1)S(1)}, bf16[1,256,512]{2,1,0:T(8,128)(2,1)S(1)}, u32[]{:S(2)}, u32[]{:S(2)}) %collective-permute-start.16) | collective-permute-done | bytes 262176 | tf_op jit(solution)/shard_map/ppermute | solution.py:35
  70.2 0.2 shard_map.45
  70.4 4.5 %collective-permute-start.18 = (bf16[1,256,512]{2,1,0:T(8,128)(2,1)S(1)}, bf16[1,256,512]{2,1,0:T(8,128)(2,1)S(1)}, u32[]{:S(2)}, u32[]{:S(2)}) collective-permute-start(bf16[1,256,512]{2,1,0:T(8,128)(2,1)S(1)} %get-tuple-element.32), channel_id=1, source_target_pairs={{0,2},{1,3},{2,0},{3,1},{4,6},{5,7},{6,4},{7,5},{8,10},{9,11},{10,... | collective-permute-start | bytes 786440 | tf_op jit(solution)/shard_map/ppermute | solution.py:35
  74.9 6.6 %collective-permute-done.18.refs_1_ = bf16[1,256,512]{2,1,0:T(8,128)(2,1)S(1)} collective-permute-done((bf16[1,256,512]{2,1,0:T(8,128)(2,1)S(1)}, bf16[1,256,512]{2,1,0:T(8,128)(2,1)S(1)}, u32[]{:S(2)}, u32[]{:S(2)}) %collective-permute-start.18) | collective-permute-done | bytes 262176 | tf_op jit(solution)/shard_map/ppermute | solution.py:35
  81.5 0.7 shard_map.46
  (2 shorter events, 0.0 us)
Async XLA Ops:
  0.0 9.7 %collective-permute-start.9 = (bf16[1,256,512]{2,1,0:T(8,128)(2,1)}, bf16[1,256,512]{2,1,0:T(8,128)(2,1)S(1)}, u32[]{:S(2)}, u32[]{:S(2)}) collective-permute-start(bf16[1,256,512]{2,1,0:T(8,128)(2,1)} %bitcast.4), channel_id=1, source_target_pairs={{0,4},{1,8},{2,12},{3,0},{4,5},{5,9},{6,13},{7,1},{8,6},{9,10},{10... | collective-permute-start | bytes 786440 | tf_op jit(solution)/shard_map/ppermute | solution.py:39
  3.0 12.3 %collective-permute-start.8 = (bf16[1,256,512]{2,1,0:T(8,128)(2,1)}, bf16[1,256,512]{2,1,0:T(8,128)(2,1)S(1)}, u32[]{:S(2)}, u32[]{:S(2)}) collective-permute-start(bf16[1,256,512]{2,1,0:T(8,128)(2,1)} %bitcast.5), channel_id=1, source_target_pairs={{0,8},{1,12},{2,0},{3,4},{4,9},{5,13},{6,1},{7,5},{8,10},{9,14},{1... | collective-permute-start | bytes 786440 | tf_op jit(solution)/shard_map/ppermute | solution.py:39
  5.4 16.2 %collective-permute-start.1 = (bf16[1,256,512]{2,1,0:T(8,128)(2,1)}, bf16[1,256,512]{2,1,0:T(8,128)(2,1)S(1)}, u32[]{:S(2)}, u32[]{:S(2)}) collective-permute-start(bf16[1,256,512]{2,1,0:T(8,128)(2,1)} %bitcast.6), channel_id=1, source_target_pairs={{0,12},{1,0},{2,4},{3,8},{4,13},{5,1},{6,5},{7,9},{8,14},{9,2},{10... | collective-permute-start | bytes 786440 | tf_op jit(solution)/shard_map/ppermute | solution.py:39
  6.5 15.1 %collective-permute-start = (bf16[1,256,512]{2,1,0:T(8,128)(2,1)}, bf16[1,256,512]{2,1,0:T(8,128)(2,1)S(1)}, u32[]{:S(2)}, u32[]{:S(2)}) collective-permute-start(bf16[1,256,512]{2,1,0:T(8,128)(2,1)} %bitcast.7), channel_id=1, source_target_pairs={{0,0},{1,4},{2,8},{3,12},{4,1},{5,5},{6,9},{7,13},{8,2},{9,6},{10,... | collective-permute-start | bytes 786440 | tf_op jit(solution)/shard_map/ppermute | solution.py:39
  15.3 2.3 %copy-start = (bf16[3,3,512,512]{3,2,1,0:T(8,128)(2,1)S(1)}, bf16[3,3,512,512]{3,2,1,0:T(8,128)(2,1)}, u32[]{:S(2)}) copy-start(bf16[3,3,512,512]{3,2,1,0:T(8,128)(2,1)} %refs_2_.3) | copy-start | bytes 14155780
  17.6 4.0 %copy-start.1 = (bf16[3,3,512,512]{3,2,1,0:T(8,128)(2,1)S(1)}, bf16[3,3,512,512]{3,2,1,0:T(8,128)(2,1)}, u32[]{:S(2)}) copy-start(bf16[3,3,512,512]{3,2,1,0:T(8,128)(2,1)} %refs_2_.3) | copy-start | bytes 14155780
  20.4 33.0 %slice-start = ((s8[4718592]{0:T(1024)(128)(4,1)}), s8[4194304]{0:T(1024)(128)(4,1)S(1)}, s32[]{:S(2)}) async-start(s8[4718592]{0:T(1024)(128)(4,1)} %bitcast.2), calls=%async_computation | async-start | bytes 8388608
  20.4 33.0 %slice-start.1 = ((s8[4718592]{0:T(1024)(128)(4,1)}), s8[524288]{0:T(1024)(128)(4,1)S(1)}, s32[]{:S(2)}) async-start(s8[4718592]{0:T(1024)(128)(4,1)} %bitcast.2), calls=%async_computation.1 | async-start | bytes 1048576
  20.4 4.1 %collective-permute-start.10 = (bf16[2,128,512]{2,1,0:T(8,128)(2,1)S(1)}, bf16[2,128,512]{2,1,0:T(8,128)(2,1)S(1)}, u32[]{:S(2)}, u32[]{:S(2)}) collective-permute-start(bf16[2,128,512]{2,1,0:T(8,128)(2,1)S(1)} %get-tuple-element.25), channel_id=1, source_target_pairs={{0,1},{1,0},{2,3},{3,2},{4,5},{5,4},{6,7},{7,6},{8,9},{9,8},{10,11... | collective-permute-start | bytes 786440 | tf_op jit(solution)/shard_map/ppermute | solution.py:35
  24.4 8.7 %collective-permute-start.2 = (bf16[2,128,512]{2,1,0:T(8,128)(2,1)S(1)}, bf16[2,128,512]{2,1,0:T(8,128)(2,1)S(1)}, u32[]{:S(2)}, u32[]{:S(2)}) collective-permute-start(bf16[2,128,512]{2,1,0:T(8,128)(2,1)S(1)} %get-tuple-element.20), channel_id=1, source_target_pairs={{0,1},{1,0},{2,3},{3,2},{4,5},{5,4},{6,7},{7,6},{8,9},{9,8},{10,11... | collective-permute-start | bytes 786440 | tf_op jit(solution)/shard_map/ppermute | solution.py:35
  24.5 12.9 %collective-permute-start.11 = (bf16[2,64,512]{2,1,0:T(8,128)(2,1)S(1)}, bf16[2,64,512]{2,1,0:T(8,128)(2,1)S(1)}, u32[]{:S(2)}, u32[]{:S(2)}) collective-permute-start(bf16[2,64,512]{2,1,0:T(8,128)(2,1)S(1)} %get-tuple-element.27), channel_id=1, source_target_pairs={{0,2},{1,3},{2,0},{3,1},{4,6},{5,7},{6,4},{7,5},{8,10},{9,11},{10,... | collective-permute-start | bytes 393224 | tf_op jit(solution)/shard_map/ppermute | solution.py:35
  33.2 13.1 %collective-permute-start.3 = (bf16[2,64,512]{2,1,0:T(8,128)(2,1)S(1)}, bf16[2,64,512]{2,1,0:T(8,128)(2,1)S(1)}, u32[]{:S(2)}, u32[]{:S(2)}) collective-permute-start(bf16[2,64,512]{2,1,0:T(8,128)(2,1)S(1)} %get-tuple-element.22), channel_id=1, source_target_pairs={{0,2},{1,3},{2,0},{3,1},{4,6},{5,7},{6,4},{7,5},{8,10},{9,11},{10,... | collective-permute-start | bytes 393224 | tf_op jit(solution)/shard_map/ppermute | solution.py:35
  37.5 12.3 %collective-permute-start.15 = (bf16[2,64,512]{2,1,0:T(8,128)(2,1)S(1)}, bf16[2,64,512]{2,1,0:T(8,128)(2,1)S(1)}, u32[]{:S(2)}, u32[]{:S(2)}) collective-permute-start(bf16[2,64,512]{2,1,0:T(8,128)(2,1)S(1)} %shard_map.43), channel_id=1, source_target_pairs={{0,4},{1,8},{2,12},{3,0},{4,5},{5,9},{6,13},{7,1},{8,6},{9,10},{10... | collective-permute-start | bytes 393224 | tf_op jit(solution)/shard_map/ppermute | solution.py:39
  42.6 9.1 %collective-permute-start.14 = (bf16[2,64,512]{2,1,0:T(8,128)(2,1)S(1)}, bf16[2,64,512]{2,1,0:T(8,128)(2,1)S(1)}, u32[]{:S(2)}, u32[]{:S(2)}) collective-permute-start(bf16[2,64,512]{2,1,0:T(8,128)(2,1)S(1)} %shard_map.43), channel_id=1, source_target_pairs={{0,8},{1,12},{2,0},{3,4},{4,9},{5,13},{6,1},{7,5},{8,10},{9,14},{1... | collective-permute-start | bytes 393224 | tf_op jit(solution)/shard_map/ppermute | solution.py:39
  45.6 7.1 %collective-permute-start.13 = (bf16[2,64,512]{2,1,0:T(8,128)(2,1)S(1)}, bf16[2,64,512]{2,1,0:T(8,128)(2,1)S(1)}, u32[]{:S(2)}, u32[]{:S(2)}) collective-permute-start(bf16[2,64,512]{2,1,0:T(8,128)(2,1)S(1)} %shard_map.43), channel_id=1, source_target_pairs={{0,12},{1,0},{2,4},{3,8},{4,13},{5,1},{6,5},{7,9},{8,14},{9,2},{10... | collective-permute-start | bytes 393224 | tf_op jit(solution)/shard_map/ppermute | solution.py:39
  45.6 7.8 %collective-permute-start.12 = (bf16[2,64,512]{2,1,0:T(8,128)(2,1)S(1)}, bf16[2,64,512]{2,1,0:T(8,128)(2,1)S(1)}, u32[]{:S(2)}, u32[]{:S(2)}) collective-permute-start(bf16[2,64,512]{2,1,0:T(8,128)(2,1)S(1)} %shard_map.43), channel_id=1, source_target_pairs={{0,0},{1,4},{2,8},{3,12},{4,1},{5,5},{6,9},{7,13},{8,2},{9,6},{10,... | collective-permute-start | bytes 393224 | tf_op jit(solution)/shard_map/ppermute | solution.py:39
  46.4 19.0 %collective-permute-start.7 = (bf16[2,64,512]{2,1,0:T(8,128)(2,1)S(1)}, bf16[2,64,512]{2,1,0:T(8,128)(2,1)S(1)}, u32[]{:S(2)}, u32[]{:S(2)}) collective-permute-start(bf16[2,64,512]{2,1,0:T(8,128)(2,1)S(1)} %shard_map.39), channel_id=1, source_target_pairs={{0,4},{1,8},{2,12},{3,0},{4,5},{5,9},{6,13},{7,1},{8,6},{9,10},{10... | collective-permute-start | bytes 393224 | tf_op jit(solution)/shard_map/ppermute | solution.py:39
  49.8 15.6 %collective-permute-start.6 = (bf16[2,64,512]{2,1,0:T(8,128)(2,1)S(1)}, bf16[2,64,512]{2,1,0:T(8,128)(2,1)S(1)}, u32[]{:S(2)}, u32[]{:S(2)}) collective-permute-start(bf16[2,64,512]{2,1,0:T(8,128)(2,1)S(1)} %shard_map.39), channel_id=1, source_target_pairs={{0,8},{1,12},{2,0},{3,4},{4,9},{5,13},{6,1},{7,5},{8,10},{9,14},{1... | collective-permute-start | bytes 393224 | tf_op jit(solution)/shard_map/ppermute | solution.py:39
  51.7 13.6 %collective-permute-start.5 = (bf16[2,64,512]{2,1,0:T(8,128)(2,1)S(1)}, bf16[2,64,512]{2,1,0:T(8,128)(2,1)S(1)}, u32[]{:S(2)}, u32[]{:S(2)}) collective-permute-start(bf16[2,64,512]{2,1,0:T(8,128)(2,1)S(1)} %shard_map.39), channel_id=1, source_target_pairs={{0,12},{1,0},{2,4},{3,8},{4,13},{5,1},{6,5},{7,9},{8,14},{9,2},{10... | collective-permute-start | bytes 393224 | tf_op jit(solution)/shard_map/ppermute | solution.py:39
  52.7 12.7 %collective-permute-start.4 = (bf16[2,64,512]{2,1,0:T(8,128)(2,1)S(1)}, bf16[2,64,512]{2,1,0:T(8,128)(2,1)S(1)}, u32[]{:S(2)}, u32[]{:S(2)}) collective-permute-start(bf16[2,64,512]{2,1,0:T(8,128)(2,1)S(1)} %shard_map.39), channel_id=1, source_target_pairs={{0,0},{1,4},{2,8},{3,12},{4,1},{5,5},{6,9},{7,13},{8,2},{9,6},{10,... | collective-permute-start | bytes 393224 | tf_op jit(solution)/shard_map/ppermute | solution.py:39
  56.3 12.8 %collective-permute-start.17 = (bf16[1,256,512]{2,1,0:T(8,128)(2,1)S(1)}, bf16[1,256,512]{2,1,0:T(8,128)(2,1)S(1)}, u32[]{:S(2)}, u32[]{:S(2)}) collective-permute-start(bf16[1,256,512]{2,1,0:T(8,128)(2,1)S(1)} %get-tuple-element.30), channel_id=1, source_target_pairs={{0,1},{1,0},{2,3},{3,2},{4,5},{5,4},{6,7},{7,6},{8,9},{9,8},{10,11... | collective-permute-start | bytes 786440 | tf_op jit(solution)/shard_map/ppermute | solution.py:35
  68.3 2.0 %collective-permute-start.16 = (bf16[1,256,512]{2,1,0:T(8,128)(2,1)S(1)}, bf16[1,256,512]{2,1,0:T(8,128)(2,1)S(1)}, u32[]{:S(2)}, u32[]{:S(2)}) collective-permute-start(bf16[1,256,512]{2,1,0:T(8,128)(2,1)S(1)} %get-tuple-element.29), channel_id=1, source_target_pairs={{0,1},{1,0},{2,3},{3,2},{4,5},{5,4},{6,7},{7,6},{8,9},{9,8},{10,11... | collective-permute-start | bytes 786440 | tf_op jit(solution)/shard_map/ppermute | solution.py:35
  70.4 11.1 %collective-permute-start.18 = (bf16[1,256,512]{2,1,0:T(8,128)(2,1)S(1)}, bf16[1,256,512]{2,1,0:T(8,128)(2,1)S(1)}, u32[]{:S(2)}, u32[]{:S(2)}) collective-permute-start(bf16[1,256,512]{2,1,0:T(8,128)(2,1)S(1)} %get-tuple-element.32), channel_id=1, source_target_pairs={{0,2},{1,3},{2,0},{3,1},{4,6},{5,7},{6,4},{7,5},{8,10},{9,11},{10,... | collective-permute-start | bytes 786440 | tf_op jit(solution)/shard_map/ppermute | solution.py:35

commit v2 on v0

v2 whole, which is shorter than its diff:
```python
import functools

import jax
import jax.numpy as jnp
from jax import lax
from jax.experimental import pallas as pl
from jax.experimental.pallas import tpu as pltpu
from jax.sharding import PartitionSpec as P

VMEM = pl.BlockSpec(memory_space=pltpu.VMEM)
F32, BF16 = jnp.float32, jnp.bfloat16


def where_am_i():
    return lax.axis_index("chan"), lax.axis_index("img")


def after(x, *first):
    return lax.optimization_barrier((x, first))[0]


class Plan:
    def __init__(self, mesh, features, kernel):
        self.levels, self.cols = mesh.shape["chan"], mesh.shape["img"]
        self.pairs, self.ratio = self.cols // 2, self.levels // self.cols
        self.width = features.shape[2]
        self.pixels = features.shape[1] * features.shape[2]
        self.piece = features.shape[3]
        self.c_in, self.c_out = kernel.shape[2], kernel.shape[3]
        self.share = self.pixels // self.cols
        self.bits = self.cols.bit_length() - 1

    def wide(self, frames):
        return (frames, self.pixels + 2 * self.width, 3 * self.c_in)

    def spread_frame(self, x, turn):
        taken = []
        for e in range(self.ratio):
            moves = []
            for k in range(self.levels):
                for f in range(self.cols):
                    level = (f - turn) % self.cols * self.ratio + (k % self.ratio - e) % self.ratio
                    moves.append((k * self.cols + f, level * self.cols + k // self.ratio))
            taken.append(lax.ppermute(x, ("chan", "img"), moves))
        return taken

    def spread(self, x, turn):
        taken = []
        for e in range(self.ratio):
            moves = []
            for level in range(self.levels):
                v, u = level // self.ratio, level % self.ratio
                core, pair = v // self.pairs, (v + turn) % self.pairs
                for col in range(self.cols):
                    source = col * self.ratio + (u + e) % self.ratio
                    moves.append((source * self.cols + 2 * pair + core, level * self.cols + col))
            taken.append(lax.ppermute(x, ("chan", "img"), moves))
        return taken

    def lanes(self, level, e):
        if self.ratio == 1:
            return 0
        return pl.multiple_of((level + e) % self.ratio * self.piece, 128)

    def first_row(self, col):
        at, size = 0, self.pixels
        for bit in range(self.bits):
            size //= 2
            at = at + (col // 2**bit) % 2 * size
        return at

    def swap(self, x, bit):
        return lax.ppermute(x, "img", [(i, i ^ (1 << bit)) for i in range(self.cols)])

    def call(self, body, inputs, outputs, flops=0, scratch=()):
        moved = sum(x.size * x.dtype.itemsize for x in inputs)
        return pl.pallas_call(
            body,
            in_specs=[VMEM] * len(inputs),
            out_specs=[VMEM] * len(outputs),
            out_shape=[jax.ShapeDtypeStruct(*o) for o in outputs],
            scratch_shapes=list(scratch),
            cost_estimate=pl.CostEstimate(flops=flops, bytes_accessed=moved, transcendentals=0),
            compiler_params=pltpu.CompilerParams(vmem_limit_bytes=24 * 2**20),
        )(*inputs)


def stage_body(source, target, arrived):
    copy = pltpu.make_async_copy(source, target, arrived)
    copy.start()
    copy.wait()


def stage(kernel):
    return pl.pallas_call(
        stage_body,
        in_specs=[pl.BlockSpec(memory_space=pl.ANY)],
        out_specs=VMEM,
        out_shape=jax.ShapeDtypeStruct(kernel.shape, kernel.dtype),
        scratch_shapes=[pltpu.SemaphoreType.DMA],
        cost_estimate=pl.CostEstimate(flops=0, bytes_accessed=4 * kernel.size, transcendentals=0),
        compiler_params=pltpu.CompilerParams(vmem_limit_bytes=24 * 2**20),
    )(kernel)


def join_body(own, came, out):
    core = lax.axis_index("img") % 2
    out[pl.ds(core, 1)] = own[...].reshape((1,) + own.shape)
    out[pl.ds(1 - core, 1)] = came[...].reshape((1,) + came.shape)


def join(plan, own):
    return plan.call(join_body, [own, plan.swap(own, 0)], [((2,) + own.shape, own.dtype)])[0]


def place(plan, rows, frame, row_at, lane_at, wide):
    x = rows.astype(F32)
    column = lax.broadcasted_iota(jnp.int32, x.shape, 0) % plan.width
    left = jnp.where(column == 0, 0.0, pltpu.roll(x, 1, 0))
    right = jnp.where(column == plan.width - 1, 0.0, pltpu.roll(x, x.shape[0] - 1, 0))
    for b, moved in enumerate((left, x, right)):
        wide[frame, pl.ds(row_at, x.shape[0]), pl.ds(b * plan.c_in + lane_at, plan.piece)] = moved.astype(BF16)


def clear_edges(plan, wide):
    zero = jnp.zeros((plan.width, wide.shape[2]), BF16)
    for f in range(wide.shape[0]):
        wide[f, 0 : plan.width, :] = zero
        wide[f, plan.width + plan.pixels :, :] = zero


def times(plan, rows, kernel):
    summed = None
    for a in range(3):
        term = jnp.dot(rows(a), kernel[a].reshape(3 * plan.c_in, plan.c_out), preferred_element_type=F32)
        summed = term if summed is None else summed + term
    return summed


def half_rows(plan, wide, core, a):
    half = plan.pixels // 2
    rows = pl.ds(pl.multiple_of(core * half + a * plan.width, 16), half)
    return wide[:, rows, :].reshape(-1, 3 * plan.c_in)


def one_body(plan, *refs):
    pieces, (kernel, send, keep, wide) = refs[:-4], refs[-4:]
    level, col = where_am_i()
    clear_edges(plan, wide)
    for n, piece in enumerate(pieces):
        place(plan, piece[...], n // plan.ratio, plan.width, plan.lanes(level, n % plan.ratio), wide)
    halves = lambda a: jnp.concatenate([half_rows(plan, wide, core, a) for core in (1 - col % 2, col % 2)], axis=0)
    summed = times(plan, halves, kernel)
    size = summed.shape[0] // 2
    send[...] = summed[:size].astype(BF16).reshape(send.shape)
    keep[...] = summed[size:].reshape(keep.shape)


def conv_one(plan, pieces, kernel):
    frames = len(pieces) // plan.ratio
    half = (frames, plan.pixels // 2, plan.c_out)
    flops = 18 * frames * plan.pixels * plan.c_in * plan.c_out
    outputs = [(half, BF16), (half, F32)]
    scratch = [pltpu.VMEM(plan.wide(frames), BF16)]
    return plan.call(functools.partial(one_body, plan), [*pieces, kernel], outputs, flops, scratch)


def halve_body(bit, kept, came, keep, send):
    half = keep.shape[1]
    mine = (lax.axis_index("img") // 2**bit) % 2 * half
    a = pl.ds(pl.multiple_of(mine, 16), half)
    b = pl.ds(pl.multiple_of(half - mine, 16), half)
    send[...] = (kept[:, b, :] + came[:, b, :].astype(F32)).astype(BF16)
    keep[...] = kept[:, a, :] + came[:, a, :].astype(F32)


def silu_body(kept, came, hidden):
    v = kept[...] + came[...].astype(F32)
    hidden[...] = (v / (1.0 + jnp.exp(-v))).astype(BF16)


def halve(plan, bit, keep, came):
    half = (keep.shape[0], keep.shape[1] // 2, plan.c_out)
    return plan.call(functools.partial(halve_body, bit), [keep, came], [(half, F32), (half, BF16)])


def sum_one(plan, keep, came):
    keep, send = halve(plan, 1, keep, came)
    for bit in range(2, plan.bits):
        keep, send = halve(plan, bit, keep, plan.swap(send, bit - 1))
    return keep, send


def add_silu(plan, keep, came):
    return plan.call(silu_body, [keep, came], [(keep.shape, BF16)])[0]


def conv_two_body(plan, chosen, *refs):
    pieces, (kernel, out, wide) = refs[:-3], refs[-3:]
    level = lax.axis_index("chan")
    clear_edges(plan, wide)
    for n, piece in enumerate(pieces):
        turn, e = n // plan.ratio, n % plan.ratio
        pair = (level // plan.ratio + turn) % plan.pairs
        for core in range(2):
            row_at = pl.multiple_of(plan.width + plan.first_row(2 * pair + core), 16)
            for f, at in enumerate(chosen):
                place(plan, piece[core, at], f, row_at, plan.lanes(level, e), wide)
    rows = lambda a: wide[:, a * plan.width : a * plan.width + plan.pixels, :].reshape(-1, 3 * plan.c_in)
    out[...] = times(plan, rows, kernel).astype(out.dtype).reshape(out.shape)


def conv_two(plan, pieces, chosen, kernel, dtype):
    frames = len(chosen)
    return plan.call(
        functools.partial(conv_two_body, plan, chosen),
        [*pieces, kernel],
        [((frames, plan.pixels, plan.c_out), dtype)],
        18 * frames * plan.pixels * plan.c_in * plan.c_out,
        [pltpu.VMEM(plan.wide(frames), BF16)],
    )[0]


def aligned(bit, came, n):
    low = (lax.axis_index("img") // 2**bit) % 2 == 0
    return jnp.where(low, came[n - 1 if n else came.shape[0] - 1].astype(F32), came[n].astype(F32))


def merge_body(bit, at, kept, came, out):
    for n, t in enumerate(at):
        out[n] = (kept[n].astype(F32) + aligned(bit, came, t)).astype(out.dtype)


def merge(plan, bit, kept, came, at, dtype):
    body = functools.partial(merge_body, bit, at)
    return plan.call(body, [kept, came], [(kept.shape, dtype)])[0]


def last_body(kept, first, came, out):
    out[...] = (kept[...] + aligned(0, first, 0)[None] + came[...].astype(F32)).astype(BF16)


def sum_rest(plan, here, first, send):
    if plan.bits == 2:
        came = plan.swap(send, 1)
        return plan.call(last_body, [here, first, came], [(here.shape, BF16)])[0]
    keep = merge(plan, 0, here, first, range(0, 2 * here.shape[0], 2), F32)
    for bit in range(1, plan.bits):
        came = plan.swap(send, bit)
        count = keep.shape[0]
        total = merge(plan, bit, keep, came, range(count), F32 if count > 1 else BF16)
        keep, send = total[0::2], total[1::2].astype(BF16)
    return total


def shards(mesh, features, kernel_one, kernel_two):
    plan = Plan(mesh, features, kernel_one)
    block = features.reshape(plan.pixels, plan.piece)
    odd = list(range(1, plan.cols, 2))
    even = list(range(2, plan.cols, 4)) + list(range(0, plan.cols, 4))
    early = [p for d in odd for p in plan.spread_frame(block, d)]
    kernel_one = stage(kernel_one)
    late = [p for d in even for p in plan.spread_frame(block, d)]
    last = plan.bits - 1
    send, keep = conv_one(plan, early, kernel_one)
    keep, ahead = sum_one(plan, keep, after(plan.swap(send, 0), late))
    send, kept = conv_one(plan, after(late, ahead), kernel_one)
    hidden = join(plan, add_silu(plan, keep, after(plan.swap(ahead, last), send)))
    odds = [p for t in range(plan.pairs) for p in plan.spread(hidden, t)]
    keep, behind = sum_one(plan, kept, plan.swap(send, 0))
    hidden = join(plan, add_silu(plan, keep, plan.swap(behind, last)))
    evens = [p for t in range(plan.pairs) for p in plan.spread(hidden, t)]
    count = len(odd)
    sums = conv_two(plan, after(odds, hidden), range(count), kernel_two, BF16)
    came = plan.swap(after(sums, evens), 0)
    here = conv_two(plan, evens, range(count // 2), kernel_two, F32)
    send = merge(plan, 0, here, came, range(1, count, 2), BF16)
    here = conv_two(plan, evens, range(count // 2, count), kernel_two, F32)
    return sum_rest(plan, here, came, send).reshape(features.shape)


def solution(mesh):
    placed = (
        P(("groups", "img"), None, None, "chan"),
        P(None, None, "img", "chan"),
        P(None, None, "img", "chan"),
    )
    return jax.shard_map(
        functools.partial(shards, mesh),
        mesh=mesh,
        in_specs=placed,
        out_specs=P(("groups", "img"), None, None, "chan"),
        check_vma=False,
    )
```

time: 294 us -> 78.3 us (0.27)
  waiting for transfers between devices: 121 us -> 23.1 us
  local copies, waits for them, and re-layouts: 84.4 us -> 2.35 us
  starting transfers between devices: 0.12 us -> 39.5 us
  matrix products: 35 us -> 0 us
  blocking collectives: 34.1 us -> 0 us
  between operations: 13.4 us -> 0.16 us
  Pallas kernels: 0 us -> 12.9 us
  other arithmetic: 3.67 us -> 0.01 us
    all_gather x2 -> x0, waiting for transfers between devices: 60.3 us -> none  [apply_layer(): whole = lax.all_gather(active, 'chan', axis=3, tiled=True)]
    reduce_scatter x2 -> x0, waiting for transfers between devices: 60.3 us -> none  [apply_layer(): lax.psum_scatter(conv_padded(padded, kernel), 'img', scatter_dimension=0,...]
    ppermute x0 -> x16, starting transfers between devices: none -> 39.5 us  [the longest x8 23.6 us: swap(): return lax.ppermute(x, 'img', [(i, i ^ 1 << bit) for i in range(self.cols)])]
    dot_general x18 -> x0, matrix products: 35 us -> none  [conv_padded(): jnp.dot(window, kernel[offset_y, offset_x], preferred_element_type=jnp.fl...]
    all_to_all x2 -> x0, blocking collectives: 34.1 us -> none  [apply_layer(): lax.all_to_all(whole, 'img', split_axis=3, concat_axis=0, tiled=True)]
    unnamed x4 -> x6, local copies, waits for them, and re-layouts: 34.7 us -> 2.35 us
    ppermute x0 -> x16, waiting for transfers between devices: none -> 23.1 us  [the longest x8 10.5 us: swap(): return lax.ppermute(x, 'img', [(i, i ^ 1 << bit) for i in range(self.cols)])]
    all_gather x2 -> x0, local copies, waits for them, and re-layouts: 19.3 us -> none  [apply_layer(): whole = lax.all_gather(active, 'chan', axis=3, tiled=True)]
  transfers between devices with their start and end apart: 4 -> 16, of which waited for: 4 -> 8; matrix products, arithmetic and copies ran while one was open for 0% -> 0% of each run, Pallas kernels for 0% -> 12%
where the time goes in v2:
time: 78.3 us; the launch traced here: 78.1 us
  starting transfers between devices  39.5 us (50%)
  waiting for transfers between devices  23.1 us (30%)
  Pallas kernels  12.9 us (16%)
  local copies, waits for them, and re-layouts  2.35 us (3%)
    ppermute x8, starting transfers between devices, swap(): return lax.ppermute(x, 'img', [(i, i ^ 1 << bit) for i in range(self.cols)])  23.6 us
    pallas_call x13, Pallas kernels, call(): pl.pallas_call(body, in_specs=[VMEM] * len(inputs), out_specs=[VMEM] * le...  12.6 us
    ppermute x8, waiting for transfers between devices, swap(): return lax.ppermute(x, 'img', [(i, i ^ 1 << bit) for i in range(self.cols)])  10.5 us
    ppermute x4, waiting for transfers between devices, spread_frame(): taken.append(lax.ppermute(x, ('chan', 'img'), moves))  8.79 us
    ppermute x4, starting transfers between devices, spread_frame(): taken.append(lax.ppermute(x, ('chan', 'img'), moves))  8.17 us
    ppermute x4, starting transfers between devices, spread(): taken.append(lax.ppermute(x, ('chan', 'img'), moves))  7.74 us
    ppermute x4, waiting for transfers between devices, spread(): taken.append(lax.ppermute(x, ('chan', 'img'), moves))  3.83 us
    unnamed x6, local copies, waits for them, and re-layouts  2.35 us
  transfers between devices with their start and end apart: 16, of which 8 were waited for; matrix products, arithmetic and copies ran while one was open for 0% of the time, Pallas kernels for 12%

profile of v2, /device:TPU:0, one launch (start us, length us, event | category | flops | bytes accessed | tf_op | source)
XLA Modules:
  0.0 78.1 jit_solution(940808909268593205)
XLA Ops:
  0.0 5.0 %collective-permute-start.2 = (bf16[256,512]{1,0:T(8,128)(2,1)}, bf16[256,512]{1,0:T(8,128)(2,1)S(1)}, u32[]{:S(2)}, u32[]{:S(2)}) collective-permute-start(bf16[256,512]{1,0:T(8,128)(2,1)} %bitcast.4), channel_id=1, source_target_pairs={{0,12},{1,0},{2,4},{3,8},{4,13},{5,1},{6,5},{7,9},{8,14},{9,2},{10... | collective-permute-start | bytes 786440 | tf_op jit(solution)/shard_map/ppermute | solution.py:44
  5.0 0.0 collective-permute-start.3
  5.1 1.5 %collective-permute-start = (bf16[256,512]{1,0:T(8,128)(2,1)}, bf16[256,512]{1,0:T(8,128)(2,1)S(1)}, u32[]{:S(2)}, u32[]{:S(2)}) collective-permute-start(bf16[256,512]{1,0:T(8,128)(2,1)} %bitcast.6), channel_id=1, source_target_pairs={{0,8},{1,12},{2,0},{3,4},{4,9},{5,13},{6,1},{7,5},{8,10},{9,14},{1... | collective-permute-start | bytes 786440 | tf_op jit(solution)/shard_map/ppermute | solution.py:44
  6.6 1.6 %collective-permute-start.1 = (bf16[256,512]{1,0:T(8,128)(2,1)}, bf16[256,512]{1,0:T(8,128)(2,1)S(1)}, u32[]{:S(2)}, u32[]{:S(2)}) collective-permute-start(bf16[256,512]{1,0:T(8,128)(2,1)} %bitcast.7), channel_id=1, source_target_pairs={{0,0},{1,4},{2,8},{3,12},{4,1},{5,5},{6,9},{7,13},{8,2},{9,6},{10,... | collective-permute-start | bytes 786440 | tf_op jit(solution)/shard_map/ppermute | solution.py:44
  8.2 0.0 copy-start
  8.2 2.3 %copy-done = bf16[3,3,512,512]{3,2,1,0:T(8,128)(2,1)S(1)} copy-done((bf16[3,3,512,512]{3,2,1,0:T(8,128)(2,1)S(1)}, bf16[3,3,512,512]{3,2,1,0:T(8,128)(2,1)}, u32[]{:S(2)}) %copy-start) | copy-done | bytes 4718616
  10.5 0.3 shard_map.37.refs_2_
  10.8 0.4 collective-permute-done.2.refs_0_
  11.2 5.6 %collective-permute-done.3.refs_1_ = bf16[256,512]{1,0:T(8,128)(2,1)S(1)} collective-permute-done((bf16[256,512]{1,0:T(8,128)(2,1)}, bf16[256,512]{1,0:T(8,128)(2,1)S(1)}, u32[]{:S(2)}, u32[]{:S(2)}) %collective-permute-start.3) | collective-permute-done | bytes 262176 | tf_op jit(solution)/shard_map/ppermute | solution.py:44
  16.8 2.7 %shard_map.38 = (bf16[2,128,512]{2,1,0:T(8,128)(2,1)S(1)}, f32[2,128,512]{2,1,0:T(8,128)S(1)}) custom-call(bf16[256,512]{1,0:T(8,128)(2,1)S(1)} %collective-permute-done.2.refs_0_, bf16[256,512]{1,0:T(8,128)(2,1)S(1)} %collective-permute-done.3.refs_1_, bf16[3,3,512,512]{3,2,1,0:T(8,128)(2,1)S(1)} %shard_map.37.refs_2_), custom_call_target="tpu_custom_call" | custom-call | flops 2415919104 | bytes 5242880 | tf_op jit(solution)/shard_map/pallas_call | solution.py:77
  19.6 0.1 collective-permute-start.4
  19.6 2.8 %collective-permute-done.refs_0_ = bf16[256,512]{1,0:T(8,128)(2,1)S(1)} collective-permute-done((bf16[256,512]{1,0:T(8,128)(2,1)}, bf16[256,512]{1,0:T(8,128)(2,1)S(1)}, u32[]{:S(2)}, u32[]{:S(2)}) %collective-permute-start) | collective-permute-done | bytes 262176 | tf_op jit(solution)/shard_map/ppermute | solution.py:44
  22.4 0.0 collective-permute-done.1.refs_1_
  22.4 0.0 collective-permute-done.4.came
  22.4 0.0 slice-start
  22.4 0.1 shard_map.39
  22.5 0.0 slice-start.1
  22.5 2.7 %shard_map.40 = (bf16[2,128,512]{2,1,0:T(8,128)(2,1)S(1)}, f32[2,128,512]{2,1,0:T(8,128)S(1)}) custom-call(bf16[256,512]{1,0:T(8,128)(2,1)S(1)} %collective-permute-done.refs_0_, bf16[256,512]{1,0:T(8,128)(2,1)S(1)} %collective-permute-done.1.refs_1_, bf16[3,3,512,512]{3,2,1,0:T(8,128)(2,1)S(1)} %shard_map.37.refs_2_), custom_call_target="tpu_custom_call" | custom-call | flops 2415919104 | bytes 5242880 | tf_op jit(solution)/shard_map/pallas_call | solution.py:77
  25.3 1.1 %collective-permute-start.5 = (bf16[2,128,512]{2,1,0:T(8,128)(2,1)S(1)}, bf16[2,128,512]{2,1,0:T(8,128)(2,1)S(1)}, u32[]{:S(2)}, u32[]{:S(2)}) collective-permute-start(bf16[2,128,512]{2,1,0:T(8,128)(2,1)S(1)} %get-tuple-element.27), channel_id=1, source_target_pairs={{0,1},{1,0},{2,3},{3,2},{4,5},{5,4},{6,7},{7,6},{8,9},{9,8},{10,11... | collective-permute-start | bytes 786440 | tf_op jit(solution)/shard_map/ppermute | solution.py:73
  26.3 7.1 %collective-permute-start.10 = (bf16[2,64,512]{2,1,0:T(8,128)(2,1)S(1)}, bf16[2,64,512]{2,1,0:T(8,128)(2,1)S(1)}, u32[]{:S(2)}, u32[]{:S(2)}) collective-permute-start(bf16[2,64,512]{2,1,0:T(8,128)(2,1)S(1)} %get-tuple-element.23), channel_id=1, source_target_pairs={{0,2},{1,3},{2,0},{3,1},{4,6},{5,7},{6,4},{7,5},{8,10},{9,11},{10,... | collective-permute-start | bytes 393224 | tf_op jit(solution)/shard_map/ppermute | solution.py:73
  33.4 4.1 %collective-permute-done.10.came = bf16[2,64,512]{2,1,0:T(8,128)(2,1)S(1)} collective-permute-done((bf16[2,64,512]{2,1,0:T(8,128)(2,1)S(1)}, bf16[2,64,512]{2,1,0:T(8,128)(2,1)S(1)}, u32[]{:S(2)}, u32[]{:S(2)}) %collective-permute-start.10) | collective-permute-done | bytes 131104 | tf_op jit(solution)/shard_map/ppermute | solution.py:73
  37.5 0.1 shard_map.45.own
  37.6 0.1 collective-permute-start.11
  37.7 0.0 collective-permute-done.5.came
  37.7 0.1 shard_map.41
  37.7 1.8 %collective-permute-start.6 = (bf16[2,64,512]{2,1,0:T(8,128)(2,1)S(1)}, bf16[2,64,512]{2,1,0:T(8,128)(2,1)S(1)}, u32[]{:S(2)}, u32[]{:S(2)}) collective-permute-start(bf16[2,64,512]{2,1,0:T(8,128)(2,1)S(1)} %get-tuple-element.29), channel_id=1, source_target_pairs={{0,2},{1,3},{2,0},{3,1},{4,6},{5,7},{6,4},{7,5},{8,10},{9,11},{10,... | collective-permute-start | bytes 393224 | tf_op jit(solution)/shard_map/ppermute | solution.py:73
  39.6 0.0 collective-permute-done.11.came
  39.6 0.7 collective-permute-start.12
  40.3 3.1 %collective-permute-start.13 = (bf16[2,2,64,512]{3,2,1,0:T(8,128)(2,1)S(1)}, bf16[2,2,64,512]{3,2,1,0:T(8,128)(2,1)S(1)}, u32[]{:S(2)}, u32[]{:S(2)}) collective-permute-start(bf16[2,2,64,512]{3,2,1,0:T(8,128)(2,1)S(1)} %shard_map.46), channel_id=1, source_target_pairs={{2,0},{6,1},{10,2},{14,3},{0,4},{4,5},{8,6},{12,7},{3,8},{7,9},{11... | collective-permute-start | bytes 786440 | tf_op jit(solution)/shard_map/ppermute | solution.py:57
  43.4 0.3 collective-permute-done.6.came
  43.7 0.1 shard_map.42.own
  43.8 2.3 %collective-permute-start.7 = (bf16[2,64,512]{2,1,0:T(8,128)(2,1)S(1)}, bf16[2,64,512]{2,1,0:T(8,128)(2,1)S(1)}, u32[]{:S(2)}, u32[]{:S(2)}) collective-permute-start(bf16[2,64,512]{2,1,0:T(8,128)(2,1)S(1)} %shard_map.42.own), channel_id=1, source_target_pairs={{0,1},{1,0},{2,3},{3,2},{4,5},{5,4},{6,7},{7,6},{8,9},{9,8},{10,11... | collective-permute-start | bytes 393224 | tf_op jit(solution)/shard_map/ppermute | solution.py:73
  46.0 1.0 %collective-permute-done.7.came = bf16[2,64,512]{2,1,0:T(8,128)(2,1)S(1)} collective-permute-done((bf16[2,64,512]{2,1,0:T(8,128)(2,1)S(1)}, bf16[2,64,512]{2,1,0:T(8,128)(2,1)S(1)}, u32[]{:S(2)}, u32[]{:S(2)}) %collective-permute-start.7) | collective-permute-done | bytes 131104 | tf_op jit(solution)/shard_map/ppermute | solution.py:73
  47.1 0.7 collective-permute-start.8
  47.7 3.3 %collective-permute-start.9 = (bf16[2,2,64,512]{3,2,1,0:T(8,128)(2,1)S(1)}, bf16[2,2,64,512]{3,2,1,0:T(8,128)(2,1)S(1)}, u32[]{:S(2)}, u32[]{:S(2)}) collective-permute-start(bf16[2,2,64,512]{3,2,1,0:T(8,128)(2,1)S(1)} %shard_map.43), channel_id=1, source_target_pairs={{2,0},{6,1},{10,2},{14,3},{0,4},{4,5},{8,6},{12,7},{3,8},{7,9},{11... | collective-permute-start | bytes 786440 | tf_op jit(solution)/shard_map/ppermute | solution.py:57
  51.0 0.0 collective-permute-done.12.refs_0_
  51.0 0.0 collective-permute-done.13.refs_1_
  51.0 0.0 slice-done
  51.0 0.0 slice-done.1
  51.1 2.9 %shard_map.47 = bf16[2,256,512]{2,1,0:T(8,128)(2,1)S(1)} custom-call(bf16[2,2,64,512]{3,2,1,0:T(8,128)(2,1)S(1)} %collective-permute-done.12.refs_0_, bf16[2,2,64,512]{3,2,1,0:T(8,128)(2,1)S(1)} %collective-permute-done.13.refs_1_, bf16[3,3,512,512]{3,2,1,0:T(8,128)(2,1)S(1)} %bitcast.3), custom_call_target="tpu_custom_call" | custom-call | flops 2415919104 | bytes 5242880 | tf_op jit(solution)/shard_map/pallas_call | solution.py:77
  54.0 0.0 collective-permute-done.8.refs_0_
  54.0 3.8 %collective-permute-done.9.refs_1_ = bf16[2,2,64,512]{3,2,1,0:T(8,128)(2,1)S(1)} collective-permute-done((bf16[2,2,64,512]{3,2,1,0:T(8,128)(2,1)S(1)}, bf16[2,2,64,512]{3,2,1,0:T(8,128)(2,1)S(1)}, u32[]{:S(2)}, u32[]{:S(2)}) %collective-permute-start.9) | collective-permute-done | bytes 262176 | tf_op jit(solution)/shard_map/ppermute | solution.py:57
  57.8 2.0 %collective-permute-start.14 = (bf16[2,256,512]{2,1,0:T(8,128)(2,1)S(1)}, bf16[2,256,512]{2,1,0:T(8,128)(2,1)S(1)}, u32[]{:S(2)}, u32[]{:S(2)}) collective-permute-start(bf16[2,256,512]{2,1,0:T(8,128)(2,1)S(1)} %shard_map.47), channel_id=1, source_target_pairs={{0,1},{1,0},{2,3},{3,2},{4,5},{5,4},{6,7},{7,6},{8,9},{9,8},{10,11... | collective-permute-start | bytes 1572872 | tf_op jit(solution)/shard_map/ppermute | solution.py:73
  59.8 1.5 %shard_map.48.kept = f32[1,256,512]{2,1,0:T(8,128)S(1)} custom-call(bf16[2,2,64,512]{3,2,1,0:T(8,128)(2,1)S(1)} %collective-permute-done.8.refs_0_, bf16[2,2,64,512]{3,2,1,0:T(8,128)(2,1)S(1)} %collective-permute-done.9.refs_1_, bf16[3,3,512,512]{3,2,1,0:T(8,128)(2,1)S(1)} %bitcast.3), custom_call_target="tpu_custom_call" | custom-call | flops 1207959552 | bytes 5242880 | tf_op jit(solution)/shard_map/pallas_call | solution.py:77
  61.3 0.0 collective-permute-done.14.came.first
  61.4 0.1 shard_map.49
  61.5 9.2 %collective-permute-start.15 = (bf16[1,256,512]{2,1,0:T(8,128)(2,1)S(1)}, bf16[1,256,512]{2,1,0:T(8,128)(2,1)S(1)}, u32[]{:S(2)}, u32[]{:S(2)}) collective-permute-start(bf16[1,256,512]{2,1,0:T(8,128)(2,1)S(1)} %shard_map.49), channel_id=1, source_target_pairs={{0,2},{1,3},{2,0},{3,1},{4,6},{5,7},{6,4},{7,5},{8,10},{9,11},{10,... | collective-permute-start | bytes 786440 | tf_op jit(solution)/shard_map/ppermute | solution.py:73
  70.6 1.5 %shard_map.44.kept = f32[1,256,512]{2,1,0:T(8,128)S(1)} custom-call(bf16[2,2,64,512]{3,2,1,0:T(8,128)(2,1)S(1)} %collective-permute-done.8.refs_0_, bf16[2,2,64,512]{3,2,1,0:T(8,128)(2,1)S(1)} %collective-permute-done.9.refs_1_, bf16[3,3,512,512]{3,2,1,0:T(8,128)(2,1)S(1)} %bitcast.3), custom_call_target="tpu_custom_call" | custom-call | flops 1207959552 | bytes 5242880 | tf_op jit(solution)/shard_map/pallas_call | solution.py:77
  72.1 5.1 %collective-permute-done.15.came = bf16[1,256,512]{2,1,0:T(8,128)(2,1)S(1)} collective-permute-done((bf16[1,256,512]{2,1,0:T(8,128)(2,1)S(1)}, bf16[1,256,512]{2,1,0:T(8,128)(2,1)S(1)}, u32[]{:S(2)}, u32[]{:S(2)}) %collective-permute-start.15) | collective-permute-done | bytes 262176 | tf_op jit(solution)/shard_map/ppermute | solution.py:73
  77.2 0.8 %shard_map.50 = bf16[1,256,512]{2,1,0:T(8,128)(2,1)} custom-call(f32[1,256,512]{2,1,0:T(8,128)S(1)} %shard_map.44.kept, bf16[2,256,512]{2,1,0:T(8,128)(2,1)S(1)} %collective-permute-done.14.came.first, bf16[1,256,512]{2,1,0:T(8,128)(2,1)S(1)} %collective-permute-done.15.came), custom_call_target="tpu_custom_call" | custom-call | bytes 1310720 | tf_op jit(solution)/shard_map/pallas_call | solution.py:77
  (3 shorter events, 0.1 us)
Async XLA Ops:
  0.0 11.2 %collective-permute-start.2 = (bf16[256,512]{1,0:T(8,128)(2,1)}, bf16[256,512]{1,0:T(8,128)(2,1)S(1)}, u32[]{:S(2)}, u32[]{:S(2)}) collective-permute-start(bf16[256,512]{1,0:T(8,128)(2,1)} %bitcast.4), channel_id=1, source_target_pairs={{0,12},{1,0},{2,4},{3,8},{4,13},{5,1},{6,5},{7,9},{8,14},{9,2},{10... | collective-permute-start | bytes 786440 | tf_op jit(solution)/shard_map/ppermute | solution.py:44
  5.0 11.8 %collective-permute-start.3 = (bf16[256,512]{1,0:T(8,128)(2,1)}, bf16[256,512]{1,0:T(8,128)(2,1)S(1)}, u32[]{:S(2)}, u32[]{:S(2)}) collective-permute-start(bf16[256,512]{1,0:T(8,128)(2,1)} %bitcast.5), channel_id=1, source_target_pairs={{0,4},{1,8},{2,12},{3,0},{4,5},{5,9},{6,13},{7,1},{8,6},{9,10},{10... | collective-permute-start | bytes 786440 | tf_op jit(solution)/shard_map/ppermute | solution.py:44
  5.1 17.4 %collective-permute-start = (bf16[256,512]{1,0:T(8,128)(2,1)}, bf16[256,512]{1,0:T(8,128)(2,1)S(1)}, u32[]{:S(2)}, u32[]{:S(2)}) collective-permute-start(bf16[256,512]{1,0:T(8,128)(2,1)} %bitcast.6), channel_id=1, source_target_pairs={{0,8},{1,12},{2,0},{3,4},{4,9},{5,13},{6,1},{7,5},{8,10},{9,14},{1... | collective-permute-start | bytes 786440 | tf_op jit(solution)/shard_map/ppermute | solution.py:44
  6.6 15.9 %collective-permute-start.1 = (bf16[256,512]{1,0:T(8,128)(2,1)}, bf16[256,512]{1,0:T(8,128)(2,1)S(1)}, u32[]{:S(2)}, u32[]{:S(2)}) collective-permute-start(bf16[256,512]{1,0:T(8,128)(2,1)} %bitcast.7), channel_id=1, source_target_pairs={{0,0},{1,4},{2,8},{3,12},{4,1},{5,5},{6,9},{7,13},{8,2},{9,6},{10,... | collective-permute-start | bytes 786440 | tf_op jit(solution)/shard_map/ppermute | solution.py:44
  8.2 2.3 %copy-start = (bf16[3,3,512,512]{3,2,1,0:T(8,128)(2,1)S(1)}, bf16[3,3,512,512]{3,2,1,0:T(8,128)(2,1)}, u32[]{:S(2)}) copy-start(bf16[3,3,512,512]{3,2,1,0:T(8,128)(2,1)} %source.1) | copy-start | bytes 14155780
  19.6 2.9 %collective-permute-start.4 = (bf16[2,128,512]{2,1,0:T(8,128)(2,1)S(1)}, bf16[2,128,512]{2,1,0:T(8,128)(2,1)S(1)}, u32[]{:S(2)}, u32[]{:S(2)}) collective-permute-start(bf16[2,128,512]{2,1,0:T(8,128)(2,1)S(1)} %get-tuple-element.21), channel_id=1, source_target_pairs={{0,1},{1,0},{2,3},{3,2},{4,5},{5,4},{6,7},{7,6},{8,9},{9,8},{10,11... | collective-permute-start | bytes 786440 | tf_op jit(solution)/shard_map/ppermute | solution.py:73
  22.4 28.6 %slice-start = ((s8[4718592]{0:T(1024)(128)(4,1)}), s8[4194304]{0:T(1024)(128)(4,1)S(1)}, s32[]{:S(2)}) async-start(s8[4718592]{0:T(1024)(128)(4,1)} %bitcast.2), calls=%async_computation | async-start | bytes 8388608
  22.5 28.5 %slice-start.1 = ((s8[4718592]{0:T(1024)(128)(4,1)}), s8[524288]{0:T(1024)(128)(4,1)S(1)}, s32[]{:S(2)}) async-start(s8[4718592]{0:T(1024)(128)(4,1)} %bitcast.2), calls=%async_computation.1 | async-start | bytes 1048576
  25.3 12.4 %collective-permute-start.5 = (bf16[2,128,512]{2,1,0:T(8,128)(2,1)S(1)}, bf16[2,128,512]{2,1,0:T(8,128)(2,1)S(1)}, u32[]{:S(2)}, u32[]{:S(2)}) collective-permute-start(bf16[2,128,512]{2,1,0:T(8,128)(2,1)S(1)} %get-tuple-element.27), channel_id=1, source_target_pairs={{0,1},{1,0},{2,3},{3,2},{4,5},{5,4},{6,7},{7,6},{8,9},{9,8},{10,11... | collective-permute-start | bytes 786440 | tf_op jit(solution)/shard_map/ppermute | solution.py:73
  26.3 11.2 %collective-permute-start.10 = (bf16[2,64,512]{2,1,0:T(8,128)(2,1)S(1)}, bf16[2,64,512]{2,1,0:T(8,128)(2,1)S(1)}, u32[]{:S(2)}, u32[]{:S(2)}) collective-permute-start(bf16[2,64,512]{2,1,0:T(8,128)(2,1)S(1)} %get-tuple-element.23), channel_id=1, source_target_pairs={{0,2},{1,3},{2,0},{3,1},{4,6},{5,7},{6,4},{7,5},{8,10},{9,11},{10,... | collective-permute-start | bytes 393224 | tf_op jit(solution)/shard_map/ppermute | solution.py:73
  37.6 2.0 %collective-permute-start.11 = (bf16[2,64,512]{2,1,0:T(8,128)(2,1)S(1)}, bf16[2,64,512]{2,1,0:T(8,128)(2,1)S(1)}, u32[]{:S(2)}, u32[]{:S(2)}) collective-permute-start(bf16[2,64,512]{2,1,0:T(8,128)(2,1)S(1)} %shard_map.45.own), channel_id=1, source_target_pairs={{0,1},{1,0},{2,3},{3,2},{4,5},{5,4},{6,7},{7,6},{8,9},{9,8},{10,11... | collective-permute-start | bytes 393224 | tf_op jit(solution)/shard_map/ppermute | solution.py:73
  37.7 6.0 %collective-permute-start.6 = (bf16[2,64,512]{2,1,0:T(8,128)(2,1)S(1)}, bf16[2,64,512]{2,1,0:T(8,128)(2,1)S(1)}, u32[]{:S(2)}, u32[]{:S(2)}) collective-permute-start(bf16[2,64,512]{2,1,0:T(8,128)(2,1)S(1)} %get-tuple-element.29), channel_id=1, source_target_pairs={{0,2},{1,3},{2,0},{3,1},{4,6},{5,7},{6,4},{7,5},{8,10},{9,11},{10,... | collective-permute-start | bytes 393224 | tf_op jit(solution)/shard_map/ppermute | solution.py:73
  39.6 11.4 %collective-permute-start.12 = (bf16[2,2,64,512]{3,2,1,0:T(8,128)(2,1)S(1)}, bf16[2,2,64,512]{3,2,1,0:T(8,128)(2,1)S(1)}, u32[]{:S(2)}, u32[]{:S(2)}) collective-permute-start(bf16[2,2,64,512]{3,2,1,0:T(8,128)(2,1)S(1)} %shard_map.46), channel_id=1, source_target_pairs={{0,0},{4,1},{8,2},{12,3},{2,4},{6,5},{10,6},{14,7},{1,8},{5,9},{9,... | collective-permute-start | bytes 786440 | tf_op jit(solution)/shard_map/ppermute | solution.py:57
  40.3 10.8 %collective-permute-start.13 = (bf16[2,2,64,512]{3,2,1,0:T(8,128)(2,1)S(1)}, bf16[2,2,64,512]{3,2,1,0:T(8,128)(2,1)S(1)}, u32[]{:S(2)}, u32[]{:S(2)}) collective-permute-start(bf16[2,2,64,512]{3,2,1,0:T(8,128)(2,1)S(1)} %shard_map.46), channel_id=1, source_target_pairs={{2,0},{6,1},{10,2},{14,3},{0,4},{4,5},{8,6},{12,7},{3,8},{7,9},{11... | collective-permute-start | bytes 786440 | tf_op jit(solution)/shard_map/ppermute | solution.py:57
  43.8 3.3 %collective-permute-start.7 = (bf16[2,64,512]{2,1,0:T(8,128)(2,1)S(1)}, bf16[2,64,512]{2,1,0:T(8,128)(2,1)S(1)}, u32[]{:S(2)}, u32[]{:S(2)}) collective-permute-start(bf16[2,64,512]{2,1,0:T(8,128)(2,1)S(1)} %shard_map.42.own), channel_id=1, source_target_pairs={{0,1},{1,0},{2,3},{3,2},{4,5},{5,4},{6,7},{7,6},{8,9},{9,8},{10,11... | collective-permute-start | bytes 393224 | tf_op jit(solution)/shard_map/ppermute | solution.py:73
  47.1 6.9 %collective-permute-start.8 = (bf16[2,2,64,512]{3,2,1,0:T(8,128)(2,1)S(1)}, bf16[2,2,64,512]{3,2,1,0:T(8,128)(2,1)S(1)}, u32[]{:S(2)}, u32[]{:S(2)}) collective-permute-start(bf16[2,2,64,512]{3,2,1,0:T(8,128)(2,1)S(1)} %shard_map.43), channel_id=1, source_target_pairs={{0,0},{4,1},{8,2},{12,3},{2,4},{6,5},{10,6},{14,7},{1,8},{5,9},{9,... | collective-permute-start | bytes 786440 | tf_op jit(solution)/shard_map/ppermute | solution.py:57
  47.7 10.0 %collective-permute-start.9 = (bf16[2,2,64,512]{3,2,1,0:T(8,128)(2,1)S(1)}, bf16[2,2,64,512]{3,2,1,0:T(8,128)(2,1)S(1)}, u32[]{:S(2)}, u32[]{:S(2)}) collective-permute-start(bf16[2,2,64,512]{3,2,1,0:T(8,128)(2,1)S(1)} %shard_map.43), channel_id=1, source_target_pairs={{2,0},{6,1},{10,2},{14,3},{0,4},{4,5},{8,6},{12,7},{3,8},{7,9},{11... | collective-permute-start | bytes 786440 | tf_op jit(solution)/shard_map/ppermute | solution.py:57
  57.8 3.6 %collective-permute-start.14 = (bf16[2,256,512]{2,1,0:T(8,128)(2,1)S(1)}, bf16[2,256,512]{2,1,0:T(8,128)(2,1)S(1)}, u32[]{:S(2)}, u32[]{:S(2)}) collective-permute-start(bf16[2,256,512]{2,1,0:T(8,128)(2,1)S(1)} %shard_map.47), channel_id=1, source_target_pairs={{0,1},{1,0},{2,3},{3,2},{4,5},{5,4},{6,7},{7,6},{8,9},{9,8},{10,11... | collective-permute-start | bytes 1572872 | tf_op jit(solution)/shard_map/ppermute | solution.py:73
  61.5 15.8 %collective-permute-start.15 = (bf16[1,256,512]{2,1,0:T(8,128)(2,1)S(1)}, bf16[1,256,512]{2,1,0:T(8,128)(2,1)S(1)}, u32[]{:S(2)}, u32[]{:S(2)}) collective-permute-start(bf16[1,256,512]{2,1,0:T(8,128)(2,1)S(1)} %shard_map.49), channel_id=1, source_target_pairs={{0,2},{1,3},{2,0},{3,1},{4,6},{5,7},{6,4},{7,5},{8,10},{9,11},{10,... | collective-permute-start | bytes 786440 | tf_op jit(solution)/shard_map/ppermute | solution.py:73

commit v3 on v2

--- a/solution.py
+++ b/solution.py
@@ -267,7 +267,7 @@
     send, kept = conv_one(plan, after(late, ahead), kernel_one)
     hidden = join(plan, add_silu(plan, keep, after(plan.swap(ahead, last), send)))
     odds = [p for t in range(plan.pairs) for p in plan.spread(hidden, t)]
-    keep, behind = sum_one(plan, kept, plan.swap(send, 0))
+    keep, behind = sum_one(plan, kept, after(plan.swap(send, 0), hidden))
     hidden = join(plan, add_silu(plan, keep, plan.swap(behind, last)))
     evens = [p for t in range(plan.pairs) for p in plan.spread(hidden, t)]
     count = len(odd)

time: 78.3 us -> 75.3 us (0.962)
  waiting for transfers between devices: 23.1 us -> 20.3 us
    ppermute x8, waiting for transfers between devices: 10.5 us -> 7.67 us  [swap(): return lax.ppermute(x, 'img', [(i, i ^ 1 << bit) for i in range(self.cols)])]
  transfers between devices with their start and end apart: 16 -> 16, of which waited for: 8 -> 10; matrix products, arithmetic and copies ran while one was open for 0% -> 0% of each run, Pallas kernels for 12% -> 16%
where the time goes in v3:
time: 75.3 us; the launch traced here: 75.1 us
  starting transfers between devices  39.4 us (52%)
  waiting for transfers between devices  20.3 us (27%)
  Pallas kernels  12.9 us (17%)
  local copies, waits for them, and re-layouts  2.35 us (3%)
    ppermute x8, starting transfers between devices, swap(): return lax.ppermute(x, 'img', [(i, i ^ 1 << bit) for i in range(self.cols)])  23.8 us
    pallas_call x13, Pallas kernels, call(): pl.pallas_call(body, in_specs=[VMEM] * len(inputs), out_specs=[VMEM] * le...  12.6 us
    ppermute x4, waiting for transfers between devices, spread_frame(): taken.append(lax.ppermute(x, ('chan', 'img'), moves))  8.79 us
    ppermute x4, starting transfers between devices, spread_frame(): taken.append(lax.ppermute(x, ('chan', 'img'), moves))  8.17 us
    ppermute x8, waiting for transfers between devices, swap(): return lax.ppermute(x, 'img', [(i, i ^ 1 << bit) for i in range(self.cols)])  7.67 us
    ppermute x4, starting transfers between devices, spread(): taken.append(lax.ppermute(x, ('chan', 'img'), moves))  7.41 us
    ppermute x4, waiting for transfers between devices, spread(): taken.append(lax.ppermute(x, ('chan', 'img'), moves))  3.85 us
    unnamed x6, local copies, waits for them, and re-layouts  2.35 us
  transfers between devices with their start and end apart: 16, of which 10 were waited for; matrix products, arithmetic and copies ran while one was open for 0% of the time, Pallas kernels for 16%

profile of v3, /device:TPU:0, one launch (start us, length us, event | category | flops | bytes accessed | tf_op | source)
XLA Modules:
  0.0 75.1 jit_solution(14432790121621637375)
XLA Ops:
  0.0 5.0 %collective-permute-start.2 = (bf16[256,512]{1,0:T(8,128)(2,1)}, bf16[256,512]{1,0:T(8,128)(2,1)S(1)}, u32[]{:S(2)}, u32[]{:S(2)}) collective-permute-start(bf16[256,512]{1,0:T(8,128)(2,1)} %bitcast.4), channel_id=1, source_target_pairs={{0,12},{1,0},{2,4},{3,8},{4,13},{5,1},{6,5},{7,9},{8,14},{9,2},{10... | collective-permute-start | bytes 786440 | tf_op jit(solution)/shard_map/ppermute | solution.py:44
  5.0 0.0 collective-permute-start.3
  5.1 1.5 %collective-permute-start = (bf16[256,512]{1,0:T(8,128)(2,1)}, bf16[256,512]{1,0:T(8,128)(2,1)S(1)}, u32[]{:S(2)}, u32[]{:S(2)}) collective-permute-start(bf16[256,512]{1,0:T(8,128)(2,1)} %bitcast.6), channel_id=1, source_target_pairs={{0,8},{1,12},{2,0},{3,4},{4,9},{5,13},{6,1},{7,5},{8,10},{9,14},{1... | collective-permute-start | bytes 786440 | tf_op jit(solution)/shard_map/ppermute | solution.py:44
  6.6 1.6 %collective-permute-start.1 = (bf16[256,512]{1,0:T(8,128)(2,1)}, bf16[256,512]{1,0:T(8,128)(2,1)S(1)}, u32[]{:S(2)}, u32[]{:S(2)}) collective-permute-start(bf16[256,512]{1,0:T(8,128)(2,1)} %bitcast.7), channel_id=1, source_target_pairs={{0,0},{1,4},{2,8},{3,12},{4,1},{5,5},{6,9},{7,13},{8,2},{9,6},{10,... | collective-permute-start | bytes 786440 | tf_op jit(solution)/shard_map/ppermute | solution.py:44
  8.2 0.0 copy-start
  8.2 2.3 %copy-done = bf16[3,3,512,512]{3,2,1,0:T(8,128)(2,1)S(1)} copy-done((bf16[3,3,512,512]{3,2,1,0:T(8,128)(2,1)S(1)}, bf16[3,3,512,512]{3,2,1,0:T(8,128)(2,1)}, u32[]{:S(2)}) %copy-start) | copy-done | bytes 4718616
  10.5 0.3 shard_map.37.refs_2_
  10.8 0.4 collective-permute-done.2.refs_0_
  11.2 5.6 %collective-permute-done.3.refs_1_ = bf16[256,512]{1,0:T(8,128)(2,1)S(1)} collective-permute-done((bf16[256,512]{1,0:T(8,128)(2,1)}, bf16[256,512]{1,0:T(8,128)(2,1)S(1)}, u32[]{:S(2)}, u32[]{:S(2)}) %collective-permute-start.3) | collective-permute-done | bytes 262176 | tf_op jit(solution)/shard_map/ppermute | solution.py:44
  16.8 2.7 %shard_map.38 = (bf16[2,128,512]{2,1,0:T(8,128)(2,1)S(1)}, f32[2,128,512]{2,1,0:T(8,128)S(1)}) custom-call(bf16[256,512]{1,0:T(8,128)(2,1)S(1)} %collective-permute-done.2.refs_0_, bf16[256,512]{1,0:T(8,128)(2,1)S(1)} %collective-permute-done.3.refs_1_, bf16[3,3,512,512]{3,2,1,0:T(8,128)(2,1)S(1)} %shard_map.37.refs_2_), custom_call_target="tpu_custom_call" | custom-call | flops 2415919104 | bytes 5242880 | tf_op jit(solution)/shard_map/pallas_call | solution.py:77
  19.6 0.1 collective-permute-start.4
  19.6 2.8 %collective-permute-done.refs_0_ = bf16[256,512]{1,0:T(8,128)(2,1)S(1)} collective-permute-done((bf16[256,512]{1,0:T(8,128)(2,1)}, bf16[256,512]{1,0:T(8,128)(2,1)S(1)}, u32[]{:S(2)}, u32[]{:S(2)}) %collective-permute-start) | collective-permute-done | bytes 262176 | tf_op jit(solution)/shard_map/ppermute | solution.py:44
  22.4 0.0 collective-permute-done.1.refs_1_
  22.4 0.0 collective-permute-done.4.came
  22.5 0.0 slice-start
  22.5 0.0 slice-start.1
  22.5 8.1 %collective-permute-start.6 = (bf16[2,64,512]{2,1,0:T(8,128)(2,1)S(1)}, bf16[2,64,512]{2,1,0:T(8,128)(2,1)S(1)}, u32[]{:S(2)}, u32[]{:S(2)}) collective-permute-start(bf16[2,64,512]{2,1,0:T(8,128)(2,1)S(1)} %get-tuple-element.24), channel_id=1, source_target_pairs={{0,2},{1,3},{2,0},{3,1},{4,6},{5,7},{6,4},{7,5},{8,10},{9,11},{10,... | collective-permute-start | bytes 393224 | tf_op jit(solution)/shard_map/ppermute | solution.py:73
  30.6 2.7 %shard_map.40 = (bf16[2,128,512]{2,1,0:T(8,128)(2,1)S(1)}, f32[2,128,512]{2,1,0:T(8,128)S(1)}) custom-call(bf16[256,512]{1,0:T(8,128)(2,1)S(1)} %collective-permute-done.refs_0_, bf16[256,512]{1,0:T(8,128)(2,1)S(1)} %collective-permute-done.1.refs_1_, bf16[3,3,512,512]{3,2,1,0:T(8,128)(2,1)S(1)} %shard_map.37.refs_2_), custom_call_target="tpu_custom_call" | custom-call | flops 2415919104 | bytes 5242880 | tf_op jit(solution)/shard_map/pallas_call | solution.py:77
  33.3 0.1 collective-permute-start.5
  33.4 0.2 collective-permute-done.6.came
  33.6 0.1 shard_map.41.own
  33.6 0.4 collective-permute-start.7
  34.1 1.1 %collective-permute-done.7.came = bf16[2,64,512]{2,1,0:T(8,128)(2,1)S(1)} collective-permute-done((bf16[2,64,512]{2,1,0:T(8,128)(2,1)S(1)}, bf16[2,64,512]{2,1,0:T(8,128)(2,1)S(1)}, u32[]{:S(2)}, u32[]{:S(2)}) %collective-permute-start.7) | collective-permute-done | bytes 131104 | tf_op jit(solution)/shard_map/ppermute | solution.py:73
  35.1 0.0 collective-permute-done.5.came
  35.2 0.1 shard_map.43
  35.2 2.0 %collective-permute-start.8 = (bf16[2,64,512]{2,1,0:T(8,128)(2,1)S(1)}, bf16[2,64,512]{2,1,0:T(8,128)(2,1)S(1)}, u32[]{:S(2)}, u32[]{:S(2)}) collective-permute-start(bf16[2,64,512]{2,1,0:T(8,128)(2,1)S(1)} %get-tuple-element.33), channel_id=1, source_target_pairs={{0,2},{1,3},{2,0},{3,1},{4,6},{5,7},{6,4},{7,5},{8,10},{9,11},{10,... | collective-permute-start | bytes 393224 | tf_op jit(solution)/shard_map/ppermute | solution.py:73
  37.2 0.7 collective-permute-start.12
  37.9 2.8 %collective-permute-start.13 = (bf16[2,2,64,512]{3,2,1,0:T(8,128)(2,1)S(1)}, bf16[2,2,64,512]{3,2,1,0:T(8,128)(2,1)S(1)}, u32[]{:S(2)}, u32[]{:S(2)}) collective-permute-start(bf16[2,2,64,512]{3,2,1,0:T(8,128)(2,1)S(1)} %shard_map.42), channel_id=1, source_target_pairs={{2,0},{6,1},{10,2},{14,3},{0,4},{4,5},{8,6},{12,7},{3,8},{7,9},{11... | collective-permute-start | bytes 786440 | tf_op jit(solution)/shard_map/ppermute | solution.py:57
  40.7 0.3 collective-permute-done.8.came
  41.1 0.1 shard_map.44.own
  41.1 1.4 %collective-permute-start.9 = (bf16[2,64,512]{2,1,0:T(8,128)(2,1)S(1)}, bf16[2,64,512]{2,1,0:T(8,128)(2,1)S(1)}, u32[]{:S(2)}, u32[]{:S(2)}) collective-permute-start(bf16[2,64,512]{2,1,0:T(8,128)(2,1)S(1)} %shard_map.44.own), channel_id=1, source_target_pairs={{0,1},{1,0},{2,3},{3,2},{4,5},{5,4},{6,7},{7,6},{8,9},{9,8},{10,11... | collective-permute-start | bytes 393224 | tf_op jit(solution)/shard_map/ppermute | solution.py:73
  42.5 1.0 %collective-permute-done.9.came = bf16[2,64,512]{2,1,0:T(8,128)(2,1)S(1)} collective-permute-done((bf16[2,64,512]{2,1,0:T(8,128)(2,1)S(1)}, bf16[2,64,512]{2,1,0:T(8,128)(2,1)S(1)}, u32[]{:S(2)}, u32[]{:S(2)}) %collective-permute-start.9) | collective-permute-done | bytes 131104 | tf_op jit(solution)/shard_map/ppermute | solution.py:73
  43.5 0.7 collective-permute-start.10
  44.2 3.3 %collective-permute-start.11 = (bf16[2,2,64,512]{3,2,1,0:T(8,128)(2,1)S(1)}, bf16[2,2,64,512]{3,2,1,0:T(8,128)(2,1)S(1)}, u32[]{:S(2)}, u32[]{:S(2)}) collective-permute-start(bf16[2,2,64,512]{3,2,1,0:T(8,128)(2,1)S(1)} %shard_map.45), channel_id=1, source_target_pairs={{2,0},{6,1},{10,2},{14,3},{0,4},{4,5},{8,6},{12,7},{3,8},{7,9},{11... | collective-permute-start | bytes 786440 | tf_op jit(solution)/shard_map/ppermute | solution.py:57
  47.5 0.0 collective-permute-done.12.refs_0_
  47.5 0.7 collective-permute-done.13.refs_1_
  48.2 0.0 slice-done
  48.2 0.0 slice-done.1
  48.2 2.9 %shard_map.47 = bf16[2,256,512]{2,1,0:T(8,128)(2,1)S(1)} custom-call(bf16[2,2,64,512]{3,2,1,0:T(8,128)(2,1)S(1)} %collective-permute-done.12.refs_0_, bf16[2,2,64,512]{3,2,1,0:T(8,128)(2,1)S(1)} %collective-permute-done.13.refs_1_, bf16[3,3,512,512]{3,2,1,0:T(8,128)(2,1)S(1)} %bitcast.3), custom_call_target="tpu_custom_call" | custom-call | flops 2415919104 | bytes 5242880 | tf_op jit(solution)/shard_map/pallas_call | solution.py:77
  51.1 0.0 collective-permute-done.10.refs_0_
  51.1 3.2 %collective-permute-done.11.refs_1_ = bf16[2,2,64,512]{3,2,1,0:T(8,128)(2,1)S(1)} collective-permute-done((bf16[2,2,64,512]{3,2,1,0:T(8,128)(2,1)S(1)}, bf16[2,2,64,512]{3,2,1,0:T(8,128)(2,1)S(1)}, u32[]{:S(2)}, u32[]{:S(2)}) %collective-permute-start.11) | collective-permute-done | bytes 262176 | tf_op jit(solution)/shard_map/ppermute | solution.py:57
  54.3 2.1 %collective-permute-start.14 = (bf16[2,256,512]{2,1,0:T(8,128)(2,1)S(1)}, bf16[2,256,512]{2,1,0:T(8,128)(2,1)S(1)}, u32[]{:S(2)}, u32[]{:S(2)}) collective-permute-start(bf16[2,256,512]{2,1,0:T(8,128)(2,1)S(1)} %shard_map.47), channel_id=1, source_target_pairs={{0,1},{1,0},{2,3},{3,2},{4,5},{5,4},{6,7},{7,6},{8,9},{9,8},{10,11... | collective-permute-start | bytes 1572872 | tf_op jit(solution)/shard_map/ppermute | solution.py:73
  56.4 1.5 %shard_map.48.kept = f32[1,256,512]{2,1,0:T(8,128)S(1)} custom-call(bf16[2,2,64,512]{3,2,1,0:T(8,128)(2,1)S(1)} %collective-permute-done.10.refs_0_, bf16[2,2,64,512]{3,2,1,0:T(8,128)(2,1)S(1)} %collective-permute-done.11.refs_1_, bf16[3,3,512,512]{3,2,1,0:T(8,128)(2,1)S(1)} %bitcast.3), custom_call_target="tpu_custom_call" | custom-call | flops 1207959552 | bytes 5242880 | tf_op jit(solution)/shard_map/pallas_call | solution.py:77
  57.9 0.0 collective-permute-done.14.came.first
  58.0 0.1 shard_map.49
  58.0 9.6 %collective-permute-start.15 = (bf16[1,256,512]{2,1,0:T(8,128)(2,1)S(1)}, bf16[1,256,512]{2,1,0:T(8,128)(2,1)S(1)}, u32[]{:S(2)}, u32[]{:S(2)}) collective-permute-start(bf16[1,256,512]{2,1,0:T(8,128)(2,1)S(1)} %shard_map.49), channel_id=1, source_target_pairs={{0,2},{1,3},{2,0},{3,1},{4,6},{5,7},{6,4},{7,5},{8,10},{9,11},{10,... | collective-permute-start | bytes 786440 | tf_op jit(solution)/shard_map/ppermute | solution.py:73
  67.7 1.5 %shard_map.46.kept = f32[1,256,512]{2,1,0:T(8,128)S(1)} custom-call(bf16[2,2,64,512]{3,2,1,0:T(8,128)(2,1)S(1)} %collective-permute-done.10.refs_0_, bf16[2,2,64,512]{3,2,1,0:T(8,128)(2,1)S(1)} %collective-permute-done.11.refs_1_, bf16[3,3,512,512]{3,2,1,0:T(8,128)(2,1)S(1)} %bitcast.3), custom_call_target="tpu_custom_call" | custom-call | flops 1207959552 | bytes 5242880 | tf_op jit(solution)/shard_map/pallas_call | solution.py:77
  69.2 5.1 %collective-permute-done.15.came = bf16[1,256,512]{2,1,0:T(8,128)(2,1)S(1)} collective-permute-done((bf16[1,256,512]{2,1,0:T(8,128)(2,1)S(1)}, bf16[1,256,512]{2,1,0:T(8,128)(2,1)S(1)}, u32[]{:S(2)}, u32[]{:S(2)}) %collective-permute-start.15) | collective-permute-done | bytes 262176 | tf_op jit(solution)/shard_map/ppermute | solution.py:73
  74.3 0.8 %shard_map.50 = bf16[1,256,512]{2,1,0:T(8,128)(2,1)} custom-call(f32[1,256,512]{2,1,0:T(8,128)S(1)} %shard_map.46.kept, bf16[2,256,512]{2,1,0:T(8,128)(2,1)S(1)} %collective-permute-done.14.came.first, bf16[1,256,512]{2,1,0:T(8,128)(2,1)S(1)} %collective-permute-done.15.came), custom_call_target="tpu_custom_call" | custom-call | bytes 1310720 | tf_op jit(solution)/shard_map/pallas_call | solution.py:77
  (4 shorter events, 0.1 us)
Async XLA Ops:
  0.0 11.2 %collective-permute-start.2 = (bf16[256,512]{1,0:T(8,128)(2,1)}, bf16[256,512]{1,0:T(8,128)(2,1)S(1)}, u32[]{:S(2)}, u32[]{:S(2)}) collective-permute-start(bf16[256,512]{1,0:T(8,128)(2,1)} %bitcast.4), channel_id=1, source_target_pairs={{0,12},{1,0},{2,4},{3,8},{4,13},{5,1},{6,5},{7,9},{8,14},{9,2},{10... | collective-permute-start | bytes 786440 | tf_op jit(solution)/shard_map/ppermute | solution.py:44
  5.0 11.8 %collective-permute-start.3 = (bf16[256,512]{1,0:T(8,128)(2,1)}, bf16[256,512]{1,0:T(8,128)(2,1)S(1)}, u32[]{:S(2)}, u32[]{:S(2)}) collective-permute-start(bf16[256,512]{1,0:T(8,128)(2,1)} %bitcast.5), channel_id=1, source_target_pairs={{0,4},{1,8},{2,12},{3,0},{4,5},{5,9},{6,13},{7,1},{8,6},{9,10},{10... | collective-permute-start | bytes 786440 | tf_op jit(solution)/shard_map/ppermute | solution.py:44
  5.1 17.4 %collective-permute-start = (bf16[256,512]{1,0:T(8,128)(2,1)}, bf16[256,512]{1,0:T(8,128)(2,1)S(1)}, u32[]{:S(2)}, u32[]{:S(2)}) collective-permute-start(bf16[256,512]{1,0:T(8,128)(2,1)} %bitcast.6), channel_id=1, source_target_pairs={{0,8},{1,12},{2,0},{3,4},{4,9},{5,13},{6,1},{7,5},{8,10},{9,14},{1... | collective-permute-start | bytes 786440 | tf_op jit(solution)/shard_map/ppermute | solution.py:44
  6.6 15.9 %collective-permute-start.1 = (bf16[256,512]{1,0:T(8,128)(2,1)}, bf16[256,512]{1,0:T(8,128)(2,1)S(1)}, u32[]{:S(2)}, u32[]{:S(2)}) collective-permute-start(bf16[256,512]{1,0:T(8,128)(2,1)} %bitcast.7), channel_id=1, source_target_pairs={{0,0},{1,4},{2,8},{3,12},{4,1},{5,5},{6,9},{7,13},{8,2},{9,6},{10,... | collective-permute-start | bytes 786440 | tf_op jit(solution)/shard_map/ppermute | solution.py:44
  8.2 2.3 %copy-start = (bf16[3,3,512,512]{3,2,1,0:T(8,128)(2,1)S(1)}, bf16[3,3,512,512]{3,2,1,0:T(8,128)(2,1)}, u32[]{:S(2)}) copy-start(bf16[3,3,512,512]{3,2,1,0:T(8,128)(2,1)} %source.1) | copy-start | bytes 14155780
  19.6 2.9 %collective-permute-start.4 = (bf16[2,128,512]{2,1,0:T(8,128)(2,1)S(1)}, bf16[2,128,512]{2,1,0:T(8,128)(2,1)S(1)}, u32[]{:S(2)}, u32[]{:S(2)}) collective-permute-start(bf16[2,128,512]{2,1,0:T(8,128)(2,1)S(1)} %get-tuple-element.22), channel_id=1, source_target_pairs={{0,1},{1,0},{2,3},{3,2},{4,5},{5,4},{6,7},{7,6},{8,9},{9,8},{10,11... | collective-permute-start | bytes 786440 | tf_op jit(solution)/shard_map/ppermute | solution.py:73
  22.5 25.7 %slice-start = ((s8[4718592]{0:T(1024)(128)(4,1)}), s8[4194304]{0:T(1024)(128)(4,1)S(1)}, s32[]{:S(2)}) async-start(s8[4718592]{0:T(1024)(128)(4,1)} %bitcast.2), calls=%async_computation | async-start | bytes 8388608
  22.5 25.7 %slice-start.1 = ((s8[4718592]{0:T(1024)(128)(4,1)}), s8[524288]{0:T(1024)(128)(4,1)S(1)}, s32[]{:S(2)}) async-start(s8[4718592]{0:T(1024)(128)(4,1)} %bitcast.2), calls=%async_computation.1 | async-start | bytes 1048576
  22.5 11.0 %collective-permute-start.6 = (bf16[2,64,512]{2,1,0:T(8,128)(2,1)S(1)}, bf16[2,64,512]{2,1,0:T(8,128)(2,1)S(1)}, u32[]{:S(2)}, u32[]{:S(2)}) collective-permute-start(bf16[2,64,512]{2,1,0:T(8,128)(2,1)S(1)} %get-tuple-element.24), channel_id=1, source_target_pairs={{0,2},{1,3},{2,0},{3,1},{4,6},{5,7},{6,4},{7,5},{8,10},{9,11},{10,... | collective-permute-start | bytes 393224 | tf_op jit(solution)/shard_map/ppermute | solution.py:73
  33.3 1.8 %collective-permute-start.5 = (bf16[2,128,512]{2,1,0:T(8,128)(2,1)S(1)}, bf16[2,128,512]{2,1,0:T(8,128)(2,1)S(1)}, u32[]{:S(2)}, u32[]{:S(2)}) collective-permute-start(bf16[2,128,512]{2,1,0:T(8,128)(2,1)S(1)} %get-tuple-element.28), channel_id=1, source_target_pairs={{0,1},{1,0},{2,3},{3,2},{4,5},{5,4},{6,7},{7,6},{8,9},{9,8},{10,11... | collective-permute-start | bytes 786440 | tf_op jit(solution)/shard_map/ppermute | solution.py:73
  33.6 1.5 %collective-permute-start.7 = (bf16[2,64,512]{2,1,0:T(8,128)(2,1)S(1)}, bf16[2,64,512]{2,1,0:T(8,128)(2,1)S(1)}, u32[]{:S(2)}, u32[]{:S(2)}) collective-permute-start(bf16[2,64,512]{2,1,0:T(8,128)(2,1)S(1)} %shard_map.41.own), channel_id=1, source_target_pairs={{0,1},{1,0},{2,3},{3,2},{4,5},{5,4},{6,7},{7,6},{8,9},{9,8},{10,11... | collective-permute-start | bytes 393224 | tf_op jit(solution)/shard_map/ppermute | solution.py:73
  35.2 5.8 %collective-permute-start.8 = (bf16[2,64,512]{2,1,0:T(8,128)(2,1)S(1)}, bf16[2,64,512]{2,1,0:T(8,128)(2,1)S(1)}, u32[]{:S(2)}, u32[]{:S(2)}) collective-permute-start(bf16[2,64,512]{2,1,0:T(8,128)(2,1)S(1)} %get-tuple-element.33), channel_id=1, source_target_pairs={{0,2},{1,3},{2,0},{3,1},{4,6},{5,7},{6,4},{7,5},{8,10},{9,11},{10,... | collective-permute-start | bytes 393224 | tf_op jit(solution)/shard_map/ppermute | solution.py:73
  37.2 10.3 %collective-permute-start.12 = (bf16[2,2,64,512]{3,2,1,0:T(8,128)(2,1)S(1)}, bf16[2,2,64,512]{3,2,1,0:T(8,128)(2,1)S(1)}, u32[]{:S(2)}, u32[]{:S(2)}) collective-permute-start(bf16[2,2,64,512]{3,2,1,0:T(8,128)(2,1)S(1)} %shard_map.42), channel_id=1, source_target_pairs={{0,0},{4,1},{8,2},{12,3},{2,4},{6,5},{10,6},{14,7},{1,8},{5,9},{9,... | collective-permute-start | bytes 786440 | tf_op jit(solution)/shard_map/ppermute | solution.py:57
  37.9 10.3 %collective-permute-start.13 = (bf16[2,2,64,512]{3,2,1,0:T(8,128)(2,1)S(1)}, bf16[2,2,64,512]{3,2,1,0:T(8,128)(2,1)S(1)}, u32[]{:S(2)}, u32[]{:S(2)}) collective-permute-start(bf16[2,2,64,512]{3,2,1,0:T(8,128)(2,1)S(1)} %shard_map.42), channel_id=1, source_target_pairs={{2,0},{6,1},{10,2},{14,3},{0,4},{4,5},{8,6},{12,7},{3,8},{7,9},{11... | collective-permute-start | bytes 786440 | tf_op jit(solution)/shard_map/ppermute | solution.py:57
  41.1 2.4 %collective-permute-start.9 = (bf16[2,64,512]{2,1,0:T(8,128)(2,1)S(1)}, bf16[2,64,512]{2,1,0:T(8,128)(2,1)S(1)}, u32[]{:S(2)}, u32[]{:S(2)}) collective-permute-start(bf16[2,64,512]{2,1,0:T(8,128)(2,1)S(1)} %shard_map.44.own), channel_id=1, source_target_pairs={{0,1},{1,0},{2,3},{3,2},{4,5},{5,4},{6,7},{7,6},{8,9},{9,8},{10,11... | collective-permute-start | bytes 393224 | tf_op jit(solution)/shard_map/ppermute | solution.py:73
  43.5 7.6 %collective-permute-start.10 = (bf16[2,2,64,512]{3,2,1,0:T(8,128)(2,1)S(1)}, bf16[2,2,64,512]{3,2,1,0:T(8,128)(2,1)S(1)}, u32[]{:S(2)}, u32[]{:S(2)}) collective-permute-start(bf16[2,2,64,512]{3,2,1,0:T(8,128)(2,1)S(1)} %shard_map.45), channel_id=1, source_target_pairs={{0,0},{4,1},{8,2},{12,3},{2,4},{6,5},{10,6},{14,7},{1,8},{5,9},{9,... | collective-permute-start | bytes 786440 | tf_op jit(solution)/shard_map/ppermute | solution.py:57
  44.2 10.0 %collective-permute-start.11 = (bf16[2,2,64,512]{3,2,1,0:T(8,128)(2,1)S(1)}, bf16[2,2,64,512]{3,2,1,0:T(8,128)(2,1)S(1)}, u32[]{:S(2)}, u32[]{:S(2)}) collective-permute-start(bf16[2,2,64,512]{3,2,1,0:T(8,128)(2,1)S(1)} %shard_map.45), channel_id=1, source_target_pairs={{2,0},{6,1},{10,2},{14,3},{0,4},{4,5},{8,6},{12,7},{3,8},{7,9},{11... | collective-permute-start | bytes 786440 | tf_op jit(solution)/shard_map/ppermute | solution.py:57
  54.3 3.7 %collective-permute-start.14 = (bf16[2,256,512]{2,1,0:T(8,128)(2,1)S(1)}, bf16[2,256,512]{2,1,0:T(8,128)(2,1)S(1)}, u32[]{:S(2)}, u32[]{:S(2)}) collective-permute-start(bf16[2,256,512]{2,1,0:T(8,128)(2,1)S(1)} %shard_map.47), channel_id=1, source_target_pairs={{0,1},{1,0},{2,3},{3,2},{4,5},{5,4},{6,7},{7,6},{8,9},{9,8},{10,11... | collective-permute-start | bytes 1572872 | tf_op jit(solution)/shard_map/ppermute | solution.py:73
  58.0 16.2 %collective-permute-start.15 = (bf16[1,256,512]{2,1,0:T(8,128)(2,1)S(1)}, bf16[1,256,512]{2,1,0:T(8,128)(2,1)S(1)}, u32[]{:S(2)}, u32[]{:S(2)}) collective-permute-start(bf16[1,256,512]{2,1,0:T(8,128)(2,1)S(1)} %shard_map.49), channel_id=1, source_target_pairs={{0,2},{1,3},{2,0},{3,1},{4,6},{5,7},{6,4},{7,5},{8,10},{9,11},{10,... | collective-permute-start | bytes 786440 | tf_op jit(solution)/shard_map/ppermute | solution.py:73

commit v4 on v3

--- a/solution.py
+++ b/solution.py
@@ -144,7 +144,8 @@
 
 
 def one_body(plan, *refs):
-    pieces, (kernel, send, keep, wide) = refs[:-4], refs[-4:]
+    frames = refs[-1].shape[0]
+    pieces, (kernel, keep, *sends, wide) = refs[: frames * plan.ratio], refs[frames * plan.ratio :]
     level, col = where_am_i()
     clear_edges(plan, wide)
     for n, piece in enumerate(pieces):
@@ -152,26 +153,60 @@
     halves = lambda a: jnp.concatenate([half_rows(plan, wide, core, a) for core in (1 - col % 2, col % 2)], axis=0)
     summed = times(plan, halves, kernel)
     size = summed.shape[0] // 2
-    send[...] = summed[:size].astype(BF16).reshape(send.shape)
     keep[...] = summed[size:].reshape(keep.shape)
+    for n, send in enumerate(sends):
+        rows = send.shape[0]
+        send[...] = summed[n * rows : (n + 1) * rows].astype(BF16)
 
 
 def conv_one(plan, pieces, kernel):
     frames = len(pieces) // plan.ratio
     half = (frames, plan.pixels // 2, plan.c_out)
     flops = 18 * frames * plan.pixels * plan.c_in * plan.c_out
-    outputs = [(half, BF16), (half, F32)]
+    outputs = [(half, F32)] + [(half[1:], BF16)] * frames
     scratch = [pltpu.VMEM(plan.wide(frames), BF16)]
-    return plan.call(functools.partial(one_body, plan), [*pieces, kernel], outputs, flops, scratch)
-
-
-def halve_body(bit, kept, came, keep, send):
+    keep, *sends = plan.call(functools.partial(one_body, plan), [*pieces, kernel], outputs, flops, scratch)
+    return keep, [plan.swap(send, 0) for send in sends]
+
+
+def one_sent_body(plan, *refs):
+    frames = refs[-1].shape[0]
+    pieces, (kernel, *sends, wide) = refs[: frames * plan.ratio], refs[frames * plan.ratio :]
+    level, col = where_am_i()
+    clear_edges(plan, wide)
+    for n, piece in enumerate(pieces):
+        place(plan, piece[...], n // plan.ratio, plan.width, plan.lanes(level, n % plan.ratio), wide)
+    summed = times(plan, lambda a: half_rows(plan, wide, 1 - col % 2, a), kernel)
+    for n, send in enumerate(sends):
+        rows = send.shape[0]
+        send[...] = summed[n * rows : (n + 1) * rows].astype(BF16)
+
+
+def one_kept_body(plan, wide, kernel, keep):
+    col = lax.axis_index("img")
+    keep[...] = times(plan, lambda a: half_rows(plan, wide, col % 2, a), kernel).reshape(keep.shape)
+
+
+def conv_one_in_two(plan, pieces, kernel):
+    frames = len(pieces) // plan.ratio
+    half = (frames, plan.pixels // 2, plan.c_out)
+    flops = 9 * frames * plan.pixels * plan.c_in * plan.c_out
+    outputs = [(half[1:], BF16)] * frames + [(plan.wide(frames), BF16)]
+    *sends, wide = plan.call(functools.partial(one_sent_body, plan), [*pieces, kernel], outputs, flops)
+    cames = [plan.swap(send, 0) for send in sends]
+    keep = plan.call(functools.partial(one_kept_body, plan), [wide, kernel], [(half, F32)], flops)[0]
+    return keep, cames
+
+
+def halve_body(bit, kept, *refs):
+    *cames, keep, send = refs
     half = keep.shape[1]
     mine = (lax.axis_index("img") // 2**bit) % 2 * half
     a = pl.ds(pl.multiple_of(mine, 16), half)
     b = pl.ds(pl.multiple_of(half - mine, 16), half)
-    send[...] = (kept[:, b, :] + came[:, b, :].astype(F32)).astype(BF16)
-    keep[...] = kept[:, a, :] + came[:, a, :].astype(F32)
+    for n, came in enumerate(cames):
+        send[n] = (kept[n, b, :] + came[b, :].astype(F32)).astype(BF16)
+        keep[n] = kept[n, a, :] + came[a, :].astype(F32)
 
 
 def silu_body(kept, came, hidden):
@@ -179,15 +214,16 @@
     hidden[...] = (v / (1.0 + jnp.exp(-v))).astype(BF16)
 
 
-def halve(plan, bit, keep, came):
+def halve(plan, bit, keep, cames):
     half = (keep.shape[0], keep.shape[1] // 2, plan.c_out)
-    return plan.call(functools.partial(halve_body, bit), [keep, came], [(half, F32), (half, BF16)])
-
-
-def sum_one(plan, keep, came):
-    keep, send = halve(plan, 1, keep, came)
+    return plan.call(functools.partial(halve_body, bit), [keep, *cames], [(half, F32), (half, BF16)])
+
+
+def sum_one(plan, keep, cames):
+    keep, send = halve(plan, 1, keep, cames)
     for bit in range(2, plan.bits):
-        keep, send = halve(plan, bit, keep, plan.swap(send, bit - 1))
+        came = plan.swap(send, bit - 1)
+        keep, send = halve(plan, bit, keep, [came[n] for n in range(came.shape[0])])
     return keep, send
 
 
@@ -262,12 +298,11 @@
     kernel_one = stage(kernel_one)
     late = [p for d in even for p in plan.spread_frame(block, d)]
     last = plan.bits - 1
-    send, keep = conv_one(plan, early, kernel_one)
-    keep, ahead = sum_one(plan, keep, after(plan.swap(send, 0), late))
-    send, kept = conv_one(plan, after(late, ahead), kernel_one)
-    hidden = join(plan, add_silu(plan, keep, after(plan.swap(ahead, last), send)))
+    keep, ahead = sum_one(plan, *conv_one_in_two(plan, early, kernel_one))
+    kept, cames = conv_one(plan, after(late, ahead), kernel_one)
+    hidden = join(plan, add_silu(plan, keep, after(plan.swap(ahead, last), kept)))
     odds = [p for t in range(plan.pairs) for p in plan.spread(hidden, t)]
-    keep, behind = sum_one(plan, kept, after(plan.swap(send, 0), hidden))
+    keep, behind = sum_one(plan, kept, after(cames, hidden))
     hidden = join(plan, add_silu(plan, keep, plan.swap(behind, last)))
     evens = [p for t in range(plan.pairs) for p in plan.spread(hidden, t)]
     count = len(odd)

time: 75.3 us -> 74.1 us (0.984)
  waiting for transfers between devices: 20.3 us -> 18.5 us
    ppermute x4, waiting for transfers between devices: 8.79 us -> 5.99 us  [spread_frame(): taken.append(lax.ppermute(x, ('chan', 'img'), moves))]
    ppermute x8 -> x10, waiting for transfers between devices: 7.67 us -> 8.7 us  [swap(): return lax.ppermute(x, 'img', [(i, i ^ 1 << bit) for i in range(self.cols)])]
    ppermute x8 -> x10, starting transfers between devices: 23.8 us -> 23.6 us  [swap(): return lax.ppermute(x, 'img', [(i, i ^ 1 << bit) for i in range(self.cols)])]
    pallas_call x13 -> x14, Pallas kernels: 12.6 us -> 12.8 us  [call(): pl.pallas_call(body, in_specs=[VMEM] * len(inputs), out_specs=[VMEM] * le...]
  transfers between devices with their start and end apart: 16 -> 18, of which waited for: 10 -> 10; matrix products, arithmetic and copies ran while one was open for 0% -> 0% of each run, Pallas kernels for 16% -> 16%
where the time goes in v4:
time: 74.1 us; the launch traced here: 73.3 us
  starting transfers between devices  39.2 us (53%)
  waiting for transfers between devices  18.5 us (25%)
  Pallas kernels  13.1 us (18%)
  local copies, waits for them, and re-layouts  2.35 us (3%)
    ppermute x10, starting transfers between devices, swap(): return lax.ppermute(x, 'img', [(i, i ^ 1 << bit) for i in range(self.cols)])  23.6 us
    pallas_call x14, Pallas kernels, call(): pl.pallas_call(body, in_specs=[VMEM] * len(inputs), out_specs=[VMEM] * le...  12.8 us
    ppermute x10, waiting for transfers between devices, swap(): return lax.ppermute(x, 'img', [(i, i ^ 1 << bit) for i in range(self.cols)])  8.7 us
    ppermute x4, starting transfers between devices, spread_frame(): taken.append(lax.ppermute(x, ('chan', 'img'), moves))  8.17 us
    ppermute x4, starting transfers between devices, spread(): taken.append(lax.ppermute(x, ('chan', 'img'), moves))  7.45 us
    ppermute x4, waiting for transfers between devices, spread_frame(): taken.append(lax.ppermute(x, ('chan', 'img'), moves))  5.99 us
    ppermute x4, waiting for transfers between devices, spread(): taken.append(lax.ppermute(x, ('chan', 'img'), moves))  3.82 us
    unnamed x6, local copies, waits for them, and re-layouts  2.35 us
  transfers between devices with their start and end apart: 18, of which 10 were waited for; matrix products, arithmetic and copies ran while one was open for 0% of the time, Pallas kernels for 16%

profile of v4, /device:TPU:0, one launch (start us, length us, event | category | flops | bytes accessed | tf_op | source)
XLA Modules:
  0.0 73.3 jit_solution(5048612122125173861)
XLA Ops:
  0.0 5.0 %collective-permute-start.2 = (bf16[256,512]{1,0:T(8,128)(2,1)}, bf16[256,512]{1,0:T(8,128)(2,1)S(1)}, u32[]{:S(2)}, u32[]{:S(2)}) collective-permute-start(bf16[256,512]{1,0:T(8,128)(2,1)} %bitcast.4), channel_id=1, source_target_pairs={{0,12},{1,0},{2,4},{3,8},{4,13},{5,1},{6,5},{7,9},{8,14},{9,2},{10... | collective-permute-start | bytes 786440 | tf_op jit(solution)/shard_map/ppermute | solution.py:44
  5.0 0.0 collective-permute-start.3
  5.1 1.5 %collective-permute-start = (bf16[256,512]{1,0:T(8,128)(2,1)}, bf16[256,512]{1,0:T(8,128)(2,1)S(1)}, u32[]{:S(2)}, u32[]{:S(2)}) collective-permute-start(bf16[256,512]{1,0:T(8,128)(2,1)} %bitcast.6), channel_id=1, source_target_pairs={{0,8},{1,12},{2,0},{3,4},{4,9},{5,13},{6,1},{7,5},{8,10},{9,14},{1... | collective-permute-start | bytes 786440 | tf_op jit(solution)/shard_map/ppermute | solution.py:44
  6.6 1.6 %collective-permute-start.1 = (bf16[256,512]{1,0:T(8,128)(2,1)}, bf16[256,512]{1,0:T(8,128)(2,1)S(1)}, u32[]{:S(2)}, u32[]{:S(2)}) collective-permute-start(bf16[256,512]{1,0:T(8,128)(2,1)} %bitcast.7), channel_id=1, source_target_pairs={{0,0},{1,4},{2,8},{3,12},{4,1},{5,5},{6,9},{7,13},{8,2},{9,6},{10,... | collective-permute-start | bytes 786440 | tf_op jit(solution)/shard_map/ppermute | solution.py:44
  8.2 0.0 copy-start
  8.2 2.3 %copy-done = bf16[3,3,512,512]{3,2,1,0:T(8,128)(2,1)S(1)} copy-done((bf16[3,3,512,512]{3,2,1,0:T(8,128)(2,1)S(1)}, bf16[3,3,512,512]{3,2,1,0:T(8,128)(2,1)}, u32[]{:S(2)}) %copy-start) | copy-done | bytes 4718616
  10.5 0.3 shard_map.37.refs_2_.kernel
  10.8 0.4 collective-permute-done.2.refs_0_
  11.2 5.6 %collective-permute-done.3.refs_1_ = bf16[256,512]{1,0:T(8,128)(2,1)S(1)} collective-permute-done((bf16[256,512]{1,0:T(8,128)(2,1)}, bf16[256,512]{1,0:T(8,128)(2,1)S(1)}, u32[]{:S(2)}, u32[]{:S(2)}) %collective-permute-start.3) | collective-permute-done | bytes 262176 | tf_op jit(solution)/shard_map/ppermute | solution.py:44
  16.8 1.5 %shard_map.38 = (bf16[128,512]{1,0:T(8,128)(2,1)S(1)}, bf16[128,512]{1,0:T(8,128)(2,1)S(1)}, bf16[2,288,1536]{2,1,0:T(8,128)(2,1)S(1)}) custom-call(bf16[256,512]{1,0:T(8,128)(2,1)S(1)} %collective-permute-done.2.refs_0_, bf16[256,512]{1,0:T(8,128)(2,1)S(1)} %collective-permute-done.3.refs_1_, bf16[3,3,512,512]{3,2,1,0:T(8,128)(2,1)S(1)} %shard_map.37.refs_2_.kernel), custom_call_target="tpu_custom_call" | custom-call | flops 1207959552 | bytes 5242880 | tf_op jit(solution)/shard_map/pallas_call | solution.py:77
  18.4 0.1 collective-permute-start.4
  18.4 0.5 collective-permute-start.5
  18.9 1.4 %shard_map.39.kept = f32[2,128,512]{2,1,0:T(8,128)S(1)} custom-call(bf16[2,288,1536]{2,1,0:T(8,128)(2,1)S(1)} %get-tuple-element.23.wide, bf16[3,3,512,512]{3,2,1,0:T(8,128)(2,1)S(1)} %shard_map.37.refs_2_.kernel), custom_call_target="tpu_custom_call" | custom-call | flops 1207959552 | bytes 6488064 | tf_op jit(solution)/shard_map/pallas_call | solution.py:77
  20.3 0.0 collective-permute-done.4.refs_0_
  20.3 0.0 collective-permute-done.5.refs_1_
  20.3 0.1 shard_map.40
  20.4 0.0 slice-start
  20.4 0.0 slice-start.1
  20.4 8.5 %collective-permute-start.8 = (bf16[2,64,512]{2,1,0:T(8,128)(2,1)S(1)}, bf16[2,64,512]{2,1,0:T(8,128)(2,1)S(1)}, u32[]{:S(2)}, u32[]{:S(2)}) collective-permute-start(bf16[2,64,512]{2,1,0:T(8,128)(2,1)S(1)} %get-tuple-element.26), channel_id=1, source_target_pairs={{0,2},{1,3},{2,0},{3,1},{4,6},{5,7},{6,4},{7,5},{8,10},{9,11},{10,... | collective-permute-start | bytes 393224 | tf_op jit(solution)/shard_map/ppermute | solution.py:73
  29.0 0.0 collective-permute-done.refs_0_
  29.0 0.0 collective-permute-done.1.refs_1_
  29.0 2.7 %shard_map.41 = (f32[2,128,512]{2,1,0:T(8,128)S(1)}, bf16[128,512]{1,0:T(8,128)(2,1)S(1)}, bf16[128,512]{1,0:T(8,128)(2,1)S(1)}) custom-call(bf16[256,512]{1,0:T(8,128)(2,1)S(1)} %collective-permute-done.refs_0_, bf16[256,512]{1,0:T(8,128)(2,1)S(1)} %collective-permute-done.1.refs_1_, bf16[3,3,512,512]{3,2,1,0:T(8,128)(2,1)S(1)} %shard_map.37.refs_2_.kernel), custom_call_target="tpu_custom_call" | custom-call | flops 2415919104 | bytes 5242880 | tf_op jit(solution)/shard_map/pallas_call | solution.py:77
  31.7 1.0 %collective-permute-done.8.came = bf16[2,64,512]{2,1,0:T(8,128)(2,1)S(1)} collective-permute-done((bf16[2,64,512]{2,1,0:T(8,128)(2,1)S(1)}, bf16[2,64,512]{2,1,0:T(8,128)(2,1)S(1)}, u32[]{:S(2)}, u32[]{:S(2)}) %collective-permute-start.8) | collective-permute-done | bytes 131104 | tf_op jit(solution)/shard_map/ppermute | solution.py:73
  32.7 0.1 shard_map.42.own
  32.8 0.1 collective-permute-start.9
  32.9 0.5 collective-permute-start.6
  33.4 0.1 collective-permute-start.7
  33.4 0.8 %collective-permute-done.9.came = bf16[2,64,512]{2,1,0:T(8,128)(2,1)S(1)} collective-permute-done((bf16[2,64,512]{2,1,0:T(8,128)(2,1)S(1)}, bf16[2,64,512]{2,1,0:T(8,128)(2,1)S(1)}, u32[]{:S(2)}, u32[]{:S(2)}) %collective-permute-start.9) | collective-permute-done | bytes 131104 | tf_op jit(solution)/shard_map/ppermute | solution.py:73
  34.2 0.2 collective-permute-done.6.refs_0_
  34.4 0.3 collective-permute-done.7.refs_1_
  34.8 1.8 %collective-permute-start.10 = (bf16[2,64,512]{2,1,0:T(8,128)(2,1)S(1)}, bf16[2,64,512]{2,1,0:T(8,128)(2,1)S(1)}, u32[]{:S(2)}, u32[]{:S(2)}) collective-permute-start(bf16[2,64,512]{2,1,0:T(8,128)(2,1)S(1)} %get-tuple-element.37), channel_id=1, source_target_pairs={{0,2},{1,3},{2,0},{3,1},{4,6},{5,7},{6,4},{7,5},{8,10},{9,11},{10,... | collective-permute-start | bytes 393224 | tf_op jit(solution)/shard_map/ppermute | solution.py:73
  36.6 0.7 collective-permute-start.14
  37.2 2.8 %collective-permute-start.15 = (bf16[2,2,64,512]{3,2,1,0:T(8,128)(2,1)S(1)}, bf16[2,2,64,512]{3,2,1,0:T(8,128)(2,1)S(1)}, u32[]{:S(2)}, u32[]{:S(2)}) collective-permute-start(bf16[2,2,64,512]{3,2,1,0:T(8,128)(2,1)S(1)} %shard_map.43), channel_id=1, source_target_pairs={{2,0},{6,1},{10,2},{14,3},{0,4},{4,5},{8,6},{12,7},{3,8},{7,9},{11... | collective-permute-start | bytes 786440 | tf_op jit(solution)/shard_map/ppermute | solution.py:57
  40.1 0.3 collective-permute-done.10.came
  40.4 0.1 shard_map.45.own
  40.5 1.4 %collective-permute-start.11 = (bf16[2,64,512]{2,1,0:T(8,128)(2,1)S(1)}, bf16[2,64,512]{2,1,0:T(8,128)(2,1)S(1)}, u32[]{:S(2)}, u32[]{:S(2)}) collective-permute-start(bf16[2,64,512]{2,1,0:T(8,128)(2,1)S(1)} %shard_map.45.own), channel_id=1, source_target_pairs={{0,1},{1,0},{2,3},{3,2},{4,5},{5,4},{6,7},{7,6},{8,9},{9,8},{10,11... | collective-permute-start | bytes 393224 | tf_op jit(solution)/shard_map/ppermute | solution.py:73
  41.9 1.0 %collective-permute-done.11.came = bf16[2,64,512]{2,1,0:T(8,128)(2,1)S(1)} collective-permute-done((bf16[2,64,512]{2,1,0:T(8,128)(2,1)S(1)}, bf16[2,64,512]{2,1,0:T(8,128)(2,1)S(1)}, u32[]{:S(2)}, u32[]{:S(2)}) %collective-permute-start.11) | collective-permute-done | bytes 131104 | tf_op jit(solution)/shard_map/ppermute | solution.py:73
  42.9 0.7 collective-permute-start.12
  43.6 3.3 %collective-permute-start.13 = (bf16[2,2,64,512]{3,2,1,0:T(8,128)(2,1)S(1)}, bf16[2,2,64,512]{3,2,1,0:T(8,128)(2,1)S(1)}, u32[]{:S(2)}, u32[]{:S(2)}) collective-permute-start(bf16[2,2,64,512]{3,2,1,0:T(8,128)(2,1)S(1)} %shard_map.46), channel_id=1, source_target_pairs={{2,0},{6,1},{10,2},{14,3},{0,4},{4,5},{8,6},{12,7},{3,8},{7,9},{11... | collective-permute-start | bytes 786440 | tf_op jit(solution)/shard_map/ppermute | solution.py:57
  46.9 0.0 collective-permute-done.14.refs_0_
  46.9 0.0 collective-permute-done.15.refs_1_
  46.9 0.0 slice-done
  46.9 0.0 slice-done.1
  46.9 2.9 %shard_map.48 = bf16[2,256,512]{2,1,0:T(8,128)(2,1)S(1)} custom-call(bf16[2,2,64,512]{3,2,1,0:T(8,128)(2,1)S(1)} %collective-permute-done.14.refs_0_, bf16[2,2,64,512]{3,2,1,0:T(8,128)(2,1)S(1)} %collective-permute-done.15.refs_1_, bf16[3,3,512,512]{3,2,1,0:T(8,128)(2,1)S(1)} %bitcast.3), custom_call_target="tpu_custom_call" | custom-call | flops 2415919104 | bytes 5242880 | tf_op jit(solution)/shard_map/pallas_call | solution.py:77
  49.8 0.0 collective-permute-done.12.refs_0_
  49.8 3.8 %collective-permute-done.13.refs_1_ = bf16[2,2,64,512]{3,2,1,0:T(8,128)(2,1)S(1)} collective-permute-done((bf16[2,2,64,512]{3,2,1,0:T(8,128)(2,1)S(1)}, bf16[2,2,64,512]{3,2,1,0:T(8,128)(2,1)S(1)}, u32[]{:S(2)}, u32[]{:S(2)}) %collective-permute-start.13) | collective-permute-done | bytes 262176 | tf_op jit(solution)/shard_map/ppermute | solution.py:57
  53.6 2.2 %collective-permute-start.16 = (bf16[2,256,512]{2,1,0:T(8,128)(2,1)S(1)}, bf16[2,256,512]{2,1,0:T(8,128)(2,1)S(1)}, u32[]{:S(2)}, u32[]{:S(2)}) collective-permute-start(bf16[2,256,512]{2,1,0:T(8,128)(2,1)S(1)} %shard_map.48), channel_id=1, source_target_pairs={{0,1},{1,0},{2,3},{3,2},{4,5},{5,4},{6,7},{7,6},{8,9},{9,8},{10,11... | collective-permute-start | bytes 1572872 | tf_op jit(solution)/shard_map/ppermute | solution.py:73
  55.8 1.5 %shard_map.49.kept = f32[1,256,512]{2,1,0:T(8,128)S(1)} custom-call(bf16[2,2,64,512]{3,2,1,0:T(8,128)(2,1)S(1)} %collective-permute-done.12.refs_0_, bf16[2,2,64,512]{3,2,1,0:T(8,128)(2,1)S(1)} %collective-permute-done.13.refs_1_, bf16[3,3,512,512]{3,2,1,0:T(8,128)(2,1)S(1)} %bitcast.3), custom_call_target="tpu_custom_call" | custom-call | flops 1207959552 | bytes 5242880 | tf_op jit(solution)/shard_map/pallas_call | solution.py:77
  57.3 0.0 collective-permute-done.16.came.first
  57.3 0.1 shard_map.50
  57.4 8.5 %collective-permute-start.17 = (bf16[1,256,512]{2,1,0:T(8,128)(2,1)S(1)}, bf16[1,256,512]{2,1,0:T(8,128)(2,1)S(1)}, u32[]{:S(2)}, u32[]{:S(2)}) collective-permute-start(bf16[1,256,512]{2,1,0:T(8,128)(2,1)S(1)} %shard_map.50), channel_id=1, source_target_pairs={{0,2},{1,3},{2,0},{3,1},{4,6},{5,7},{6,4},{7,5},{8,10},{9,11},{10,... | collective-permute-start | bytes 786440 | tf_op jit(solution)/shard_map/ppermute | solution.py:73
  65.9 1.5 %shard_map.47.kept = f32[1,256,512]{2,1,0:T(8,128)S(1)} custom-call(bf16[2,2,64,512]{3,2,1,0:T(8,128)(2,1)S(1)} %collective-permute-done.12.refs_0_, bf16[2,2,64,512]{3,2,1,0:T(8,128)(2,1)S(1)} %collective-permute-done.13.refs_1_, bf16[3,3,512,512]{3,2,1,0:T(8,128)(2,1)S(1)} %bitcast.3), custom_call_target="tpu_custom_call" | custom-call | flops 1207959552 | bytes 5242880 | tf_op jit(solution)/shard_map/pallas_call | solution.py:77
  67.4 5.1 %collective-permute-done.17.came = bf16[1,256,512]{2,1,0:T(8,128)(2,1)S(1)} collective-permute-done((bf16[1,256,512]{2,1,0:T(8,128)(2,1)S(1)}, bf16[1,256,512]{2,1,0:T(8,128)(2,1)S(1)}, u32[]{:S(2)}, u32[]{:S(2)}) %collective-permute-start.17) | collective-permute-done | bytes 262176 | tf_op jit(solution)/shard_map/ppermute | solution.py:73
  72.5 0.8 %shard_map.51 = bf16[1,256,512]{2,1,0:T(8,128)(2,1)} custom-call(f32[1,256,512]{2,1,0:T(8,128)S(1)} %shard_map.47.kept, bf16[2,256,512]{2,1,0:T(8,128)(2,1)S(1)} %collective-permute-done.16.came.first, bf16[1,256,512]{2,1,0:T(8,128)(2,1)S(1)} %collective-permute-done.17.came), custom_call_target="tpu_custom_call" | custom-call | bytes 1310720 | tf_op jit(solution)/shard_map/pallas_call | solution.py:77
  (4 shorter events, 0.1 us)
Async XLA Ops:
  0.0 11.2 %collective-permute-start.2 = (bf16[256,512]{1,0:T(8,128)(2,1)}, bf16[256,512]{1,0:T(8,128)(2,1)S(1)}, u32[]{:S(2)}, u32[]{:S(2)}) collective-permute-start(bf16[256,512]{1,0:T(8,128)(2,1)} %bitcast.4), channel_id=1, source_target_pairs={{0,12},{1,0},{2,4},{3,8},{4,13},{5,1},{6,5},{7,9},{8,14},{9,2},{10... | collective-permute-start | bytes 786440 | tf_op jit(solution)/shard_map/ppermute | solution.py:44
  5.0 11.8 %collective-permute-start.3 = (bf16[256,512]{1,0:T(8,128)(2,1)}, bf16[256,512]{1,0:T(8,128)(2,1)S(1)}, u32[]{:S(2)}, u32[]{:S(2)}) collective-permute-start(bf16[256,512]{1,0:T(8,128)(2,1)} %bitcast.5), channel_id=1, source_target_pairs={{0,4},{1,8},{2,12},{3,0},{4,5},{5,9},{6,13},{7,1},{8,6},{9,10},{10... | collective-permute-start | bytes 786440 | tf_op jit(solution)/shard_map/ppermute | solution.py:44
  5.1 23.9 %collective-permute-start = (bf16[256,512]{1,0:T(8,128)(2,1)}, bf16[256,512]{1,0:T(8,128)(2,1)S(1)}, u32[]{:S(2)}, u32[]{:S(2)}) collective-permute-start(bf16[256,512]{1,0:T(8,128)(2,1)} %bitcast.6), channel_id=1, source_target_pairs={{0,8},{1,12},{2,0},{3,4},{4,9},{5,13},{6,1},{7,5},{8,10},{9,14},{1... | collective-permute-start | bytes 786440 | tf_op jit(solution)/shard_map/ppermute | solution.py:44
  6.6 22.4 %collective-permute-start.1 = (bf16[256,512]{1,0:T(8,128)(2,1)}, bf16[256,512]{1,0:T(8,128)(2,1)S(1)}, u32[]{:S(2)}, u32[]{:S(2)}) collective-permute-start(bf16[256,512]{1,0:T(8,128)(2,1)} %bitcast.7), channel_id=1, source_target_pairs={{0,0},{1,4},{2,8},{3,12},{4,1},{5,5},{6,9},{7,13},{8,2},{9,6},{10,... | collective-permute-start | bytes 786440 | tf_op jit(solution)/shard_map/ppermute | solution.py:44
  8.2 2.3 %copy-start = (bf16[3,3,512,512]{3,2,1,0:T(8,128)(2,1)S(1)}, bf16[3,3,512,512]{3,2,1,0:T(8,128)(2,1)}, u32[]{:S(2)}) copy-start(bf16[3,3,512,512]{3,2,1,0:T(8,128)(2,1)} %source.1) | copy-start | bytes 14155780
  18.4 2.0 %collective-permute-start.4 = (bf16[128,512]{1,0:T(8,128)(2,1)S(1)}, bf16[128,512]{1,0:T(8,128)(2,1)S(1)}, u32[]{:S(2)}, u32[]{:S(2)}) collective-permute-start(bf16[128,512]{1,0:T(8,128)(2,1)S(1)} %get-tuple-element.24), channel_id=1, source_target_pairs={{0,1},{1,0},{2,3},{3,2},{4,5},{5,4},{6,7},{7,6},{8,9},{9,8},{10,11... | collective-permute-start | bytes 393224 | tf_op jit(solution)/shard_map/ppermute | solution.py:73
  18.4 1.9 %collective-permute-start.5 = (bf16[128,512]{1,0:T(8,128)(2,1)S(1)}, bf16[128,512]{1,0:T(8,128)(2,1)S(1)}, u32[]{:S(2)}, u32[]{:S(2)}) collective-permute-start(bf16[128,512]{1,0:T(8,128)(2,1)S(1)} %get-tuple-element.25), channel_id=1, source_target_pairs={{0,1},{1,0},{2,3},{3,2},{4,5},{5,4},{6,7},{7,6},{8,9},{9,8},{10,11... | collective-permute-start | bytes 393224 | tf_op jit(solution)/shard_map/ppermute | solution.py:73
  20.4 26.5 %slice-start = ((s8[4718592]{0:T(1024)(128)(4,1)}), s8[4194304]{0:T(1024)(128)(4,1)S(1)}, s32[]{:S(2)}) async-start(s8[4718592]{0:T(1024)(128)(4,1)} %bitcast.2), calls=%async_computation | async-start | bytes 8388608
  20.4 26.5 %slice-start.1 = ((s8[4718592]{0:T(1024)(128)(4,1)}), s8[524288]{0:T(1024)(128)(4,1)S(1)}, s32[]{:S(2)}) async-start(s8[4718592]{0:T(1024)(128)(4,1)} %bitcast.2), calls=%async_computation.1 | async-start | bytes 1048576
  20.4 12.3 %collective-permute-start.8 = (bf16[2,64,512]{2,1,0:T(8,128)(2,1)S(1)}, bf16[2,64,512]{2,1,0:T(8,128)(2,1)S(1)}, u32[]{:S(2)}, u32[]{:S(2)}) collective-permute-start(bf16[2,64,512]{2,1,0:T(8,128)(2,1)S(1)} %get-tuple-element.26), channel_id=1, source_target_pairs={{0,2},{1,3},{2,0},{3,1},{4,6},{5,7},{6,4},{7,5},{8,10},{9,11},{10,... | collective-permute-start | bytes 393224 | tf_op jit(solution)/shard_map/ppermute | solution.py:73
  32.8 1.4 %collective-permute-start.9 = (bf16[2,64,512]{2,1,0:T(8,128)(2,1)S(1)}, bf16[2,64,512]{2,1,0:T(8,128)(2,1)S(1)}, u32[]{:S(2)}, u32[]{:S(2)}) collective-permute-start(bf16[2,64,512]{2,1,0:T(8,128)(2,1)S(1)} %shard_map.42.own), channel_id=1, source_target_pairs={{0,1},{1,0},{2,3},{3,2},{4,5},{5,4},{6,7},{7,6},{8,9},{9,8},{10,11... | collective-permute-start | bytes 393224 | tf_op jit(solution)/shard_map/ppermute | solution.py:73
  32.9 1.5 %collective-permute-start.6 = (bf16[128,512]{1,0:T(8,128)(2,1)S(1)}, bf16[128,512]{1,0:T(8,128)(2,1)S(1)}, u32[]{:S(2)}, u32[]{:S(2)}) collective-permute-start(bf16[128,512]{1,0:T(8,128)(2,1)S(1)} %get-tuple-element.30), channel_id=1, source_target_pairs={{0,1},{1,0},{2,3},{3,2},{4,5},{5,4},{6,7},{7,6},{8,9},{9,8},{10,11... | collective-permute-start | bytes 393224 | tf_op jit(solution)/shard_map/ppermute | solution.py:73
  33.4 1.3 %collective-permute-start.7 = (bf16[128,512]{1,0:T(8,128)(2,1)S(1)}, bf16[128,512]{1,0:T(8,128)(2,1)S(1)}, u32[]{:S(2)}, u32[]{:S(2)}) collective-permute-start(bf16[128,512]{1,0:T(8,128)(2,1)S(1)} %get-tuple-element.31), channel_id=1, source_target_pairs={{0,1},{1,0},{2,3},{3,2},{4,5},{5,4},{6,7},{7,6},{8,9},{9,8},{10,11... | collective-permute-start | bytes 393224 | tf_op jit(solution)/shard_map/ppermute | solution.py:73
  34.8 5.7 %collective-permute-start.10 = (bf16[2,64,512]{2,1,0:T(8,128)(2,1)S(1)}, bf16[2,64,512]{2,1,0:T(8,128)(2,1)S(1)}, u32[]{:S(2)}, u32[]{:S(2)}) collective-permute-start(bf16[2,64,512]{2,1,0:T(8,128)(2,1)S(1)} %get-tuple-element.37), channel_id=1, source_target_pairs={{0,2},{1,3},{2,0},{3,1},{4,6},{5,7},{6,4},{7,5},{8,10},{9,11},{10,... | collective-permute-start | bytes 393224 | tf_op jit(solution)/shard_map/ppermute | solution.py:73
  36.6 10.3 %collective-permute-start.14 = (bf16[2,2,64,512]{3,2,1,0:T(8,128)(2,1)S(1)}, bf16[2,2,64,512]{3,2,1,0:T(8,128)(2,1)S(1)}, u32[]{:S(2)}, u32[]{:S(2)}) collective-permute-start(bf16[2,2,64,512]{3,2,1,0:T(8,128)(2,1)S(1)} %shard_map.43), channel_id=1, source_target_pairs={{0,0},{4,1},{8,2},{12,3},{2,4},{6,5},{10,6},{14,7},{1,8},{5,9},{9,... | collective-permute-start | bytes 786440 | tf_op jit(solution)/shard_map/ppermute | solution.py:57
  37.2 9.6 %collective-permute-start.15 = (bf16[2,2,64,512]{3,2,1,0:T(8,128)(2,1)S(1)}, bf16[2,2,64,512]{3,2,1,0:T(8,128)(2,1)S(1)}, u32[]{:S(2)}, u32[]{:S(2)}) collective-permute-start(bf16[2,2,64,512]{3,2,1,0:T(8,128)(2,1)S(1)} %shard_map.43), channel_id=1, source_target_pairs={{2,0},{6,1},{10,2},{14,3},{0,4},{4,5},{8,6},{12,7},{3,8},{7,9},{11... | collective-permute-start | bytes 786440 | tf_op jit(solution)/shard_map/ppermute | solution.py:57
  40.5 2.4 %collective-permute-start.11 = (bf16[2,64,512]{2,1,0:T(8,128)(2,1)S(1)}, bf16[2,64,512]{2,1,0:T(8,128)(2,1)S(1)}, u32[]{:S(2)}, u32[]{:S(2)}) collective-permute-start(bf16[2,64,512]{2,1,0:T(8,128)(2,1)S(1)} %shard_map.45.own), channel_id=1, source_target_pairs={{0,1},{1,0},{2,3},{3,2},{4,5},{5,4},{6,7},{7,6},{8,9},{9,8},{10,11... | collective-permute-start | bytes 393224 | tf_op jit(solution)/shard_map/ppermute | solution.py:73
  42.9 6.9 %collective-permute-start.12 = (bf16[2,2,64,512]{3,2,1,0:T(8,128)(2,1)S(1)}, bf16[2,2,64,512]{3,2,1,0:T(8,128)(2,1)S(1)}, u32[]{:S(2)}, u32[]{:S(2)}) collective-permute-start(bf16[2,2,64,512]{3,2,1,0:T(8,128)(2,1)S(1)} %shard_map.46), channel_id=1, source_target_pairs={{0,0},{4,1},{8,2},{12,3},{2,4},{6,5},{10,6},{14,7},{1,8},{5,9},{9,... | collective-permute-start | bytes 786440 | tf_op jit(solution)/shard_map/ppermute | solution.py:57
  43.6 10.0 %collective-permute-start.13 = (bf16[2,2,64,512]{3,2,1,0:T(8,128)(2,1)S(1)}, bf16[2,2,64,512]{3,2,1,0:T(8,128)(2,1)S(1)}, u32[]{:S(2)}, u32[]{:S(2)}) collective-permute-start(bf16[2,2,64,512]{3,2,1,0:T(8,128)(2,1)S(1)} %shard_map.46), channel_id=1, source_target_pairs={{2,0},{6,1},{10,2},{14,3},{0,4},{4,5},{8,6},{12,7},{3,8},{7,9},{11... | collective-permute-start | bytes 786440 | tf_op jit(solution)/shard_map/ppermute | solution.py:57
  53.6 3.7 %collective-permute-start.16 = (bf16[2,256,512]{2,1,0:T(8,128)(2,1)S(1)}, bf16[2,256,512]{2,1,0:T(8,128)(2,1)S(1)}, u32[]{:S(2)}, u32[]{:S(2)}) collective-permute-start(bf16[2,256,512]{2,1,0:T(8,128)(2,1)S(1)} %shard_map.48), channel_id=1, source_target_pairs={{0,1},{1,0},{2,3},{3,2},{4,5},{5,4},{6,7},{7,6},{8,9},{9,8},{10,11... | collective-permute-start | bytes 1572872 | tf_op jit(solution)/shard_map/ppermute | solution.py:73
  57.4 15.1 %collective-permute-start.17 = (bf16[1,256,512]{2,1,0:T(8,128)(2,1)S(1)}, bf16[1,256,512]{2,1,0:T(8,128)(2,1)S(1)}, u32[]{:S(2)}, u32[]{:S(2)}) collective-permute-start(bf16[1,256,512]{2,1,0:T(8,128)(2,1)S(1)} %shard_map.50), channel_id=1, source_target_pairs={{0,2},{1,3},{2,0},{3,1},{4,6},{5,7},{6,4},{7,5},{8,10},{9,11},{10,... | collective-permute-start | bytes 786440 | tf_op jit(solution)/shard_map/ppermute | solution.py:73

commit v5 on v4

--- a/solution.py
+++ b/solution.py
@@ -29,6 +29,7 @@
         self.c_in, self.c_out = kernel.shape[2], kernel.shape[3]
         self.share = self.pixels // self.cols
         self.bits = self.cols.bit_length() - 1
+        self.order = [0, *range(self.bits - 1, 0, -1)]
 
     def wide(self, frames):
         return (frames, self.pixels + 2 * self.width, 3 * self.c_in)
@@ -62,13 +63,6 @@
             return 0
         return pl.multiple_of((level + e) % self.ratio * self.piece, 128)
 
-    def first_row(self, col):
-        at, size = 0, self.pixels
-        for bit in range(self.bits):
-            size //= 2
-            at = at + (col // 2**bit) % 2 * size
-        return at
-
     def swap(self, x, bit):
         return lax.ppermute(x, "img", [(i, i ^ (1 << bit)) for i in range(self.cols)])
 
@@ -138,9 +132,12 @@
 
 
 def half_rows(plan, wide, core, a):
-    half = plan.pixels // 2
-    rows = pl.ds(pl.multiple_of(core * half + a * plan.width, 16), half)
-    return wide[:, rows, :].reshape(-1, 3 * plan.c_in)
+    blocks = []
+    for f in range(wide.shape[0]):
+        for pair in range(plan.pairs):
+            start = (2 * pair + core) * plan.share + a * plan.width
+            blocks.append(wide[f, pl.ds(pl.multiple_of(start, 16), plan.share), :])
+    return jnp.concatenate(blocks, axis=0)
 
 
 def one_body(plan, *refs):
@@ -220,10 +217,10 @@
 
 
 def sum_one(plan, keep, cames):
-    keep, send = halve(plan, 1, keep, cames)
-    for bit in range(2, plan.bits):
-        came = plan.swap(send, bit - 1)
-        keep, send = halve(plan, bit, keep, [came[n] for n in range(came.shape[0])])
+    keep, send = halve(plan, plan.order[1], keep, cames)
+    for n in range(2, plan.bits):
+        came = plan.swap(send, plan.order[n - 1])
+        keep, send = halve(plan, plan.order[n], keep, [came[f] for f in range(came.shape[0])])
     return keep, send
 
 
@@ -239,7 +236,7 @@
         turn, e = n // plan.ratio, n % plan.ratio
         pair = (level // plan.ratio + turn) % plan.pairs
         for core in range(2):
-            row_at = pl.multiple_of(plan.width + plan.first_row(2 * pair + core), 16)
+            row_at = pl.multiple_of(plan.width + (2 * pair + core) * plan.share, 16)
             for f, at in enumerate(chosen):
                 place(plan, piece[core, at], f, row_at, plan.lanes(level, e), wide)
     rows = lambda a: wide[:, a * plan.width : a * plan.width + plan.pixels, :].reshape(-1, 3 * plan.c_in)
@@ -255,6 +252,33 @@
         18 * frames * plan.pixels * plan.c_in * plan.c_out,
         [pltpu.VMEM(plan.wide(frames), BF16)],
     )[0]
+
+
+def conv_for_other(plan, pieces, first, kernel, parts):
+    return plan.call(
+        functools.partial(for_other_body, plan, first),
+        [*pieces, kernel],
+        [((plan.pixels // parts, plan.c_out), BF16)] * parts,
+        18 * plan.pixels * plan.c_in * plan.c_out,
+        [pltpu.VMEM(plan.wide(1), BF16)],
+    )
+
+
+def for_other_body(plan, first, *refs):
+    count = plan.pairs * plan.ratio
+    pieces, kernel, outs, wide = refs[:count], refs[count], refs[count + 1 : -1], refs[-1]
+    level, col = where_am_i()
+    clear_edges(plan, wide)
+    for n, piece in enumerate(pieces):
+        turn, e = n // plan.ratio, n % plan.ratio
+        pair = (level // plan.ratio + turn) % plan.pairs
+        for core in range(2):
+            row_at = pl.multiple_of(plan.width + (2 * pair + core) * plan.share, 16)
+            place(plan, piece[core, (col + first) % 2], 0, row_at, plan.lanes(level, e), wide)
+    total = times(plan, lambda a: wide[0, a * plan.width : a * plan.width + plan.pixels, :], kernel)
+    size = plan.pixels // len(outs)
+    for n, out in enumerate(outs):
+        out[...] = total[n * size : (n + 1) * size].astype(BF16)
 
 
 def aligned(bit, came, n):
@@ -289,6 +313,77 @@
     return total
 
 
+def part_of(plan, part):
+    first = lax.axis_index("chan") // plan.ratio % plan.pairs == 0
+    size = plan.pixels // 2 - plan.width
+    if part == 0:
+        return jnp.where(first, 0, plan.pixels - size), size
+    if part == 1:
+        return jnp.where(first, size, 0), plan.pixels - size
+    return 0, plan.pixels
+
+
+def part_body(plan, part, frame, turns, *refs):
+    count = turns * plan.ratio
+    pieces, kernel, cames, (out, wide, added) = refs[:count], refs[count], refs[count + 1 : -3], refs[-3:]
+    level, col = where_am_i()
+    clear_edges(plan, wide)
+    for n, piece in enumerate(pieces):
+        turn, e = n // plan.ratio, n % plan.ratio
+        pair = (level // plan.ratio + turn) % plan.pairs
+        for core in range(2):
+            row_at = pl.multiple_of(plan.width + (2 * pair + core) * plan.share, 16)
+            place(plan, piece[core, frame], 0, row_at, plan.lanes(level, e), wide)
+    for n, came in enumerate(cames):
+        added[n * came.shape[0] : (n + 1) * came.shape[0], :] = came[...]
+    start, size = part_of(plan, part)
+    at = lambda a: pl.ds(pl.multiple_of(start + a * plan.width, 16), size)
+    total = times(plan, lambda a: wide[0, at(a), :], kernel)
+    out[...] = (total + added[at(0), :].astype(F32)).astype(out.dtype)
+
+
+def conv_part(plan, part, frame, pieces, kernel, cames, dtype):
+    size = [plan.pixels // 2 - plan.width, plan.pixels // 2 + plan.width, plan.pixels][part]
+    return plan.call(
+        functools.partial(part_body, plan, part, frame, len(pieces) // plan.ratio),
+        [*pieces, kernel, *cames],
+        [((size, plan.c_out), dtype)],
+        18 * size * plan.c_in * plan.c_out,
+        [pltpu.VMEM(plan.wide(1), BF16), pltpu.VMEM((plan.pixels, plan.c_out), BF16)],
+    )[0]
+
+
+def put_body(plan, kept, *refs):
+    *cames, out = refs
+    for part, came in enumerate(cames):
+        start, size = part_of(plan, part)
+        rows = pl.ds(pl.multiple_of(start, 16), size)
+        out[rows, :] = (kept[rows, :] + came[...].astype(F32)).astype(BF16)
+
+
+def sum_in_parts(plan, odds, evens, hidden, kernel):
+    odds = after(odds, hidden)
+    frames = len(odds[0][0])
+    if plan.pairs != 2:
+        sums = conv_two(plan, odds, range(frames), kernel, BF16)
+        came = plan.swap(after(sums, evens), 0)
+        here = conv_two(plan, evens, range(frames // 2), kernel, F32)
+        send = merge(plan, 0, here, came, range(1, frames, 2), BF16)
+        here = conv_two(plan, evens, range(frames // 2, frames), kernel, F32)
+        return sum_rest(plan, here, came, send)
+    cames = [plan.swap(part, 0) for part in conv_for_other(plan, odds, 1, kernel, 2)]
+    own = conv_for_other(plan, odds, 0, kernel, 1)[0]
+    near, both = after(evens[: plan.ratio], own), evens
+    sums = conv_part(plan, 0, 0, near, kernel, cames, BF16)
+    early = plan.swap(sums, 1)
+    sums = conv_part(plan, 1, 0, after(both, sums), kernel, cames, BF16)
+    late = plan.swap(sums, 1)
+    early = after(early, sums)
+    kept = conv_part(plan, 2, 1, after(both, early), kernel, [plan.swap(own, 0)], F32)
+    body = functools.partial(put_body, plan)
+    return plan.call(body, [kept, early, late], [(kept.shape, BF16)])[0]
+
+
 def shards(mesh, features, kernel_one, kernel_two):
     plan = Plan(mesh, features, kernel_one)
     block = features.reshape(plan.pixels, plan.piece)
@@ -297,7 +392,7 @@
     early = [p for d in odd for p in plan.spread_frame(block, d)]
     kernel_one = stage(kernel_one)
     late = [p for d in even for p in plan.spread_frame(block, d)]
-    last = plan.bits - 1
+    last = plan.order[-1]
     keep, ahead = sum_one(plan, *conv_one_in_two(plan, early, kernel_one))
     kept, cames = conv_one(plan, after(late, ahead), kernel_one)
     hidden = join(plan, add_silu(plan, keep, after(plan.swap(ahead, last), kept)))
@@ -305,13 +400,7 @@
     keep, behind = sum_one(plan, kept, after(cames, hidden))
     hidden = join(plan, add_silu(plan, keep, plan.swap(behind, last)))
     evens = [p for t in range(plan.pairs) for p in plan.spread(hidden, t)]
-    count = len(odd)
-    sums = conv_two(plan, after(odds, hidden), range(count), kernel_two, BF16)
-    came = plan.swap(after(sums, evens), 0)
-    here = conv_two(plan, evens, range(count // 2), kernel_two, F32)
-    send = merge(plan, 0, here, came, range(1, count, 2), BF16)
-    here = conv_two(plan, evens, range(count // 2, count), kernel_two, F32)
-    return sum_rest(plan, here, came, send).reshape(features.shape)
+    return sum_in_parts(plan, odds, evens, hidden, kernel_two).reshape(features.shape)
 
 
 def solution(mesh):

time: 74.1 us -> 71.9 us (0.970)
  waiting for transfers between devices: 18.5 us -> 13.3 us
  starting transfers between devices: 39.2 us -> 42.7 us
    ppermute x4, waiting for transfers between devices: 3.82 us -> 0.01 us  [spread(): taken.append(lax.ppermute(x, ('chan', 'img'), moves))]
    ppermute x10 -> x13, starting transfers between devices: 23.6 us -> 27.1 us  [swap(): return lax.ppermute(x, 'img', [(i, i ^ 1 << bit) for i in range(self.cols)])]
    ppermute x10 -> x13, waiting for transfers between devices: 8.7 us -> 7.29 us  [swap(): return lax.ppermute(x, 'img', [(i, i ^ 1 << bit) for i in range(self.cols)])]
    pallas_call x14 -> x15, Pallas kernels: 12.8 us -> 12.8 us  [call(): pl.pallas_call(body, in_specs=[VMEM] * len(inputs), out_specs=[VMEM] * le...]
  transfers between devices with their start and end apart: 18 -> 21, of which waited for: 10 -> 10; matrix products, arithmetic and copies ran while one was open for 0% -> 0% of each run, Pallas kernels for 16% -> 17%
where the time goes in v5:
time: 71.9 us; the launch traced here: 71.7 us
  starting transfers between devices  42.7 us (59%)
  waiting for transfers between devices  13.3 us (18%)
  Pallas kernels  13.2 us (18%)
  local copies, waits for them, and re-layouts  2.35 us (3%)
    ppermute x13, starting transfers between devices, swap(): return lax.ppermute(x, 'img', [(i, i ^ 1 << bit) for i in range(self.cols)])  27.1 us
    pallas_call x15, Pallas kernels, call(): pl.pallas_call(body, in_specs=[VMEM] * len(inputs), out_specs=[VMEM] * le...  12.8 us
    ppermute x4, starting transfers between devices, spread_frame(): taken.append(lax.ppermute(x, ('chan', 'img'), moves))  8.17 us
    ppermute x4, starting transfers between devices, spread(): taken.append(lax.ppermute(x, ('chan', 'img'), moves))  7.45 us
    ppermute x13, waiting for transfers between devices, swap(): return lax.ppermute(x, 'img', [(i, i ^ 1 << bit) for i in range(self.cols)])  7.29 us
    ppermute x4, waiting for transfers between devices, spread_frame(): taken.append(lax.ppermute(x, ('chan', 'img'), moves))  5.99 us
    unnamed x6, local copies, waits for them, and re-layouts  2.35 us
  transfers between devices with their start and end apart: 21, of which 10 were waited for; matrix products, arithmetic and copies ran while one was open for 0% of the time, Pallas kernels for 17%

profile of v5, /device:TPU:0, one launch (start us, length us, event | category | flops | bytes accessed | tf_op | source)
XLA Modules:
  0.0 71.7 jit_solution(3790158037672635135)
XLA Ops:
  0.0 5.0 %collective-permute-start.2 = (bf16[256,512]{1,0:T(8,128)(2,1)}, bf16[256,512]{1,0:T(8,128)(2,1)S(1)}, u32[]{:S(2)}, u32[]{:S(2)}) collective-permute-start(bf16[256,512]{1,0:T(8,128)(2,1)} %bitcast.4), channel_id=1, source_target_pairs={{0,12},{1,0},{2,4},{3,8},{4,13},{5,1},{6,5},{7,9},{8,14},{9,2},{10... | collective-permute-start | bytes 786440 | tf_op jit(solution)/shard_map/ppermute | solution.py:45
  5.0 0.0 collective-permute-start.3
  5.1 1.5 %collective-permute-start = (bf16[256,512]{1,0:T(8,128)(2,1)}, bf16[256,512]{1,0:T(8,128)(2,1)S(1)}, u32[]{:S(2)}, u32[]{:S(2)}) collective-permute-start(bf16[256,512]{1,0:T(8,128)(2,1)} %bitcast.6), channel_id=1, source_target_pairs={{0,8},{1,12},{2,0},{3,4},{4,9},{5,13},{6,1},{7,5},{8,10},{9,14},{1... | collective-permute-start | bytes 786440 | tf_op jit(solution)/shard_map/ppermute | solution.py:45
  6.6 1.6 %collective-permute-start.1 = (bf16[256,512]{1,0:T(8,128)(2,1)}, bf16[256,512]{1,0:T(8,128)(2,1)S(1)}, u32[]{:S(2)}, u32[]{:S(2)}) collective-permute-start(bf16[256,512]{1,0:T(8,128)(2,1)} %bitcast.7), channel_id=1, source_target_pairs={{0,0},{1,4},{2,8},{3,12},{4,1},{5,5},{6,9},{7,13},{8,2},{9,6},{10,... | collective-permute-start | bytes 786440 | tf_op jit(solution)/shard_map/ppermute | solution.py:45
  8.2 0.0 copy-start
  8.2 2.3 %copy-done = bf16[3,3,512,512]{3,2,1,0:T(8,128)(2,1)S(1)} copy-done((bf16[3,3,512,512]{3,2,1,0:T(8,128)(2,1)S(1)}, bf16[3,3,512,512]{3,2,1,0:T(8,128)(2,1)}, u32[]{:S(2)}) %copy-start) | copy-done | bytes 4718616
  10.5 0.3 shard_map.37.refs_2_.kernel
  10.8 0.4 collective-permute-done.2.refs_0_
  11.2 5.6 %collective-permute-done.3.refs_1_ = bf16[256,512]{1,0:T(8,128)(2,1)S(1)} collective-permute-done((bf16[256,512]{1,0:T(8,128)(2,1)}, bf16[256,512]{1,0:T(8,128)(2,1)S(1)}, u32[]{:S(2)}, u32[]{:S(2)}) %collective-permute-start.3) | collective-permute-done | bytes 262176 | tf_op jit(solution)/shard_map/ppermute | solution.py:45
  16.8 1.6 %shard_map.38 = (bf16[128,512]{1,0:T(8,128)(2,1)S(1)}, bf16[128,512]{1,0:T(8,128)(2,1)S(1)}, bf16[2,288,1536]{2,1,0:T(8,128)(2,1)S(1)}) custom-call(bf16[256,512]{1,0:T(8,128)(2,1)S(1)} %collective-permute-done.2.refs_0_, bf16[256,512]{1,0:T(8,128)(2,1)S(1)} %collective-permute-done.3.refs_1_, bf16[3,3,512,512]{3,2,1,0:T(8,128)(2,1)S(1)} %shard_map.37.refs_2_.kernel), custom_call_target="tpu_custom_call" | custom-call | flops 1207959552 | bytes 5242880 | tf_op jit(solution)/shard_map/pallas_call | solution.py:71
  18.4 0.1 collective-permute-start.4
  18.5 0.5 collective-permute-start.5
  19.0 1.4 %shard_map.39.kept = f32[2,128,512]{2,1,0:T(8,128)S(1)} custom-call(bf16[2,288,1536]{2,1,0:T(8,128)(2,1)S(1)} %get-tuple-element.30.wide, bf16[3,3,512,512]{3,2,1,0:T(8,128)(2,1)S(1)} %shard_map.37.refs_2_.kernel), custom_call_target="tpu_custom_call" | custom-call | flops 1207959552 | bytes 6488064 | tf_op jit(solution)/shard_map/pallas_call | solution.py:71
  20.3 0.0 collective-permute-done.4.refs_0_
  20.3 0.0 collective-permute-done.5.refs_1_
  20.4 0.1 shard_map.40
  20.4 0.0 slice-start
  20.4 0.0 slice-start.1
  20.5 8.5 %collective-permute-start.8 = (bf16[2,64,512]{2,1,0:T(8,128)(2,1)S(1)}, bf16[2,64,512]{2,1,0:T(8,128)(2,1)S(1)}, u32[]{:S(2)}, u32[]{:S(2)}) collective-permute-start(bf16[2,64,512]{2,1,0:T(8,128)(2,1)S(1)} %get-tuple-element.33), channel_id=1, source_target_pairs={{0,2},{1,3},{2,0},{3,1},{4,6},{5,7},{6,4},{7,5},{8,10},{9,11},{10,... | collective-permute-start | bytes 393224 | tf_op jit(solution)/shard_map/ppermute | solution.py:67
  29.0 0.0 collective-permute-done.refs_0_
  29.0 0.0 collective-permute-done.1.refs_1_
  29.0 2.7 %shard_map.41 = (f32[2,128,512]{2,1,0:T(8,128)S(1)}, bf16[128,512]{1,0:T(8,128)(2,1)S(1)}, bf16[128,512]{1,0:T(8,128)(2,1)S(1)}) custom-call(bf16[256,512]{1,0:T(8,128)(2,1)S(1)} %collective-permute-done.refs_0_, bf16[256,512]{1,0:T(8,128)(2,1)S(1)} %collective-permute-done.1.refs_1_, bf16[3,3,512,512]{3,2,1,0:T(8,128)(2,1)S(1)} %shard_map.37.refs_2_.kernel), custom_call_target="tpu_custom_call" | custom-call | flops 2415919104 | bytes 5242880 | tf_op jit(solution)/shard_map/pallas_call | solution.py:71
  31.7 1.0 %collective-permute-done.8.came = bf16[2,64,512]{2,1,0:T(8,128)(2,1)S(1)} collective-permute-done((bf16[2,64,512]{2,1,0:T(8,128)(2,1)S(1)}, bf16[2,64,512]{2,1,0:T(8,128)(2,1)S(1)}, u32[]{:S(2)}, u32[]{:S(2)}) %collective-permute-start.8) | collective-permute-done | bytes 131104 | tf_op jit(solution)/shard_map/ppermute | solution.py:67
  32.7 0.1 shard_map.42.own
  32.8 0.1 collective-permute-start.9
  32.9 0.5 collective-permute-start.6
  33.4 0.1 collective-permute-start.7
  33.4 0.8 %collective-permute-done.9.came = bf16[2,64,512]{2,1,0:T(8,128)(2,1)S(1)} collective-permute-done((bf16[2,64,512]{2,1,0:T(8,128)(2,1)S(1)}, bf16[2,64,512]{2,1,0:T(8,128)(2,1)S(1)}, u32[]{:S(2)}, u32[]{:S(2)}) %collective-permute-start.9) | collective-permute-done | bytes 131104 | tf_op jit(solution)/shard_map/ppermute | solution.py:67
  34.2 0.2 collective-permute-done.6.refs_0_
  34.4 0.3 collective-permute-done.7.refs_1_
  34.8 1.8 %collective-permute-start.10 = (bf16[2,64,512]{2,1,0:T(8,128)(2,1)S(1)}, bf16[2,64,512]{2,1,0:T(8,128)(2,1)S(1)}, u32[]{:S(2)}, u32[]{:S(2)}) collective-permute-start(bf16[2,64,512]{2,1,0:T(8,128)(2,1)S(1)} %get-tuple-element.44), channel_id=1, source_target_pairs={{0,2},{1,3},{2,0},{3,1},{4,6},{5,7},{6,4},{7,5},{8,10},{9,11},{10,... | collective-permute-start | bytes 393224 | tf_op jit(solution)/shard_map/ppermute | solution.py:67
  36.6 0.7 collective-permute-start.14
  37.2 2.8 %collective-permute-start.15 = (bf16[2,2,64,512]{3,2,1,0:T(8,128)(2,1)S(1)}, bf16[2,2,64,512]{3,2,1,0:T(8,128)(2,1)S(1)}, u32[]{:S(2)}, u32[]{:S(2)}) collective-permute-start(bf16[2,2,64,512]{3,2,1,0:T(8,128)(2,1)S(1)} %shard_map.43), channel_id=1, source_target_pairs={{2,0},{6,1},{10,2},{14,3},{0,4},{4,5},{8,6},{12,7},{3,8},{7,9},{11... | collective-permute-start | bytes 786440 | tf_op jit(solution)/shard_map/ppermute | solution.py:58
  40.1 0.3 collective-permute-done.10.came
  40.4 0.1 shard_map.45.own
  40.5 1.4 %collective-permute-start.11 = (bf16[2,64,512]{2,1,0:T(8,128)(2,1)S(1)}, bf16[2,64,512]{2,1,0:T(8,128)(2,1)S(1)}, u32[]{:S(2)}, u32[]{:S(2)}) collective-permute-start(bf16[2,64,512]{2,1,0:T(8,128)(2,1)S(1)} %shard_map.45.own), channel_id=1, source_target_pairs={{0,1},{1,0},{2,3},{3,2},{4,5},{5,4},{6,7},{7,6},{8,9},{9,8},{10,11... | collective-permute-start | bytes 393224 | tf_op jit(solution)/shard_map/ppermute | solution.py:67
  41.9 1.0 %collective-permute-done.11.came = bf16[2,64,512]{2,1,0:T(8,128)(2,1)S(1)} collective-permute-done((bf16[2,64,512]{2,1,0:T(8,128)(2,1)S(1)}, bf16[2,64,512]{2,1,0:T(8,128)(2,1)S(1)}, u32[]{:S(2)}, u32[]{:S(2)}) %collective-permute-start.11) | collective-permute-done | bytes 131104 | tf_op jit(solution)/shard_map/ppermute | solution.py:67
  42.9 0.7 collective-permute-start.12
  43.6 3.3 %collective-permute-start.13 = (bf16[2,2,64,512]{3,2,1,0:T(8,128)(2,1)S(1)}, bf16[2,2,64,512]{3,2,1,0:T(8,128)(2,1)S(1)}, u32[]{:S(2)}, u32[]{:S(2)}) collective-permute-start(bf16[2,2,64,512]{3,2,1,0:T(8,128)(2,1)S(1)} %shard_map.46), channel_id=1, source_target_pairs={{2,0},{6,1},{10,2},{14,3},{0,4},{4,5},{8,6},{12,7},{3,8},{7,9},{11... | collective-permute-start | bytes 786440 | tf_op jit(solution)/shard_map/ppermute | solution.py:58
  46.9 0.0 collective-permute-done.14.refs_0_
  46.9 0.0 collective-permute-done.15.refs_1_
  46.9 0.0 slice-done
  46.9 0.0 slice-done.1
  46.9 1.4 %shard_map.48 = (bf16[128,512]{1,0:T(8,128)(2,1)S(1)}, bf16[128,512]{1,0:T(8,128)(2,1)S(1)}) custom-call(bf16[2,2,64,512]{3,2,1,0:T(8,128)(2,1)S(1)} %collective-permute-done.14.refs_0_, bf16[2,2,64,512]{3,2,1,0:T(8,128)(2,1)S(1)} %collective-permute-done.15.refs_1_, bf16[3,3,512,512]{3,2,1,0:T(8,128)(2,1)S(1)} %bitcast.3), custom_call_target="tpu_custom_call" | custom-call | flops 1207959552 | bytes 5242880 | tf_op jit(solution)/shard_map/pallas_call | solution.py:71
  48.3 2.4 %collective-permute-start.16 = (bf16[128,512]{1,0:T(8,128)(2,1)S(1)}, bf16[128,512]{1,0:T(8,128)(2,1)S(1)}, u32[]{:S(2)}, u32[]{:S(2)}) collective-permute-start(bf16[128,512]{1,0:T(8,128)(2,1)S(1)} %get-tuple-element.48), channel_id=1, source_target_pairs={{0,1},{1,0},{2,3},{3,2},{4,5},{5,4},{6,7},{7,6},{8,9},{9,8},{10,11... | collective-permute-start | bytes 393224 | tf_op jit(solution)/shard_map/ppermute | solution.py:67
  50.8 0.1 collective-permute-start.17
  50.9 1.4 %shard_map.47 = bf16[256,512]{1,0:T(8,128)(2,1)S(1)} custom-call(bf16[2,2,64,512]{3,2,1,0:T(8,128)(2,1)S(1)} %collective-permute-done.14.refs_0_, bf16[2,2,64,512]{3,2,1,0:T(8,128)(2,1)S(1)} %collective-permute-done.15.refs_1_, bf16[3,3,512,512]{3,2,1,0:T(8,128)(2,1)S(1)} %bitcast.3), custom_call_target="tpu_custom_call" | custom-call | flops 1207959552 | bytes 5242880 | tf_op jit(solution)/shard_map/pallas_call | solution.py:71
  52.3 0.5 collective-permute-start.19
  52.8 0.0 collective-permute-done.12.refs_0_
  52.8 0.0 collective-permute-done.16.refs_2_.refs_3_
  52.8 0.0 collective-permute-done.17.refs_3_.refs_4_
  52.8 0.9 %shard_map.49 = bf16[112,512]{1,0:T(8,128)(2,1)S(1)} custom-call(bf16[2,2,64,512]{3,2,1,0:T(8,128)(2,1)S(1)} %collective-permute-done.12.refs_0_, bf16[3,3,512,512]{3,2,1,0:T(8,128)(2,1)S(1)} %bitcast.3, bf16[128,512]{1,0:T(8,128)(2,1)S(1)} %collective-permute-done.16.refs_2_.refs_3_, bf16[128,512]{1,0:T(8,128)(2,1)S(1)} %collective-permute-done.17.refs_3_.refs_4_), custom_call_target="tpu_custom_call" | custom-call | flops 528482304 | bytes 5242880 | tf_op jit(solution)/shard_map/pallas_call | solution.py:71
  53.7 11.1 %collective-permute-start.18 = (bf16[112,512]{1,0:T(8,128)(2,1)S(1)}, bf16[112,512]{1,0:T(8,128)(2,1)S(1)}, u32[]{:S(2)}, u32[]{:S(2)}) collective-permute-start(bf16[112,512]{1,0:T(8,128)(2,1)S(1)} %shard_map.49), channel_id=1, source_target_pairs={{0,2},{1,3},{2,0},{3,1},{4,6},{5,7},{6,4},{7,5},{8,10},{9,11},{10,... | collective-permute-start | bytes 344072 | tf_op jit(solution)/shard_map/ppermute | solution.py:67
  64.8 0.0 collective-permute-done.13.refs_1_
  64.8 1.0 %shard_map.50 = bf16[144,512]{1,0:T(8,128)(2,1)S(1)} custom-call(bf16[2,2,64,512]{3,2,1,0:T(8,128)(2,1)S(1)} %collective-permute-done.12.refs_0_, bf16[2,2,64,512]{3,2,1,0:T(8,128)(2,1)S(1)} %collective-permute-done.13.refs_1_, bf16[3,3,512,512]{3,2,1,0:T(8,128)(2,1)S(1)} %bitcast.3, bf16[128,512]{1,0:T(8,128)(2,1)S(1)} %collective-permute-done.16.refs_2_.refs_3_, ...), custom_call_target="tpu_custom_call" | custom-call | flops 679477248 | bytes 5505024 | tf_op jit(solution)/shard_map/pallas_call | solution.py:71
  65.7 0.1 collective-permute-start.20
  65.8 1.7 %collective-permute-done.18.refs_0_ = bf16[112,512]{1,0:T(8,128)(2,1)S(1)} collective-permute-done((bf16[112,512]{1,0:T(8,128)(2,1)S(1)}, bf16[112,512]{1,0:T(8,128)(2,1)S(1)}, u32[]{:S(2)}, u32[]{:S(2)}) %collective-permute-start.18) | collective-permute-done | bytes 114720 | tf_op jit(solution)/shard_map/ppermute | solution.py:67
  67.6 0.0 collective-permute-done.19.refs_3_
  67.6 1.4 %shard_map.51.kept = f32[256,512]{1,0:T(8,128)S(1)} custom-call(bf16[2,2,64,512]{3,2,1,0:T(8,128)(2,1)S(1)} %collective-permute-done.12.refs_0_, bf16[2,2,64,512]{3,2,1,0:T(8,128)(2,1)S(1)} %collective-permute-done.13.refs_1_, bf16[3,3,512,512]{3,2,1,0:T(8,128)(2,1)S(1)} %bitcast.3, bf16[256,512]{1,0:T(8,128)(2,1)S(1)} %collective-permute-done.19.refs_3_), custom_call_target="tpu_custom_call" | custom-call | flops 1207959552 | bytes 5505024 | tf_op jit(solution)/shard_map/pallas_call | solution.py:71
  69.0 2.0 %collective-permute-done.20.refs_1_ = bf16[144,512]{1,0:T(8,128)(2,1)S(1)} collective-permute-done((bf16[144,512]{1,0:T(8,128)(2,1)S(1)}, bf16[144,512]{1,0:T(8,128)(2,1)S(1)}, u32[]{:S(2)}, u32[]{:S(2)}) %collective-permute-start.20) | collective-permute-done | bytes 147488 | tf_op jit(solution)/shard_map/ppermute | solution.py:67
  71.0 0.8 %shard_map.52 = bf16[256,512]{1,0:T(8,128)(2,1)} custom-call(f32[256,512]{1,0:T(8,128)S(1)} %shard_map.51.kept, bf16[112,512]{1,0:T(8,128)(2,1)S(1)} %collective-permute-done.18.refs_0_, bf16[144,512]{1,0:T(8,128)(2,1)S(1)} %collective-permute-done.20.refs_1_), custom_call_target="tpu_custom_call" | custom-call | bytes 786432 | tf_op jit(solution)/shard_map/pallas_call | solution.py:71
  (4 shorter events, 0.1 us)
Async XLA Ops:
  0.0 11.2 %collective-permute-start.2 = (bf16[256,512]{1,0:T(8,128)(2,1)}, bf16[256,512]{1,0:T(8,128)(2,1)S(1)}, u32[]{:S(2)}, u32[]{:S(2)}) collective-permute-start(bf16[256,512]{1,0:T(8,128)(2,1)} %bitcast.4), channel_id=1, source_target_pairs={{0,12},{1,0},{2,4},{3,8},{4,13},{5,1},{6,5},{7,9},{8,14},{9,2},{10... | collective-permute-start | bytes 786440 | tf_op jit(solution)/shard_map/ppermute | solution.py:45
  5.0 11.8 %collective-permute-start.3 = (bf16[256,512]{1,0:T(8,128)(2,1)}, bf16[256,512]{1,0:T(8,128)(2,1)S(1)}, u32[]{:S(2)}, u32[]{:S(2)}) collective-permute-start(bf16[256,512]{1,0:T(8,128)(2,1)} %bitcast.5), channel_id=1, source_target_pairs={{0,4},{1,8},{2,12},{3,0},{4,5},{5,9},{6,13},{7,1},{8,6},{9,10},{10... | collective-permute-start | bytes 786440 | tf_op jit(solution)/shard_map/ppermute | solution.py:45
  5.1 23.9 %collective-permute-start = (bf16[256,512]{1,0:T(8,128)(2,1)}, bf16[256,512]{1,0:T(8,128)(2,1)S(1)}, u32[]{:S(2)}, u32[]{:S(2)}) collective-permute-start(bf16[256,512]{1,0:T(8,128)(2,1)} %bitcast.6), channel_id=1, source_target_pairs={{0,8},{1,12},{2,0},{3,4},{4,9},{5,13},{6,1},{7,5},{8,10},{9,14},{1... | collective-permute-start | bytes 786440 | tf_op jit(solution)/shard_map/ppermute | solution.py:45
  6.6 22.4 %collective-permute-start.1 = (bf16[256,512]{1,0:T(8,128)(2,1)}, bf16[256,512]{1,0:T(8,128)(2,1)S(1)}, u32[]{:S(2)}, u32[]{:S(2)}) collective-permute-start(bf16[256,512]{1,0:T(8,128)(2,1)} %bitcast.7), channel_id=1, source_target_pairs={{0,0},{1,4},{2,8},{3,12},{4,1},{5,5},{6,9},{7,13},{8,2},{9,6},{10,... | collective-permute-start | bytes 786440 | tf_op jit(solution)/shard_map/ppermute | solution.py:45
  8.2 2.3 %copy-start = (bf16[3,3,512,512]{3,2,1,0:T(8,128)(2,1)S(1)}, bf16[3,3,512,512]{3,2,1,0:T(8,128)(2,1)}, u32[]{:S(2)}) copy-start(bf16[3,3,512,512]{3,2,1,0:T(8,128)(2,1)} %source.1) | copy-start | bytes 14155780
  18.4 2.0 %collective-permute-start.4 = (bf16[128,512]{1,0:T(8,128)(2,1)S(1)}, bf16[128,512]{1,0:T(8,128)(2,1)S(1)}, u32[]{:S(2)}, u32[]{:S(2)}) collective-permute-start(bf16[128,512]{1,0:T(8,128)(2,1)S(1)} %get-tuple-element.31), channel_id=1, source_target_pairs={{0,1},{1,0},{2,3},{3,2},{4,5},{5,4},{6,7},{7,6},{8,9},{9,8},{10,11... | collective-permute-start | bytes 393224 | tf_op jit(solution)/shard_map/ppermute | solution.py:67
  18.5 1.9 %collective-permute-start.5 = (bf16[128,512]{1,0:T(8,128)(2,1)S(1)}, bf16[128,512]{1,0:T(8,128)(2,1)S(1)}, u32[]{:S(2)}, u32[]{:S(2)}) collective-permute-start(bf16[128,512]{1,0:T(8,128)(2,1)S(1)} %get-tuple-element.32), channel_id=1, source_target_pairs={{0,1},{1,0},{2,3},{3,2},{4,5},{5,4},{6,7},{7,6},{8,9},{9,8},{10,11... | collective-permute-start | bytes 393224 | tf_op jit(solution)/shard_map/ppermute | solution.py:67
  20.4 26.4 %slice-start = ((s8[4718592]{0:T(1024)(128)(4,1)}), s8[4194304]{0:T(1024)(128)(4,1)S(1)}, s32[]{:S(2)}) async-start(s8[4718592]{0:T(1024)(128)(4,1)} %bitcast.2), calls=%async_computation | async-start | bytes 8388608
  20.4 26.4 %slice-start.1 = ((s8[4718592]{0:T(1024)(128)(4,1)}), s8[524288]{0:T(1024)(128)(4,1)S(1)}, s32[]{:S(2)}) async-start(s8[4718592]{0:T(1024)(128)(4,1)} %bitcast.2), calls=%async_computation.1 | async-start | bytes 1048576
  20.5 12.3 %collective-permute-start.8 = (bf16[2,64,512]{2,1,0:T(8,128)(2,1)S(1)}, bf16[2,64,512]{2,1,0:T(8,128)(2,1)S(1)}, u32[]{:S(2)}, u32[]{:S(2)}) collective-permute-start(bf16[2,64,512]{2,1,0:T(8,128)(2,1)S(1)} %get-tuple-element.33), channel_id=1, source_target_pairs={{0,2},{1,3},{2,0},{3,1},{4,6},{5,7},{6,4},{7,5},{8,10},{9,11},{10,... | collective-permute-start | bytes 393224 | tf_op jit(solution)/shard_map/ppermute | solution.py:67
  32.8 1.4 %collective-permute-start.9 = (bf16[2,64,512]{2,1,0:T(8,128)(2,1)S(1)}, bf16[2,64,512]{2,1,0:T(8,128)(2,1)S(1)}, u32[]{:S(2)}, u32[]{:S(2)}) collective-permute-start(bf16[2,64,512]{2,1,0:T(8,128)(2,1)S(1)} %shard_map.42.own), channel_id=1, source_target_pairs={{0,1},{1,0},{2,3},{3,2},{4,5},{5,4},{6,7},{7,6},{8,9},{9,8},{10,11... | collective-permute-start | bytes 393224 | tf_op jit(solution)/shard_map/ppermute | solution.py:67
  32.9 1.5 %collective-permute-start.6 = (bf16[128,512]{1,0:T(8,128)(2,1)S(1)}, bf16[128,512]{1,0:T(8,128)(2,1)S(1)}, u32[]{:S(2)}, u32[]{:S(2)}) collective-permute-start(bf16[128,512]{1,0:T(8,128)(2,1)S(1)} %get-tuple-element.37), channel_id=1, source_target_pairs={{0,1},{1,0},{2,3},{3,2},{4,5},{5,4},{6,7},{7,6},{8,9},{9,8},{10,11... | collective-permute-start | bytes 393224 | tf_op jit(solution)/shard_map/ppermute | solution.py:67
  33.4 1.3 %collective-permute-start.7 = (bf16[128,512]{1,0:T(8,128)(2,1)S(1)}, bf16[128,512]{1,0:T(8,128)(2,1)S(1)}, u32[]{:S(2)}, u32[]{:S(2)}) collective-permute-start(bf16[128,512]{1,0:T(8,128)(2,1)S(1)} %get-tuple-element.38), channel_id=1, source_target_pairs={{0,1},{1,0},{2,3},{3,2},{4,5},{5,4},{6,7},{7,6},{8,9},{9,8},{10,11... | collective-permute-start | bytes 393224 | tf_op jit(solution)/shard_map/ppermute | solution.py:67
  34.8 5.7 %collective-permute-start.10 = (bf16[2,64,512]{2,1,0:T(8,128)(2,1)S(1)}, bf16[2,64,512]{2,1,0:T(8,128)(2,1)S(1)}, u32[]{:S(2)}, u32[]{:S(2)}) collective-permute-start(bf16[2,64,512]{2,1,0:T(8,128)(2,1)S(1)} %get-tuple-element.44), channel_id=1, source_target_pairs={{0,2},{1,3},{2,0},{3,1},{4,6},{5,7},{6,4},{7,5},{8,10},{9,11},{10,... | collective-permute-start | bytes 393224 | tf_op jit(solution)/shard_map/ppermute | solution.py:67
  36.6 10.3 %collective-permute-start.14 = (bf16[2,2,64,512]{3,2,1,0:T(8,128)(2,1)S(1)}, bf16[2,2,64,512]{3,2,1,0:T(8,128)(2,1)S(1)}, u32[]{:S(2)}, u32[]{:S(2)}) collective-permute-start(bf16[2,2,64,512]{3,2,1,0:T(8,128)(2,1)S(1)} %shard_map.43), channel_id=1, source_target_pairs={{0,0},{4,1},{8,2},{12,3},{2,4},{6,5},{10,6},{14,7},{1,8},{5,9},{9,... | collective-permute-start | bytes 786440 | tf_op jit(solution)/shard_map/ppermute | solution.py:58
  37.2 9.6 %collective-permute-start.15 = (bf16[2,2,64,512]{3,2,1,0:T(8,128)(2,1)S(1)}, bf16[2,2,64,512]{3,2,1,0:T(8,128)(2,1)S(1)}, u32[]{:S(2)}, u32[]{:S(2)}) collective-permute-start(bf16[2,2,64,512]{3,2,1,0:T(8,128)(2,1)S(1)} %shard_map.43), channel_id=1, source_target_pairs={{2,0},{6,1},{10,2},{14,3},{0,4},{4,5},{8,6},{12,7},{3,8},{7,9},{11... | collective-permute-start | bytes 786440 | tf_op jit(solution)/shard_map/ppermute | solution.py:58
  40.5 2.4 %collective-permute-start.11 = (bf16[2,64,512]{2,1,0:T(8,128)(2,1)S(1)}, bf16[2,64,512]{2,1,0:T(8,128)(2,1)S(1)}, u32[]{:S(2)}, u32[]{:S(2)}) collective-permute-start(bf16[2,64,512]{2,1,0:T(8,128)(2,1)S(1)} %shard_map.45.own), channel_id=1, source_target_pairs={{0,1},{1,0},{2,3},{3,2},{4,5},{5,4},{6,7},{7,6},{8,9},{9,8},{10,11... | collective-permute-start | bytes 393224 | tf_op jit(solution)/shard_map/ppermute | solution.py:67
  42.9 9.9 %collective-permute-start.12 = (bf16[2,2,64,512]{3,2,1,0:T(8,128)(2,1)S(1)}, bf16[2,2,64,512]{3,2,1,0:T(8,128)(2,1)S(1)}, u32[]{:S(2)}, u32[]{:S(2)}) collective-permute-start(bf16[2,2,64,512]{3,2,1,0:T(8,128)(2,1)S(1)} %shard_map.46), channel_id=1, source_target_pairs={{0,0},{4,1},{8,2},{12,3},{2,4},{6,5},{10,6},{14,7},{1,8},{5,9},{9,... | collective-permute-start | bytes 786440 | tf_op jit(solution)/shard_map/ppermute | solution.py:58
  43.6 21.2 %collective-permute-start.13 = (bf16[2,2,64,512]{3,2,1,0:T(8,128)(2,1)S(1)}, bf16[2,2,64,512]{3,2,1,0:T(8,128)(2,1)S(1)}, u32[]{:S(2)}, u32[]{:S(2)}) collective-permute-start(bf16[2,2,64,512]{3,2,1,0:T(8,128)(2,1)S(1)} %shard_map.46), channel_id=1, source_target_pairs={{2,0},{6,1},{10,2},{14,3},{0,4},{4,5},{8,6},{12,7},{3,8},{7,9},{11... | collective-permute-start | bytes 786440 | tf_op jit(solution)/shard_map/ppermute | solution.py:58
  48.3 4.5 %collective-permute-start.16 = (bf16[128,512]{1,0:T(8,128)(2,1)S(1)}, bf16[128,512]{1,0:T(8,128)(2,1)S(1)}, u32[]{:S(2)}, u32[]{:S(2)}) collective-permute-start(bf16[128,512]{1,0:T(8,128)(2,1)S(1)} %get-tuple-element.48), channel_id=1, source_target_pairs={{0,1},{1,0},{2,3},{3,2},{4,5},{5,4},{6,7},{7,6},{8,9},{9,8},{10,11... | collective-permute-start | bytes 393224 | tf_op jit(solution)/shard_map/ppermute | solution.py:67
  50.8 2.0 %collective-permute-start.17 = (bf16[128,512]{1,0:T(8,128)(2,1)S(1)}, bf16[128,512]{1,0:T(8,128)(2,1)S(1)}, u32[]{:S(2)}, u32[]{:S(2)}) collective-permute-start(bf16[128,512]{1,0:T(8,128)(2,1)S(1)} %get-tuple-element.49), channel_id=1, source_target_pairs={{0,1},{1,0},{2,3},{3,2},{4,5},{5,4},{6,7},{7,6},{8,9},{9,8},{10,11... | collective-permute-start | bytes 393224 | tf_op jit(solution)/shard_map/ppermute | solution.py:67
  52.3 15.2 %collective-permute-start.19 = (bf16[256,512]{1,0:T(8,128)(2,1)S(1)}, bf16[256,512]{1,0:T(8,128)(2,1)S(1)}, u32[]{:S(2)}, u32[]{:S(2)}) collective-permute-start(bf16[256,512]{1,0:T(8,128)(2,1)S(1)} %shard_map.47), channel_id=1, source_target_pairs={{0,1},{1,0},{2,3},{3,2},{4,5},{5,4},{6,7},{7,6},{8,9},{9,8},{10,11... | collective-permute-start | bytes 786440 | tf_op jit(solution)/shard_map/ppermute | solution.py:67
  53.7 13.9 %collective-permute-start.18 = (bf16[112,512]{1,0:T(8,128)(2,1)S(1)}, bf16[112,512]{1,0:T(8,128)(2,1)S(1)}, u32[]{:S(2)}, u32[]{:S(2)}) collective-permute-start(bf16[112,512]{1,0:T(8,128)(2,1)S(1)} %shard_map.49), channel_id=1, source_target_pairs={{0,2},{1,3},{2,0},{3,1},{4,6},{5,7},{6,4},{7,5},{8,10},{9,11},{10,... | collective-permute-start | bytes 344072 | tf_op jit(solution)/shard_map/ppermute | solution.py:67
  65.7 5.2 %collective-permute-start.20 = (bf16[144,512]{1,0:T(8,128)(2,1)S(1)}, bf16[144,512]{1,0:T(8,128)(2,1)S(1)}, u32[]{:S(2)}, u32[]{:S(2)}) collective-permute-start(bf16[144,512]{1,0:T(8,128)(2,1)S(1)} %shard_map.50), channel_id=1, source_target_pairs={{0,2},{1,3},{2,0},{3,1},{4,6},{5,7},{6,4},{7,5},{8,10},{9,11},{10,... | collective-permute-start | bytes 442376 | tf_op jit(solution)/shard_map/ppermute | solution.py:67

commit v6 on v5

--- a/solution.py
+++ b/solution.py
@@ -140,32 +140,6 @@
     return jnp.concatenate(blocks, axis=0)
 
 
-def one_body(plan, *refs):
-    frames = refs[-1].shape[0]
-    pieces, (kernel, keep, *sends, wide) = refs[: frames * plan.ratio], refs[frames * plan.ratio :]
-    level, col = where_am_i()
-    clear_edges(plan, wide)
-    for n, piece in enumerate(pieces):
-        place(plan, piece[...], n // plan.ratio, plan.width, plan.lanes(level, n % plan.ratio), wide)
-    halves = lambda a: jnp.concatenate([half_rows(plan, wide, core, a) for core in (1 - col % 2, col % 2)], axis=0)
-    summed = times(plan, halves, kernel)
-    size = summed.shape[0] // 2
-    keep[...] = summed[size:].reshape(keep.shape)
-    for n, send in enumerate(sends):
-        rows = send.shape[0]
-        send[...] = summed[n * rows : (n + 1) * rows].astype(BF16)
-
-
-def conv_one(plan, pieces, kernel):
-    frames = len(pieces) // plan.ratio
-    half = (frames, plan.pixels // 2, plan.c_out)
-    flops = 18 * frames * plan.pixels * plan.c_in * plan.c_out
-    outputs = [(half, F32)] + [(half[1:], BF16)] * frames
-    scratch = [pltpu.VMEM(plan.wide(frames), BF16)]
-    keep, *sends = plan.call(functools.partial(one_body, plan), [*pieces, kernel], outputs, flops, scratch)
-    return keep, [plan.swap(send, 0) for send in sends]
-
-
 def one_sent_body(plan, *refs):
     frames = refs[-1].shape[0]
     pieces, (kernel, *sends, wide) = refs[: frames * plan.ratio], refs[frames * plan.ratio :]
@@ -184,11 +158,11 @@
     keep[...] = times(plan, lambda a: half_rows(plan, wide, col % 2, a), kernel).reshape(keep.shape)
 
 
-def conv_one_in_two(plan, pieces, kernel):
+def conv_one_in_two(plan, pieces, kernel, parts):
     frames = len(pieces) // plan.ratio
     half = (frames, plan.pixels // 2, plan.c_out)
     flops = 9 * frames * plan.pixels * plan.c_in * plan.c_out
-    outputs = [(half[1:], BF16)] * frames + [(plan.wide(frames), BF16)]
+    outputs = [((half[1] // parts, half[2]), BF16)] * (frames * parts) + [(plan.wide(frames), BF16)]
     *sends, wide = plan.call(functools.partial(one_sent_body, plan), [*pieces, kernel], outputs, flops)
     cames = [plan.swap(send, 0) for send in sends]
     keep = plan.call(functools.partial(one_kept_body, plan), [wide, kernel], [(half, F32)], flops)[0]
@@ -197,13 +171,19 @@
 
 def halve_body(bit, kept, *refs):
     *cames, keep, send = refs
-    half = keep.shape[1]
-    mine = (lax.axis_index("img") // 2**bit) % 2 * half
+    frames, half = keep.shape[0], keep.shape[1]
+    low = (lax.axis_index("img") // 2**bit) % 2 == 0
+    mine = jnp.where(low, 0, half)
     a = pl.ds(pl.multiple_of(mine, 16), half)
     b = pl.ds(pl.multiple_of(half - mine, 16), half)
-    for n, came in enumerate(cames):
-        send[n] = (kept[n, b, :] + came[b, :].astype(F32)).astype(BF16)
-        keep[n] = kept[n, a, :] + came[a, :].astype(F32)
+    for n in range(frames):
+        if len(cames) == frames:
+            mine_came, other_came = cames[n][a, :], cames[n][b, :]
+        else:
+            first, second = cames[2 * n][...], cames[2 * n + 1][...]
+            mine_came, other_came = jnp.where(low, first, second), jnp.where(low, second, first)
+        send[n] = (kept[n, b, :] + other_came.astype(F32)).astype(BF16)
+        keep[n] = kept[n, a, :] + mine_came.astype(F32)
 
 
 def silu_body(kept, came, hidden):
@@ -393,12 +373,12 @@
     kernel_one = stage(kernel_one)
     late = [p for d in even for p in plan.spread_frame(block, d)]
     last = plan.order[-1]
-    keep, ahead = sum_one(plan, *conv_one_in_two(plan, early, kernel_one))
-    kept, cames = conv_one(plan, after(late, ahead), kernel_one)
-    hidden = join(plan, add_silu(plan, keep, after(plan.swap(ahead, last), kept)))
+    keep, ahead = sum_one(plan, *conv_one_in_two(plan, early, kernel_one, 1))
+    kept, cames = conv_one_in_two(plan, after(late, ahead), kernel_one, 2)
+    kept, behind = sum_one(plan, kept, cames)
+    hidden = join(plan, add_silu(plan, keep, after(plan.swap(ahead, last), behind)))
     odds = [p for t in range(plan.pairs) for p in plan.spread(hidden, t)]
-    keep, behind = sum_one(plan, kept, after(cames, hidden))
-    hidden = join(plan, add_silu(plan, keep, plan.swap(behind, last)))
+    hidden = join(plan, add_silu(plan, kept, plan.swap(behind, last)))
     evens = [p for t in range(plan.pairs) for p in plan.spread(hidden, t)]
     return sum_in_parts(plan, odds, evens, hidden, kernel_two).reshape(features.shape)
 

time: 71.9 us -> 71.2 us (level)
  waiting for transfers between devices: 13.3 us -> 11.2 us
  starting transfers between devices: 42.7 us -> 43.7 us
    ppermute x13 -> x15, waiting for transfers between devices: 7.29 us -> 5.25 us  [swap(): return lax.ppermute(x, 'img', [(i, i ^ 1 << bit) for i in range(self.cols)])]
    ppermute x13 -> x15, starting transfers between devices: 27.1 us -> 27.8 us  [swap(): return lax.ppermute(x, 'img', [(i, i ^ 1 << bit) for i in range(self.cols)])]
    pallas_call x15 -> x16, Pallas kernels: 12.8 us -> 13.1 us  [call(): pl.pallas_call(body, in_specs=[VMEM] * len(inputs), out_specs=[VMEM] * le...]
  transfers between devices with their start and end apart: 21 -> 23, of which waited for: 10 -> 6; matrix products, arithmetic and copies ran while one was open for 0% -> 0% of each run, Pallas kernels for 17% -> 18%
where the time goes in v6:
time: 71.2 us; the launch traced here: 70.9 us
  starting transfers between devices  43.7 us (61%)
  Pallas kernels  13.4 us (19%)
  waiting for transfers between devices  11.2 us (16%)
  local copies, waits for them, and re-layouts  2.34 us (3%)
    ppermute x15, starting transfers between devices, swap(): return lax.ppermute(x, 'img', [(i, i ^ 1 << bit) for i in range(self.cols)])  27.8 us
    pallas_call x16, Pallas kernels, call(): pl.pallas_call(body, in_specs=[VMEM] * len(inputs), out_specs=[VMEM] * le...  13.1 us
    ppermute x4, starting transfers between devices, spread_frame(): taken.append(lax.ppermute(x, ('chan', 'img'), moves))  8.17 us
    ppermute x4, starting transfers between devices, spread(): taken.append(lax.ppermute(x, ('chan', 'img'), moves))  7.72 us
    ppermute x4, waiting for transfers between devices, spread_frame(): taken.append(lax.ppermute(x, ('chan', 'img'), moves))  5.99 us
    ppermute x15, waiting for transfers between devices, swap(): return lax.ppermute(x, 'img', [(i, i ^ 1 << bit) for i in range(self.cols)])  5.25 us
    unnamed x6, local copies, waits for them, and re-layouts  2.34 us
  transfers between devices with their start and end apart: 23, of which 6 were waited for; matrix products, arithmetic and copies ran while one was open for 0% of the time, Pallas kernels for 18%

profile of v6, /device:TPU:0, one launch (start us, length us, event | category | flops | bytes accessed | tf_op | source)
XLA Modules:
  0.0 70.9 jit_solution(380101022286379410)
XLA Ops:
  0.0 5.0 %collective-permute-start.2 = (bf16[256,512]{1,0:T(8,128)(2,1)}, bf16[256,512]{1,0:T(8,128)(2,1)S(1)}, u32[]{:S(2)}, u32[]{:S(2)}) collective-permute-start(bf16[256,512]{1,0:T(8,128)(2,1)} %bitcast.4), channel_id=1, source_target_pairs={{0,12},{1,0},{2,4},{3,8},{4,13},{5,1},{6,5},{7,9},{8,14},{9,2},{10... | collective-permute-start | bytes 786440 | tf_op jit(solution)/shard_map/ppermute | solution.py:45
  5.0 0.0 collective-permute-start.3
  5.1 1.5 %collective-permute-start = (bf16[256,512]{1,0:T(8,128)(2,1)}, bf16[256,512]{1,0:T(8,128)(2,1)S(1)}, u32[]{:S(2)}, u32[]{:S(2)}) collective-permute-start(bf16[256,512]{1,0:T(8,128)(2,1)} %bitcast.6), channel_id=1, source_target_pairs={{0,8},{1,12},{2,0},{3,4},{4,9},{5,13},{6,1},{7,5},{8,10},{9,14},{1... | collective-permute-start | bytes 786440 | tf_op jit(solution)/shard_map/ppermute | solution.py:45
  6.6 1.6 %collective-permute-start.1 = (bf16[256,512]{1,0:T(8,128)(2,1)}, bf16[256,512]{1,0:T(8,128)(2,1)S(1)}, u32[]{:S(2)}, u32[]{:S(2)}) collective-permute-start(bf16[256,512]{1,0:T(8,128)(2,1)} %bitcast.7), channel_id=1, source_target_pairs={{0,0},{1,4},{2,8},{3,12},{4,1},{5,5},{6,9},{7,13},{8,2},{9,6},{10,... | collective-permute-start | bytes 786440 | tf_op jit(solution)/shard_map/ppermute | solution.py:45
  8.2 2.3 %copy-done = bf16[3,3,512,512]{3,2,1,0:T(8,128)(2,1)S(1)} copy-done((bf16[3,3,512,512]{3,2,1,0:T(8,128)(2,1)S(1)}, bf16[3,3,512,512]{3,2,1,0:T(8,128)(2,1)}, u32[]{:S(2)}) %copy-start) | copy-done | bytes 4718616
  10.5 0.3 shard_map.37.refs_2_.kernel
  10.8 0.4 collective-permute-done.2.refs_0_
  11.2 5.6 %collective-permute-done.3.refs_1_ = bf16[256,512]{1,0:T(8,128)(2,1)S(1)} collective-permute-done((bf16[256,512]{1,0:T(8,128)(2,1)}, bf16[256,512]{1,0:T(8,128)(2,1)S(1)}, u32[]{:S(2)}, u32[]{:S(2)}) %collective-permute-start.3) | collective-permute-done | bytes 262176 | tf_op jit(solution)/shard_map/ppermute | solution.py:45
  16.8 1.6 %shard_map.38 = (bf16[128,512]{1,0:T(8,128)(2,1)S(1)}, bf16[128,512]{1,0:T(8,128)(2,1)S(1)}, bf16[2,288,1536]{2,1,0:T(8,128)(2,1)S(1)}) custom-call(bf16[256,512]{1,0:T(8,128)(2,1)S(1)} %collective-permute-done.2.refs_0_, bf16[256,512]{1,0:T(8,128)(2,1)S(1)} %collective-permute-done.3.refs_1_, bf16[3,3,512,512]{3,2,1,0:T(8,128)(2,1)S(1)} %shard_map.37.refs_2_.kernel), custom_call_target="tpu_custom_call" | custom-call | flops 1207959552 | bytes 5242880 | tf_op jit(solution)/shard_map/pallas_call | solution.py:71
  18.4 0.1 collective-permute-start.4
  18.5 0.5 collective-permute-start.5
  19.0 1.4 %shard_map.39.kept = f32[2,128,512]{2,1,0:T(8,128)S(1)} custom-call(bf16[2,288,1536]{2,1,0:T(8,128)(2,1)S(1)} %get-tuple-element.30.wide, bf16[3,3,512,512]{3,2,1,0:T(8,128)(2,1)S(1)} %shard_map.37.refs_2_.kernel), custom_call_target="tpu_custom_call" | custom-call | flops 1207959552 | bytes 6488064 | tf_op jit(solution)/shard_map/pallas_call | solution.py:71
  20.3 0.0 collective-permute-done.4.refs_0_
  20.3 0.0 collective-permute-done.5.refs_1_
  20.4 0.1 shard_map.40
  20.4 8.5 %collective-permute-start.14 = (bf16[2,64,512]{2,1,0:T(8,128)(2,1)S(1)}, bf16[2,64,512]{2,1,0:T(8,128)(2,1)S(1)}, u32[]{:S(2)}, u32[]{:S(2)}) collective-permute-start(bf16[2,64,512]{2,1,0:T(8,128)(2,1)S(1)} %get-tuple-element.33), channel_id=1, source_target_pairs={{0,2},{1,3},{2,0},{3,1},{4,6},{5,7},{6,4},{7,5},{8,10},{9,11},{10,... | collective-permute-start | bytes 393224 | tf_op jit(solution)/shard_map/ppermute | solution.py:67
  28.9 0.0 collective-permute-done.refs_0_
  28.9 0.0 collective-permute-done.1.refs_1_
  29.0 1.5 %shard_map.41 = (bf16[64,512]{1,0:T(8,128)(2,1)S(1)}, bf16[64,512]{1,0:T(8,128)(2,1)S(1)}, bf16[64,512]{1,0:T(8,128)(2,1)S(1)}, bf16[64,512]{1,0:T(8,128)(2,1)S(1)}, bf16[2,288,1536]{2,1,0:T(8,128)(2,1)S(1)}) custom-call(bf16[256,512]{1,0:T(8,128)(2,1)S(1)} %collective-permute-done.refs_0_, bf16[256,512]{1,0:T(8,128)(2,1)S(1)} %collective-permute-done.1.refs_1_, ...), custom_call_target="tpu_custom_call" | custom-call | flops 1207959552 | bytes 5242880 | tf_op jit(solution)/shard_map/pallas_call | solution.py:71
  30.5 0.1 collective-permute-start.6
  30.6 0.5 collective-permute-start.7
  31.1 0.1 collective-permute-start.8
  31.2 0.4 collective-permute-start.9
  31.6 1.4 %shard_map.42.kept = f32[2,128,512]{2,1,0:T(8,128)S(1)} custom-call(bf16[2,288,1536]{2,1,0:T(8,128)(2,1)S(1)} %get-tuple-element.36.wide, bf16[3,3,512,512]{3,2,1,0:T(8,128)(2,1)S(1)} %shard_map.37.refs_2_.kernel), custom_call_target="tpu_custom_call" | custom-call | flops 1207959552 | bytes 6488064 | tf_op jit(solution)/shard_map/pallas_call | solution.py:71
  33.0 0.0 collective-permute-done.6.refs_0_
  33.0 0.0 collective-permute-done.7.refs_1_
  33.0 0.0 collective-permute-done.8.refs_2_
  33.0 0.0 collective-permute-done.9.refs_3_
  33.0 0.1 shard_map.43
  33.1 0.0 collective-permute-done.14.came
  33.1 0.1 shard_map.46.own
  33.2 0.1 collective-permute-start.15
  33.3 1.5 %collective-permute-start.10 = (bf16[2,64,512]{2,1,0:T(8,128)(2,1)S(1)}, bf16[2,64,512]{2,1,0:T(8,128)(2,1)S(1)}, u32[]{:S(2)}, u32[]{:S(2)}) collective-permute-start(bf16[2,64,512]{2,1,0:T(8,128)(2,1)S(1)} %get-tuple-element.42), channel_id=1, source_target_pairs={{0,2},{1,3},{2,0},{3,1},{4,6},{5,7},{6,4},{7,5},{8,10},{9,11},{10,... | collective-permute-start | bytes 393224 | tf_op jit(solution)/shard_map/ppermute | solution.py:67
  34.8 0.0 collective-permute-done.15.came
  34.9 0.7 collective-permute-start.16
  35.6 3.1 %collective-permute-start.17 = (bf16[2,2,64,512]{3,2,1,0:T(8,128)(2,1)S(1)}, bf16[2,2,64,512]{3,2,1,0:T(8,128)(2,1)S(1)}, u32[]{:S(2)}, u32[]{:S(2)}) collective-permute-start(bf16[2,2,64,512]{3,2,1,0:T(8,128)(2,1)S(1)} %shard_map.47), channel_id=1, source_target_pairs={{2,0},{6,1},{10,2},{14,3},{0,4},{4,5},{8,6},{12,7},{3,8},{7,9},{11... | collective-permute-start | bytes 786440 | tf_op jit(solution)/shard_map/ppermute | solution.py:58
  38.6 0.5 collective-permute-done.10.came
  39.2 0.1 shard_map.44.own
  39.3 2.1 %collective-permute-start.11 = (bf16[2,64,512]{2,1,0:T(8,128)(2,1)S(1)}, bf16[2,64,512]{2,1,0:T(8,128)(2,1)S(1)}, u32[]{:S(2)}, u32[]{:S(2)}) collective-permute-start(bf16[2,64,512]{2,1,0:T(8,128)(2,1)S(1)} %shard_map.44.own), channel_id=1, source_target_pairs={{0,1},{1,0},{2,3},{3,2},{4,5},{5,4},{6,7},{7,6},{8,9},{9,8},{10,11... | collective-permute-start | bytes 393224 | tf_op jit(solution)/shard_map/ppermute | solution.py:67
  41.4 1.0 %collective-permute-done.11.came = bf16[2,64,512]{2,1,0:T(8,128)(2,1)S(1)} collective-permute-done((bf16[2,64,512]{2,1,0:T(8,128)(2,1)S(1)}, bf16[2,64,512]{2,1,0:T(8,128)(2,1)S(1)}, u32[]{:S(2)}, u32[]{:S(2)}) %collective-permute-start.11) | collective-permute-done | bytes 131104 | tf_op jit(solution)/shard_map/ppermute | solution.py:67
  42.4 0.7 collective-permute-start.12
  43.1 3.3 %collective-permute-start.13 = (bf16[2,2,64,512]{3,2,1,0:T(8,128)(2,1)S(1)}, bf16[2,2,64,512]{3,2,1,0:T(8,128)(2,1)S(1)}, u32[]{:S(2)}, u32[]{:S(2)}) collective-permute-start(bf16[2,2,64,512]{3,2,1,0:T(8,128)(2,1)S(1)} %shard_map.45), channel_id=1, source_target_pairs={{2,0},{6,1},{10,2},{14,3},{0,4},{4,5},{8,6},{12,7},{3,8},{7,9},{11... | collective-permute-start | bytes 786440 | tf_op jit(solution)/shard_map/ppermute | solution.py:58
  46.4 0.0 collective-permute-done.16.refs_0_
  46.4 0.0 collective-permute-done.17.refs_1_
  46.4 0.0 slice-done
  46.4 0.0 slice-done.1
  46.4 1.4 %shard_map.49 = (bf16[128,512]{1,0:T(8,128)(2,1)S(1)}, bf16[128,512]{1,0:T(8,128)(2,1)S(1)}) custom-call(bf16[2,2,64,512]{3,2,1,0:T(8,128)(2,1)S(1)} %collective-permute-done.16.refs_0_, bf16[2,2,64,512]{3,2,1,0:T(8,128)(2,1)S(1)} %collective-permute-done.17.refs_1_, bf16[3,3,512,512]{3,2,1,0:T(8,128)(2,1)S(1)} %bitcast.3), custom_call_target="tpu_custom_call" | custom-call | flops 1207959552 | bytes 5242880 | tf_op jit(solution)/shard_map/pallas_call | solution.py:71
  47.9 2.2 %collective-permute-start.18 = (bf16[128,512]{1,0:T(8,128)(2,1)S(1)}, bf16[128,512]{1,0:T(8,128)(2,1)S(1)}, u32[]{:S(2)}, u32[]{:S(2)}) collective-permute-start(bf16[128,512]{1,0:T(8,128)(2,1)S(1)} %get-tuple-element.48), channel_id=1, source_target_pairs={{0,1},{1,0},{2,3},{3,2},{4,5},{5,4},{6,7},{7,6},{8,9},{9,8},{10,11... | collective-permute-start | bytes 393224 | tf_op jit(solution)/shard_map/ppermute | solution.py:67
  50.1 0.1 collective-permute-start.19
  50.2 1.4 %shard_map.48 = bf16[256,512]{1,0:T(8,128)(2,1)S(1)} custom-call(bf16[2,2,64,512]{3,2,1,0:T(8,128)(2,1)S(1)} %collective-permute-done.16.refs_0_, bf16[2,2,64,512]{3,2,1,0:T(8,128)(2,1)S(1)} %collective-permute-done.17.refs_1_, bf16[3,3,512,512]{3,2,1,0:T(8,128)(2,1)S(1)} %bitcast.3), custom_call_target="tpu_custom_call" | custom-call | flops 1207959552 | bytes 5242880 | tf_op jit(solution)/shard_map/pallas_call | solution.py:71
  51.6 0.5 collective-permute-start.21
  52.1 0.0 collective-permute-done.12.refs_0_
  52.1 0.0 collective-permute-done.18.refs_2_.refs_3_
  52.1 0.0 collective-permute-done.19.refs_3_.refs_4_
  52.1 0.9 %shard_map.50 = bf16[112,512]{1,0:T(8,128)(2,1)S(1)} custom-call(bf16[2,2,64,512]{3,2,1,0:T(8,128)(2,1)S(1)} %collective-permute-done.12.refs_0_, bf16[3,3,512,512]{3,2,1,0:T(8,128)(2,1)S(1)} %bitcast.3, bf16[128,512]{1,0:T(8,128)(2,1)S(1)} %collective-permute-done.18.refs_2_.refs_3_, bf16[128,512]{1,0:T(8,128)(2,1)S(1)} %collective-permute-done.19.refs_3_.refs_4_), custom_call_target="tpu_custom_call" | custom-call | flops 528482304 | bytes 5242880 | tf_op jit(solution)/shard_map/pallas_call | solution.py:71
  53.0 11.0 %collective-permute-start.20 = (bf16[112,512]{1,0:T(8,128)(2,1)S(1)}, bf16[112,512]{1,0:T(8,128)(2,1)S(1)}, u32[]{:S(2)}, u32[]{:S(2)}) collective-permute-start(bf16[112,512]{1,0:T(8,128)(2,1)S(1)} %shard_map.50), channel_id=1, source_target_pairs={{0,2},{1,3},{2,0},{3,1},{4,6},{5,7},{6,4},{7,5},{8,10},{9,11},{10,... | collective-permute-start | bytes 344072 | tf_op jit(solution)/shard_map/ppermute | solution.py:67
  64.0 0.0 collective-permute-done.13.refs_1_
  64.0 1.0 %shard_map.51 = bf16[144,512]{1,0:T(8,128)(2,1)S(1)} custom-call(bf16[2,2,64,512]{3,2,1,0:T(8,128)(2,1)S(1)} %collective-permute-done.12.refs_0_, bf16[2,2,64,512]{3,2,1,0:T(8,128)(2,1)S(1)} %collective-permute-done.13.refs_1_, bf16[3,3,512,512]{3,2,1,0:T(8,128)(2,1)S(1)} %bitcast.3, bf16[128,512]{1,0:T(8,128)(2,1)S(1)} %collective-permute-done.18.refs_2_.refs_3_, ...), custom_call_target="tpu_custom_call" | custom-call | flops 679477248 | bytes 5505024 | tf_op jit(solution)/shard_map/pallas_call | solution.py:71
  65.0 0.1 collective-permute-start.22
  65.1 1.7 %collective-permute-done.20.refs_0_ = bf16[112,512]{1,0:T(8,128)(2,1)S(1)} collective-permute-done((bf16[112,512]{1,0:T(8,128)(2,1)S(1)}, bf16[112,512]{1,0:T(8,128)(2,1)S(1)}, u32[]{:S(2)}, u32[]{:S(2)}) %collective-permute-start.20) | collective-permute-done | bytes 114720 | tf_op jit(solution)/shard_map/ppermute | solution.py:67
  66.8 0.0 collective-permute-done.21.refs_3_
  66.8 1.4 %shard_map.52.kept = f32[256,512]{1,0:T(8,128)S(1)} custom-call(bf16[2,2,64,512]{3,2,1,0:T(8,128)(2,1)S(1)} %collective-permute-done.12.refs_0_, bf16[2,2,64,512]{3,2,1,0:T(8,128)(2,1)S(1)} %collective-permute-done.13.refs_1_, bf16[3,3,512,512]{3,2,1,0:T(8,128)(2,1)S(1)} %bitcast.3, bf16[256,512]{1,0:T(8,128)(2,1)S(1)} %collective-permute-done.21.refs_3_), custom_call_target="tpu_custom_call" | custom-call | flops 1207959552 | bytes 5505024 | tf_op jit(solution)/shard_map/pallas_call | solution.py:71
  68.2 2.0 %collective-permute-done.22.refs_1_ = bf16[144,512]{1,0:T(8,128)(2,1)S(1)} collective-permute-done((bf16[144,512]{1,0:T(8,128)(2,1)S(1)}, bf16[144,512]{1,0:T(8,128)(2,1)S(1)}, u32[]{:S(2)}, u32[]{:S(2)}) %collective-permute-start.22) | collective-permute-done | bytes 147488 | tf_op jit(solution)/shard_map/ppermute | solution.py:67
  70.2 0.8 %shard_map.53 = bf16[256,512]{1,0:T(8,128)(2,1)} custom-call(f32[256,512]{1,0:T(8,128)S(1)} %shard_map.52.kept, bf16[112,512]{1,0:T(8,128)(2,1)S(1)} %collective-permute-done.20.refs_0_, bf16[144,512]{1,0:T(8,128)(2,1)S(1)} %collective-permute-done.22.refs_1_), custom_call_target="tpu_custom_call" | custom-call | bytes 786432 | tf_op jit(solution)/shard_map/pallas_call | solution.py:71
  (6 shorter events, 0.1 us)
Async XLA Ops:
  0.0 11.2 %collective-permute-start.2 = (bf16[256,512]{1,0:T(8,128)(2,1)}, bf16[256,512]{1,0:T(8,128)(2,1)S(1)}, u32[]{:S(2)}, u32[]{:S(2)}) collective-permute-start(bf16[256,512]{1,0:T(8,128)(2,1)} %bitcast.4), channel_id=1, source_target_pairs={{0,12},{1,0},{2,4},{3,8},{4,13},{5,1},{6,5},{7,9},{8,14},{9,2},{10... | collective-permute-start | bytes 786440 | tf_op jit(solution)/shard_map/ppermute | solution.py:45
  5.0 11.8 %collective-permute-start.3 = (bf16[256,512]{1,0:T(8,128)(2,1)}, bf16[256,512]{1,0:T(8,128)(2,1)S(1)}, u32[]{:S(2)}, u32[]{:S(2)}) collective-permute-start(bf16[256,512]{1,0:T(8,128)(2,1)} %bitcast.5), channel_id=1, source_target_pairs={{0,4},{1,8},{2,12},{3,0},{4,5},{5,9},{6,13},{7,1},{8,6},{9,10},{10... | collective-permute-start | bytes 786440 | tf_op jit(solution)/shard_map/ppermute | solution.py:45
  5.1 23.9 %collective-permute-start = (bf16[256,512]{1,0:T(8,128)(2,1)}, bf16[256,512]{1,0:T(8,128)(2,1)S(1)}, u32[]{:S(2)}, u32[]{:S(2)}) collective-permute-start(bf16[256,512]{1,0:T(8,128)(2,1)} %bitcast.6), channel_id=1, source_target_pairs={{0,8},{1,12},{2,0},{3,4},{4,9},{5,13},{6,1},{7,5},{8,10},{9,14},{1... | collective-permute-start | bytes 786440 | tf_op jit(solution)/shard_map/ppermute | solution.py:45
  6.6 22.4 %collective-permute-start.1 = (bf16[256,512]{1,0:T(8,128)(2,1)}, bf16[256,512]{1,0:T(8,128)(2,1)S(1)}, u32[]{:S(2)}, u32[]{:S(2)}) collective-permute-start(bf16[256,512]{1,0:T(8,128)(2,1)} %bitcast.7), channel_id=1, source_target_pairs={{0,0},{1,4},{2,8},{3,12},{4,1},{5,5},{6,9},{7,13},{8,2},{9,6},{10,... | collective-permute-start | bytes 786440 | tf_op jit(solution)/shard_map/ppermute | solution.py:45
  8.2 2.3 %copy-start = (bf16[3,3,512,512]{3,2,1,0:T(8,128)(2,1)S(1)}, bf16[3,3,512,512]{3,2,1,0:T(8,128)(2,1)}, u32[]{:S(2)}) copy-start(bf16[3,3,512,512]{3,2,1,0:T(8,128)(2,1)} %source.1) | copy-start | bytes 14155780
  18.4 2.0 %collective-permute-start.4 = (bf16[128,512]{1,0:T(8,128)(2,1)S(1)}, bf16[128,512]{1,0:T(8,128)(2,1)S(1)}, u32[]{:S(2)}, u32[]{:S(2)}) collective-permute-start(bf16[128,512]{1,0:T(8,128)(2,1)S(1)} %get-tuple-element.31), channel_id=1, source_target_pairs={{0,1},{1,0},{2,3},{3,2},{4,5},{5,4},{6,7},{7,6},{8,9},{9,8},{10,11... | collective-permute-start | bytes 393224 | tf_op jit(solution)/shard_map/ppermute | solution.py:67
  18.5 1.9 %collective-permute-start.5 = (bf16[128,512]{1,0:T(8,128)(2,1)S(1)}, bf16[128,512]{1,0:T(8,128)(2,1)S(1)}, u32[]{:S(2)}, u32[]{:S(2)}) collective-permute-start(bf16[128,512]{1,0:T(8,128)(2,1)S(1)} %get-tuple-element.32), channel_id=1, source_target_pairs={{0,1},{1,0},{2,3},{3,2},{4,5},{5,4},{6,7},{7,6},{8,9},{9,8},{10,11... | collective-permute-start | bytes 393224 | tf_op jit(solution)/shard_map/ppermute | solution.py:67
  20.4 12.7 %collective-permute-start.14 = (bf16[2,64,512]{2,1,0:T(8,128)(2,1)S(1)}, bf16[2,64,512]{2,1,0:T(8,128)(2,1)S(1)}, u32[]{:S(2)}, u32[]{:S(2)}) collective-permute-start(bf16[2,64,512]{2,1,0:T(8,128)(2,1)S(1)} %get-tuple-element.33), channel_id=1, source_target_pairs={{0,2},{1,3},{2,0},{3,1},{4,6},{5,7},{6,4},{7,5},{8,10},{9,11},{10,... | collective-permute-start | bytes 393224 | tf_op jit(solution)/shard_map/ppermute | solution.py:67
  28.9 17.4 %slice-start = ((s8[4718592]{0:T(1024)(128)(4,1)}), s8[524288]{0:T(1024)(128)(4,1)S(1)}, s32[]{:S(2)}) async-start(s8[4718592]{0:T(1024)(128)(4,1)} %bitcast.2), calls=%async_computation | async-start | bytes 1048576
  30.5 2.5 %collective-permute-start.6 = (bf16[64,512]{1,0:T(8,128)(2,1)S(1)}, bf16[64,512]{1,0:T(8,128)(2,1)S(1)}, u32[]{:S(2)}, u32[]{:S(2)}) collective-permute-start(bf16[64,512]{1,0:T(8,128)(2,1)S(1)} %get-tuple-element.37), channel_id=1, source_target_pairs={{0,1},{1,0},{2,3},{3,2},{4,5},{5,4},{6,7},{7,6},{8,9},{9,8},{10,11... | collective-permute-start | bytes 196616 | tf_op jit(solution)/shard_map/ppermute | solution.py:67
  30.6 2.4 %collective-permute-start.7 = (bf16[64,512]{1,0:T(8,128)(2,1)S(1)}, bf16[64,512]{1,0:T(8,128)(2,1)S(1)}, u32[]{:S(2)}, u32[]{:S(2)}) collective-permute-start(bf16[64,512]{1,0:T(8,128)(2,1)S(1)} %get-tuple-element.38), channel_id=1, source_target_pairs={{0,1},{1,0},{2,3},{3,2},{4,5},{5,4},{6,7},{7,6},{8,9},{9,8},{10,11... | collective-permute-start | bytes 196616 | tf_op jit(solution)/shard_map/ppermute | solution.py:67
  31.1 1.9 %collective-permute-start.8 = (bf16[64,512]{1,0:T(8,128)(2,1)S(1)}, bf16[64,512]{1,0:T(8,128)(2,1)S(1)}, u32[]{:S(2)}, u32[]{:S(2)}) collective-permute-start(bf16[64,512]{1,0:T(8,128)(2,1)S(1)} %get-tuple-element.39), channel_id=1, source_target_pairs={{0,1},{1,0},{2,3},{3,2},{4,5},{5,4},{6,7},{7,6},{8,9},{9,8},{10,11... | collective-permute-start | bytes 196616 | tf_op jit(solution)/shard_map/ppermute | solution.py:67
  31.2 1.8 %collective-permute-start.9 = (bf16[64,512]{1,0:T(8,128)(2,1)S(1)}, bf16[64,512]{1,0:T(8,128)(2,1)S(1)}, u32[]{:S(2)}, u32[]{:S(2)}) collective-permute-start(bf16[64,512]{1,0:T(8,128)(2,1)S(1)} %get-tuple-element.40), channel_id=1, source_target_pairs={{0,1},{1,0},{2,3},{3,2},{4,5},{5,4},{6,7},{7,6},{8,9},{9,8},{10,11... | collective-permute-start | bytes 196616 | tf_op jit(solution)/shard_map/ppermute | solution.py:67
  31.6 14.8 %slice-start.1 = ((s8[4718592]{0:T(1024)(128)(4,1)}), s8[4194304]{0:T(1024)(128)(4,1)S(1)}, s32[]{:S(2)}) async-start(s8[4718592]{0:T(1024)(128)(4,1)} %bitcast.2), calls=%async_computation.1 | async-start | bytes 8388608
  33.2 1.6 %collective-permute-start.15 = (bf16[2,64,512]{2,1,0:T(8,128)(2,1)S(1)}, bf16[2,64,512]{2,1,0:T(8,128)(2,1)S(1)}, u32[]{:S(2)}, u32[]{:S(2)}) collective-permute-start(bf16[2,64,512]{2,1,0:T(8,128)(2,1)S(1)} %shard_map.46.own), channel_id=1, source_target_pairs={{0,1},{1,0},{2,3},{3,2},{4,5},{5,4},{6,7},{7,6},{8,9},{9,8},{10,11... | collective-permute-start | bytes 393224 | tf_op jit(solution)/shard_map/ppermute | solution.py:67
  33.3 5.8 %collective-permute-start.10 = (bf16[2,64,512]{2,1,0:T(8,128)(2,1)S(1)}, bf16[2,64,512]{2,1,0:T(8,128)(2,1)S(1)}, u32[]{:S(2)}, u32[]{:S(2)}) collective-permute-start(bf16[2,64,512]{2,1,0:T(8,128)(2,1)S(1)} %get-tuple-element.42), channel_id=1, source_target_pairs={{0,2},{1,3},{2,0},{3,1},{4,6},{5,7},{6,4},{7,5},{8,10},{9,11},{10,... | collective-permute-start | bytes 393224 | tf_op jit(solution)/shard_map/ppermute | solution.py:67
  34.9 11.5 %collective-permute-start.16 = (bf16[2,2,64,512]{3,2,1,0:T(8,128)(2,1)S(1)}, bf16[2,2,64,512]{3,2,1,0:T(8,128)(2,1)S(1)}, u32[]{:S(2)}, u32[]{:S(2)}) collective-permute-start(bf16[2,2,64,512]{3,2,1,0:T(8,128)(2,1)S(1)} %shard_map.47), channel_id=1, source_target_pairs={{0,0},{4,1},{8,2},{12,3},{2,4},{6,5},{10,6},{14,7},{1,8},{5,9},{9,... | collective-permute-start | bytes 786440 | tf_op jit(solution)/shard_map/ppermute | solution.py:58
  35.6 10.8 %collective-permute-start.17 = (bf16[2,2,64,512]{3,2,1,0:T(8,128)(2,1)S(1)}, bf16[2,2,64,512]{3,2,1,0:T(8,128)(2,1)S(1)}, u32[]{:S(2)}, u32[]{:S(2)}) collective-permute-start(bf16[2,2,64,512]{3,2,1,0:T(8,128)(2,1)S(1)} %shard_map.47), channel_id=1, source_target_pairs={{2,0},{6,1},{10,2},{14,3},{0,4},{4,5},{8,6},{12,7},{3,8},{7,9},{11... | collective-permute-start | bytes 786440 | tf_op jit(solution)/shard_map/ppermute | solution.py:58
  39.3 3.1 %collective-permute-start.11 = (bf16[2,64,512]{2,1,0:T(8,128)(2,1)S(1)}, bf16[2,64,512]{2,1,0:T(8,128)(2,1)S(1)}, u32[]{:S(2)}, u32[]{:S(2)}) collective-permute-start(bf16[2,64,512]{2,1,0:T(8,128)(2,1)S(1)} %shard_map.44.own), channel_id=1, source_target_pairs={{0,1},{1,0},{2,3},{3,2},{4,5},{5,4},{6,7},{7,6},{8,9},{9,8},{10,11... | collective-permute-start | bytes 393224 | tf_op jit(solution)/shard_map/ppermute | solution.py:67
  42.4 9.7 %collective-permute-start.12 = (bf16[2,2,64,512]{3,2,1,0:T(8,128)(2,1)S(1)}, bf16[2,2,64,512]{3,2,1,0:T(8,128)(2,1)S(1)}, u32[]{:S(2)}, u32[]{:S(2)}) collective-permute-start(bf16[2,2,64,512]{3,2,1,0:T(8,128)(2,1)S(1)} %shard_map.45), channel_id=1, source_target_pairs={{0,0},{4,1},{8,2},{12,3},{2,4},{6,5},{10,6},{14,7},{1,8},{5,9},{9,... | collective-permute-start | bytes 786440 | tf_op jit(solution)/shard_map/ppermute | solution.py:58
  43.1 20.9 %collective-permute-start.13 = (bf16[2,2,64,512]{3,2,1,0:T(8,128)(2,1)S(1)}, bf16[2,2,64,512]{3,2,1,0:T(8,128)(2,1)S(1)}, u32[]{:S(2)}, u32[]{:S(2)}) collective-permute-start(bf16[2,2,64,512]{3,2,1,0:T(8,128)(2,1)S(1)} %shard_map.45), channel_id=1, source_target_pairs={{2,0},{6,1},{10,2},{14,3},{0,4},{4,5},{8,6},{12,7},{3,8},{7,9},{11... | collective-permute-start | bytes 786440 | tf_op jit(solution)/shard_map/ppermute | solution.py:58
  47.9 4.3 %collective-permute-start.18 = (bf16[128,512]{1,0:T(8,128)(2,1)S(1)}, bf16[128,512]{1,0:T(8,128)(2,1)S(1)}, u32[]{:S(2)}, u32[]{:S(2)}) collective-permute-start(bf16[128,512]{1,0:T(8,128)(2,1)S(1)} %get-tuple-element.48), channel_id=1, source_target_pairs={{0,1},{1,0},{2,3},{3,2},{4,5},{5,4},{6,7},{7,6},{8,9},{9,8},{10,11... | collective-permute-start | bytes 393224 | tf_op jit(solution)/shard_map/ppermute | solution.py:67
  50.1 2.0 %collective-permute-start.19 = (bf16[128,512]{1,0:T(8,128)(2,1)S(1)}, bf16[128,512]{1,0:T(8,128)(2,1)S(1)}, u32[]{:S(2)}, u32[]{:S(2)}) collective-permute-start(bf16[128,512]{1,0:T(8,128)(2,1)S(1)} %get-tuple-element.49), channel_id=1, source_target_pairs={{0,1},{1,0},{2,3},{3,2},{4,5},{5,4},{6,7},{7,6},{8,9},{9,8},{10,11... | collective-permute-start | bytes 393224 | tf_op jit(solution)/shard_map/ppermute | solution.py:67
  51.6 15.2 %collective-permute-start.21 = (bf16[256,512]{1,0:T(8,128)(2,1)S(1)}, bf16[256,512]{1,0:T(8,128)(2,1)S(1)}, u32[]{:S(2)}, u32[]{:S(2)}) collective-permute-start(bf16[256,512]{1,0:T(8,128)(2,1)S(1)} %shard_map.48), channel_id=1, source_target_pairs={{0,1},{1,0},{2,3},{3,2},{4,5},{5,4},{6,7},{7,6},{8,9},{9,8},{10,11... | collective-permute-start | bytes 786440 | tf_op jit(solution)/shard_map/ppermute | solution.py:67
  53.0 13.8 %collective-permute-start.20 = (bf16[112,512]{1,0:T(8,128)(2,1)S(1)}, bf16[112,512]{1,0:T(8,128)(2,1)S(1)}, u32[]{:S(2)}, u32[]{:S(2)}) collective-permute-start(bf16[112,512]{1,0:T(8,128)(2,1)S(1)} %shard_map.50), channel_id=1, source_target_pairs={{0,2},{1,3},{2,0},{3,1},{4,6},{5,7},{6,4},{7,5},{8,10},{9,11},{10,... | collective-permute-start | bytes 344072 | tf_op jit(solution)/shard_map/ppermute | solution.py:67
  65.0 5.2 %collective-permute-start.22 = (bf16[144,512]{1,0:T(8,128)(2,1)S(1)}, bf16[144,512]{1,0:T(8,128)(2,1)S(1)}, u32[]{:S(2)}, u32[]{:S(2)}) collective-permute-start(bf16[144,512]{1,0:T(8,128)(2,1)S(1)} %shard_map.51), channel_id=1, source_target_pairs={{0,2},{1,3},{2,0},{3,1},{4,6},{5,7},{6,4},{7,5},{8,10},{9,11},{10,... | collective-permute-start | bytes 442376 | tf_op jit(solution)/shard_map/ppermute | solution.py:67

commit v7 on v6

--- a/solution.py
+++ b/solution.py
@@ -51,8 +51,9 @@
             moves = []
             for level in range(self.levels):
                 v, u = level // self.ratio, level % self.ratio
-                core, pair = v // self.pairs, (v + turn) % self.pairs
+                core = v // self.pairs
                 for col in range(self.cols):
+                    pair = (v + col + turn) % self.pairs
                     source = col * self.ratio + (u + e) % self.ratio
                     moves.append((source * self.cols + 2 * pair + core, level * self.cols + col))
             taken.append(lax.ppermute(x, ("chan", "img"), moves))
@@ -210,11 +211,11 @@
 
 def conv_two_body(plan, chosen, *refs):
     pieces, (kernel, out, wide) = refs[:-3], refs[-3:]
-    level = lax.axis_index("chan")
+    level, col = where_am_i()
     clear_edges(plan, wide)
     for n, piece in enumerate(pieces):
         turn, e = n // plan.ratio, n % plan.ratio
-        pair = (level // plan.ratio + turn) % plan.pairs
+        pair = (level // plan.ratio + col + turn) % plan.pairs
         for core in range(2):
             row_at = pl.multiple_of(plan.width + (2 * pair + core) * plan.share, 16)
             for f, at in enumerate(chosen):
@@ -251,7 +252,7 @@
     clear_edges(plan, wide)
     for n, piece in enumerate(pieces):
         turn, e = n // plan.ratio, n % plan.ratio
-        pair = (level // plan.ratio + turn) % plan.pairs
+        pair = (level // plan.ratio + col + turn) % plan.pairs
         for core in range(2):
             row_at = pl.multiple_of(plan.width + (2 * pair + core) * plan.share, 16)
             place(plan, piece[core, (col + first) % 2], 0, row_at, plan.lanes(level, e), wide)
@@ -294,7 +295,8 @@
 
 
 def part_of(plan, part):
-    first = lax.axis_index("chan") // plan.ratio % plan.pairs == 0
+    level, col = where_am_i()
+    first = (level // plan.ratio + col) % plan.pairs == 0
     size = plan.pixels // 2 - plan.width
     if part == 0:
         return jnp.where(first, 0, plan.pixels - size), size
@@ -310,7 +312,7 @@
     clear_edges(plan, wide)
     for n, piece in enumerate(pieces):
         turn, e = n // plan.ratio, n % plan.ratio
-        pair = (level // plan.ratio + turn) % plan.pairs
+        pair = (level // plan.ratio + col + turn) % plan.pairs
         for core in range(2):
             row_at = pl.multiple_of(plan.width + (2 * pair + core) * plan.share, 16)
             place(plan, piece[core, frame], 0, row_at, plan.lanes(level, e), wide)

time: 71.2 us -> 70.8 us (level)
  waiting for transfers between devices: 11.2 us -> 10.4 us
    ppermute x15, waiting for transfers between devices: 5.25 us -> 4.44 us  [swap(): return lax.ppermute(x, 'img', [(i, i ^ 1 << bit) for i in range(self.cols)])]
  transfers between devices with their start and end apart: 23 -> 23, of which waited for: 6 -> 5; matrix products, arithmetic and copies ran while one was open for 0% -> 0% of each run, Pallas kernels for 18% -> 18%
where the time goes in v7:
time: 70.8 us; the launch traced here: 70.6 us
  starting transfers between devices  44.2 us (62%)
  Pallas kernels  13.3 us (19%)
  waiting for transfers between devices  10.4 us (15%)
  local copies, waits for them, and re-layouts  2.34 us (3%)
    ppermute x15, starting transfers between devices, swap(): return lax.ppermute(x, 'img', [(i, i ^ 1 << bit) for i in range(self.cols)])  27.7 us
    pallas_call x16, Pallas kernels, call(): pl.pallas_call(body, in_specs=[VMEM] * len(inputs), out_specs=[VMEM] * le...  13 us
    ppermute x4, starting transfers between devices, spread(): taken.append(lax.ppermute(x, ('chan', 'img'), moves))  8.3 us
    ppermute x4, starting transfers between devices, spread_frame(): taken.append(lax.ppermute(x, ('chan', 'img'), moves))  8.17 us
    ppermute x4, waiting for transfers between devices, spread_frame(): taken.append(lax.ppermute(x, ('chan', 'img'), moves))  5.99 us
    ppermute x15, waiting for transfers between devices, swap(): return lax.ppermute(x, 'img', [(i, i ^ 1 << bit) for i in range(self.cols)])  4.44 us
    unnamed x6, local copies, waits for them, and re-layouts  2.34 us
  transfers between devices with their start and end apart: 23, of which 5 were waited for; matrix products, arithmetic and copies ran while one was open for 0% of the time, Pallas kernels for 18%

profile of v7, /device:TPU:0, one launch (start us, length us, event | category | flops | bytes accessed | tf_op | source)
XLA Modules:
  0.0 70.6 jit_solution(11504304548610525251)
XLA Ops:
  0.0 5.0 %collective-permute-start.2 = (bf16[256,512]{1,0:T(8,128)(2,1)}, bf16[256,512]{1,0:T(8,128)(2,1)S(1)}, u32[]{:S(2)}, u32[]{:S(2)}) collective-permute-start(bf16[256,512]{1,0:T(8,128)(2,1)} %bitcast.4), channel_id=1, source_target_pairs={{0,12},{1,0},{2,4},{3,8},{4,13},{5,1},{6,5},{7,9},{8,14},{9,2},{10... | collective-permute-start | bytes 786440 | tf_op jit(solution)/shard_map/ppermute | solution.py:45
  5.0 0.0 collective-permute-start.3
  5.1 1.5 %collective-permute-start = (bf16[256,512]{1,0:T(8,128)(2,1)}, bf16[256,512]{1,0:T(8,128)(2,1)S(1)}, u32[]{:S(2)}, u32[]{:S(2)}) collective-permute-start(bf16[256,512]{1,0:T(8,128)(2,1)} %bitcast.6), channel_id=1, source_target_pairs={{0,8},{1,12},{2,0},{3,4},{4,9},{5,13},{6,1},{7,5},{8,10},{9,14},{1... | collective-permute-start | bytes 786440 | tf_op jit(solution)/shard_map/ppermute | solution.py:45
  6.6 1.6 %collective-permute-start.1 = (bf16[256,512]{1,0:T(8,128)(2,1)}, bf16[256,512]{1,0:T(8,128)(2,1)S(1)}, u32[]{:S(2)}, u32[]{:S(2)}) collective-permute-start(bf16[256,512]{1,0:T(8,128)(2,1)} %bitcast.7), channel_id=1, source_target_pairs={{0,0},{1,4},{2,8},{3,12},{4,1},{5,5},{6,9},{7,13},{8,2},{9,6},{10,... | collective-permute-start | bytes 786440 | tf_op jit(solution)/shard_map/ppermute | solution.py:45
  8.2 2.3 %copy-done = bf16[3,3,512,512]{3,2,1,0:T(8,128)(2,1)S(1)} copy-done((bf16[3,3,512,512]{3,2,1,0:T(8,128)(2,1)S(1)}, bf16[3,3,512,512]{3,2,1,0:T(8,128)(2,1)}, u32[]{:S(2)}) %copy-start) | copy-done | bytes 4718616
  10.5 0.3 shard_map.37.refs_2_.kernel
  10.8 0.4 collective-permute-done.2.refs_0_
  11.2 5.6 %collective-permute-done.3.refs_1_ = bf16[256,512]{1,0:T(8,128)(2,1)S(1)} collective-permute-done((bf16[256,512]{1,0:T(8,128)(2,1)}, bf16[256,512]{1,0:T(8,128)(2,1)S(1)}, u32[]{:S(2)}, u32[]{:S(2)}) %collective-permute-start.3) | collective-permute-done | bytes 262176 | tf_op jit(solution)/shard_map/ppermute | solution.py:45
  16.8 1.6 %shard_map.38 = (bf16[128,512]{1,0:T(8,128)(2,1)S(1)}, bf16[128,512]{1,0:T(8,128)(2,1)S(1)}, bf16[2,288,1536]{2,1,0:T(8,128)(2,1)S(1)}) custom-call(bf16[256,512]{1,0:T(8,128)(2,1)S(1)} %collective-permute-done.2.refs_0_, bf16[256,512]{1,0:T(8,128)(2,1)S(1)} %collective-permute-done.3.refs_1_, bf16[3,3,512,512]{3,2,1,0:T(8,128)(2,1)S(1)} %shard_map.37.refs_2_.kernel), custom_call_target="tpu_custom_call" | custom-call | flops 1207959552 | bytes 5242880 | tf_op jit(solution)/shard_map/pallas_call | solution.py:72
  18.4 0.1 collective-permute-start.4
  18.5 0.5 collective-permute-start.5
  19.0 1.4 %shard_map.39.kept = f32[2,128,512]{2,1,0:T(8,128)S(1)} custom-call(bf16[2,288,1536]{2,1,0:T(8,128)(2,1)S(1)} %get-tuple-element.30.wide, bf16[3,3,512,512]{3,2,1,0:T(8,128)(2,1)S(1)} %shard_map.37.refs_2_.kernel), custom_call_target="tpu_custom_call" | custom-call | flops 1207959552 | bytes 6488064 | tf_op jit(solution)/shard_map/pallas_call | solution.py:72
  20.3 0.0 collective-permute-done.4.refs_0_
  20.3 0.0 collective-permute-done.5.refs_1_
  20.4 0.1 shard_map.40
  20.4 8.5 %collective-permute-start.14 = (bf16[2,64,512]{2,1,0:T(8,128)(2,1)S(1)}, bf16[2,64,512]{2,1,0:T(8,128)(2,1)S(1)}, u32[]{:S(2)}, u32[]{:S(2)}) collective-permute-start(bf16[2,64,512]{2,1,0:T(8,128)(2,1)S(1)} %get-tuple-element.33), channel_id=1, source_target_pairs={{0,2},{1,3},{2,0},{3,1},{4,6},{5,7},{6,4},{7,5},{8,10},{9,11},{10,... | collective-permute-start | bytes 393224 | tf_op jit(solution)/shard_map/ppermute | solution.py:68
  28.9 0.0 collective-permute-done.refs_0_
  28.9 0.0 collective-permute-done.1.refs_1_
  29.0 1.5 %shard_map.41 = (bf16[64,512]{1,0:T(8,128)(2,1)S(1)}, bf16[64,512]{1,0:T(8,128)(2,1)S(1)}, bf16[64,512]{1,0:T(8,128)(2,1)S(1)}, bf16[64,512]{1,0:T(8,128)(2,1)S(1)}, bf16[2,288,1536]{2,1,0:T(8,128)(2,1)S(1)}) custom-call(bf16[256,512]{1,0:T(8,128)(2,1)S(1)} %collective-permute-done.refs_0_, bf16[256,512]{1,0:T(8,128)(2,1)S(1)} %collective-permute-done.1.refs_1_, ...), custom_call_target="tpu_custom_call" | custom-call | flops 1207959552 | bytes 5242880 | tf_op jit(solution)/shard_map/pallas_call | solution.py:72
  30.5 0.1 collective-permute-start.6
  30.6 0.5 collective-permute-start.7
  31.1 0.1 collective-permute-start.8
  31.2 0.4 collective-permute-start.9
  31.6 1.4 %shard_map.42.kept = f32[2,128,512]{2,1,0:T(8,128)S(1)} custom-call(bf16[2,288,1536]{2,1,0:T(8,128)(2,1)S(1)} %get-tuple-element.36.wide, bf16[3,3,512,512]{3,2,1,0:T(8,128)(2,1)S(1)} %shard_map.37.refs_2_.kernel), custom_call_target="tpu_custom_call" | custom-call | flops 1207959552 | bytes 6488064 | tf_op jit(solution)/shard_map/pallas_call | solution.py:72
  33.0 0.0 collective-permute-done.6.refs_0_
  33.0 0.0 collective-permute-done.7.refs_1_
  33.0 0.0 collective-permute-done.8.refs_2_
  33.0 0.0 collective-permute-done.9.refs_3_
  33.0 0.1 shard_map.43
  33.1 0.0 collective-permute-done.14.came
  33.1 0.1 shard_map.46.own
  33.2 0.1 collective-permute-start.15
  33.3 1.5 %collective-permute-start.10 = (bf16[2,64,512]{2,1,0:T(8,128)(2,1)S(1)}, bf16[2,64,512]{2,1,0:T(8,128)(2,1)S(1)}, u32[]{:S(2)}, u32[]{:S(2)}) collective-permute-start(bf16[2,64,512]{2,1,0:T(8,128)(2,1)S(1)} %get-tuple-element.42), channel_id=1, source_target_pairs={{0,2},{1,3},{2,0},{3,1},{4,6},{5,7},{6,4},{7,5},{8,10},{9,11},{10,... | collective-permute-start | bytes 393224 | tf_op jit(solution)/shard_map/ppermute | solution.py:68
  34.8 0.0 collective-permute-done.15.came
  34.9 0.7 collective-permute-start.16
  35.6 3.7 %collective-permute-start.17 = (bf16[2,2,64,512]{3,2,1,0:T(8,128)(2,1)S(1)}, bf16[2,2,64,512]{3,2,1,0:T(8,128)(2,1)S(1)}, u32[]{:S(2)}, u32[]{:S(2)}) collective-permute-start(bf16[2,2,64,512]{3,2,1,0:T(8,128)(2,1)S(1)} %shard_map.47), channel_id=1, source_target_pairs={{2,0},{4,1},{10,2},{12,3},{0,4},{6,5},{8,6},{14,7},{3,8},{5,9},{11... | collective-permute-start | bytes 786440 | tf_op jit(solution)/shard_map/ppermute | solution.py:59
  39.2 0.0 collective-permute-done.10.came
  39.2 0.1 shard_map.44.own
  39.3 2.8 %collective-permute-start.11 = (bf16[2,64,512]{2,1,0:T(8,128)(2,1)S(1)}, bf16[2,64,512]{2,1,0:T(8,128)(2,1)S(1)}, u32[]{:S(2)}, u32[]{:S(2)}) collective-permute-start(bf16[2,64,512]{2,1,0:T(8,128)(2,1)S(1)} %shard_map.44.own), channel_id=1, source_target_pairs={{0,1},{1,0},{2,3},{3,2},{4,5},{5,4},{6,7},{7,6},{8,9},{9,8},{10,11... | collective-permute-start | bytes 393224 | tf_op jit(solution)/shard_map/ppermute | solution.py:68
  42.2 1.0 %collective-permute-done.11.came = bf16[2,64,512]{2,1,0:T(8,128)(2,1)S(1)} collective-permute-done((bf16[2,64,512]{2,1,0:T(8,128)(2,1)S(1)}, bf16[2,64,512]{2,1,0:T(8,128)(2,1)S(1)}, u32[]{:S(2)}, u32[]{:S(2)}) %collective-permute-start.11) | collective-permute-done | bytes 131104 | tf_op jit(solution)/shard_map/ppermute | solution.py:68
  43.2 0.7 collective-permute-start.12
  43.9 3.3 %collective-permute-start.13 = (bf16[2,2,64,512]{3,2,1,0:T(8,128)(2,1)S(1)}, bf16[2,2,64,512]{3,2,1,0:T(8,128)(2,1)S(1)}, u32[]{:S(2)}, u32[]{:S(2)}) collective-permute-start(bf16[2,2,64,512]{3,2,1,0:T(8,128)(2,1)S(1)} %shard_map.45), channel_id=1, source_target_pairs={{2,0},{4,1},{10,2},{12,3},{0,4},{6,5},{8,6},{14,7},{3,8},{5,9},{11... | collective-permute-start | bytes 786440 | tf_op jit(solution)/shard_map/ppermute | solution.py:59
  47.2 0.0 collective-permute-done.16.refs_0_
  47.2 0.0 collective-permute-done.17.refs_1_
  47.2 0.0 slice-done
  47.2 0.0 slice-done.1
  47.2 1.4 %shard_map.49 = (bf16[128,512]{1,0:T(8,128)(2,1)S(1)}, bf16[128,512]{1,0:T(8,128)(2,1)S(1)}) custom-call(bf16[2,2,64,512]{3,2,1,0:T(8,128)(2,1)S(1)} %collective-permute-done.16.refs_0_, bf16[2,2,64,512]{3,2,1,0:T(8,128)(2,1)S(1)} %collective-permute-done.17.refs_1_, bf16[3,3,512,512]{3,2,1,0:T(8,128)(2,1)S(1)} %bitcast.3), custom_call_target="tpu_custom_call" | custom-call | flops 1207959552 | bytes 5242880 | tf_op jit(solution)/shard_map/pallas_call | solution.py:72
  48.7 4.2 %collective-permute-start.18 = (bf16[128,512]{1,0:T(8,128)(2,1)S(1)}, bf16[128,512]{1,0:T(8,128)(2,1)S(1)}, u32[]{:S(2)}, u32[]{:S(2)}) collective-permute-start(bf16[128,512]{1,0:T(8,128)(2,1)S(1)} %get-tuple-element.48), channel_id=1, source_target_pairs={{0,1},{1,0},{2,3},{3,2},{4,5},{5,4},{6,7},{7,6},{8,9},{9,8},{10,11... | collective-permute-start | bytes 393224 | tf_op jit(solution)/shard_map/ppermute | solution.py:68
  52.9 0.1 collective-permute-start.19
  53.0 1.4 %shard_map.48 = bf16[256,512]{1,0:T(8,128)(2,1)S(1)} custom-call(bf16[2,2,64,512]{3,2,1,0:T(8,128)(2,1)S(1)} %collective-permute-done.16.refs_0_, bf16[2,2,64,512]{3,2,1,0:T(8,128)(2,1)S(1)} %collective-permute-done.17.refs_1_, bf16[3,3,512,512]{3,2,1,0:T(8,128)(2,1)S(1)} %bitcast.3), custom_call_target="tpu_custom_call" | custom-call | flops 1207959552 | bytes 5242880 | tf_op jit(solution)/shard_map/pallas_call | solution.py:72
  54.4 0.5 collective-permute-start.21
  54.9 0.0 collective-permute-done.12.refs_0_
  54.9 0.0 collective-permute-done.18.refs_2_.refs_3_
  54.9 0.0 collective-permute-done.19.refs_3_.refs_4_
  54.9 0.8 %shard_map.50 = bf16[112,512]{1,0:T(8,128)(2,1)S(1)} custom-call(bf16[2,2,64,512]{3,2,1,0:T(8,128)(2,1)S(1)} %collective-permute-done.12.refs_0_, bf16[3,3,512,512]{3,2,1,0:T(8,128)(2,1)S(1)} %bitcast.3, bf16[128,512]{1,0:T(8,128)(2,1)S(1)} %collective-permute-done.18.refs_2_.refs_3_, bf16[128,512]{1,0:T(8,128)(2,1)S(1)} %collective-permute-done.19.refs_3_.refs_4_), custom_call_target="tpu_custom_call" | custom-call | flops 528482304 | bytes 5242880 | tf_op jit(solution)/shard_map/pallas_call | solution.py:72
  55.7 7.8 %collective-permute-start.20 = (bf16[112,512]{1,0:T(8,128)(2,1)S(1)}, bf16[112,512]{1,0:T(8,128)(2,1)S(1)}, u32[]{:S(2)}, u32[]{:S(2)}) collective-permute-start(bf16[112,512]{1,0:T(8,128)(2,1)S(1)} %shard_map.50), channel_id=1, source_target_pairs={{0,2},{1,3},{2,0},{3,1},{4,6},{5,7},{6,4},{7,5},{8,10},{9,11},{10,... | collective-permute-start | bytes 344072 | tf_op jit(solution)/shard_map/ppermute | solution.py:68
  63.5 0.0 collective-permute-done.13.refs_1_
  63.5 1.0 %shard_map.51 = bf16[144,512]{1,0:T(8,128)(2,1)S(1)} custom-call(bf16[2,2,64,512]{3,2,1,0:T(8,128)(2,1)S(1)} %collective-permute-done.12.refs_0_, bf16[2,2,64,512]{3,2,1,0:T(8,128)(2,1)S(1)} %collective-permute-done.13.refs_1_, bf16[3,3,512,512]{3,2,1,0:T(8,128)(2,1)S(1)} %bitcast.3, bf16[128,512]{1,0:T(8,128)(2,1)S(1)} %collective-permute-done.18.refs_2_.refs_3_, ...), custom_call_target="tpu_custom_call" | custom-call | flops 679477248 | bytes 5505024 | tf_op jit(solution)/shard_map/pallas_call | solution.py:72
  64.5 0.5 collective-permute-start.22
  64.9 2.1 %collective-permute-done.20.refs_0_ = bf16[112,512]{1,0:T(8,128)(2,1)S(1)} collective-permute-done((bf16[112,512]{1,0:T(8,128)(2,1)S(1)}, bf16[112,512]{1,0:T(8,128)(2,1)S(1)}, u32[]{:S(2)}, u32[]{:S(2)}) %collective-permute-start.20) | collective-permute-done | bytes 114720 | tf_op jit(solution)/shard_map/ppermute | solution.py:68
  67.1 0.0 collective-permute-done.21.refs_3_
  67.1 1.4 %shard_map.52.kept = f32[256,512]{1,0:T(8,128)S(1)} custom-call(bf16[2,2,64,512]{3,2,1,0:T(8,128)(2,1)S(1)} %collective-permute-done.12.refs_0_, bf16[2,2,64,512]{3,2,1,0:T(8,128)(2,1)S(1)} %collective-permute-done.13.refs_1_, bf16[3,3,512,512]{3,2,1,0:T(8,128)(2,1)S(1)} %bitcast.3, bf16[256,512]{1,0:T(8,128)(2,1)S(1)} %collective-permute-done.21.refs_3_), custom_call_target="tpu_custom_call" | custom-call | flops 1207959552 | bytes 5505024 | tf_op jit(solution)/shard_map/pallas_call | solution.py:72
  68.5 1.3 %collective-permute-done.22.refs_1_ = bf16[144,512]{1,0:T(8,128)(2,1)S(1)} collective-permute-done((bf16[144,512]{1,0:T(8,128)(2,1)S(1)}, bf16[144,512]{1,0:T(8,128)(2,1)S(1)}, u32[]{:S(2)}, u32[]{:S(2)}) %collective-permute-start.22) | collective-permute-done | bytes 147488 | tf_op jit(solution)/shard_map/ppermute | solution.py:68
  69.8 0.8 %shard_map.53 = bf16[256,512]{1,0:T(8,128)(2,1)} custom-call(f32[256,512]{1,0:T(8,128)S(1)} %shard_map.52.kept, bf16[112,512]{1,0:T(8,128)(2,1)S(1)} %collective-permute-done.20.refs_0_, bf16[144,512]{1,0:T(8,128)(2,1)S(1)} %collective-permute-done.22.refs_1_), custom_call_target="tpu_custom_call" | custom-call | bytes 786432 | tf_op jit(solution)/shard_map/pallas_call | solution.py:72
  (6 shorter events, 0.1 us)
Async XLA Ops:
  0.0 11.2 %collective-permute-start.2 = (bf16[256,512]{1,0:T(8,128)(2,1)}, bf16[256,512]{1,0:T(8,128)(2,1)S(1)}, u32[]{:S(2)}, u32[]{:S(2)}) collective-permute-start(bf16[256,512]{1,0:T(8,128)(2,1)} %bitcast.4), channel_id=1, source_target_pairs={{0,12},{1,0},{2,4},{3,8},{4,13},{5,1},{6,5},{7,9},{8,14},{9,2},{10... | collective-permute-start | bytes 786440 | tf_op jit(solution)/shard_map/ppermute | solution.py:45
  5.0 11.8 %collective-permute-start.3 = (bf16[256,512]{1,0:T(8,128)(2,1)}, bf16[256,512]{1,0:T(8,128)(2,1)S(1)}, u32[]{:S(2)}, u32[]{:S(2)}) collective-permute-start(bf16[256,512]{1,0:T(8,128)(2,1)} %bitcast.5), channel_id=1, source_target_pairs={{0,4},{1,8},{2,12},{3,0},{4,5},{5,9},{6,13},{7,1},{8,6},{9,10},{10... | collective-permute-start | bytes 786440 | tf_op jit(solution)/shard_map/ppermute | solution.py:45
  5.1 23.9 %collective-permute-start = (bf16[256,512]{1,0:T(8,128)(2,1)}, bf16[256,512]{1,0:T(8,128)(2,1)S(1)}, u32[]{:S(2)}, u32[]{:S(2)}) collective-permute-start(bf16[256,512]{1,0:T(8,128)(2,1)} %bitcast.6), channel_id=1, source_target_pairs={{0,8},{1,12},{2,0},{3,4},{4,9},{5,13},{6,1},{7,5},{8,10},{9,14},{1... | collective-permute-start | bytes 786440 | tf_op jit(solution)/shard_map/ppermute | solution.py:45
  6.6 22.4 %collective-permute-start.1 = (bf16[256,512]{1,0:T(8,128)(2,1)}, bf16[256,512]{1,0:T(8,128)(2,1)S(1)}, u32[]{:S(2)}, u32[]{:S(2)}) collective-permute-start(bf16[256,512]{1,0:T(8,128)(2,1)} %bitcast.7), channel_id=1, source_target_pairs={{0,0},{1,4},{2,8},{3,12},{4,1},{5,5},{6,9},{7,13},{8,2},{9,6},{10,... | collective-permute-start | bytes 786440 | tf_op jit(solution)/shard_map/ppermute | solution.py:45
  8.2 2.3 %copy-start = (bf16[3,3,512,512]{3,2,1,0:T(8,128)(2,1)S(1)}, bf16[3,3,512,512]{3,2,1,0:T(8,128)(2,1)}, u32[]{:S(2)}) copy-start(bf16[3,3,512,512]{3,2,1,0:T(8,128)(2,1)} %source.1) | copy-start | bytes 14155780
  18.4 2.0 %collective-permute-start.4 = (bf16[128,512]{1,0:T(8,128)(2,1)S(1)}, bf16[128,512]{1,0:T(8,128)(2,1)S(1)}, u32[]{:S(2)}, u32[]{:S(2)}) collective-permute-start(bf16[128,512]{1,0:T(8,128)(2,1)S(1)} %get-tuple-element.31), channel_id=1, source_target_pairs={{0,1},{1,0},{2,3},{3,2},{4,5},{5,4},{6,7},{7,6},{8,9},{9,8},{10,11... | collective-permute-start | bytes 393224 | tf_op jit(solution)/shard_map/ppermute | solution.py:68
  18.5 1.9 %collective-permute-start.5 = (bf16[128,512]{1,0:T(8,128)(2,1)S(1)}, bf16[128,512]{1,0:T(8,128)(2,1)S(1)}, u32[]{:S(2)}, u32[]{:S(2)}) collective-permute-start(bf16[128,512]{1,0:T(8,128)(2,1)S(1)} %get-tuple-element.32), channel_id=1, source_target_pairs={{0,1},{1,0},{2,3},{3,2},{4,5},{5,4},{6,7},{7,6},{8,9},{9,8},{10,11... | collective-permute-start | bytes 393224 | tf_op jit(solution)/shard_map/ppermute | solution.py:68
  20.4 12.7 %collective-permute-start.14 = (bf16[2,64,512]{2,1,0:T(8,128)(2,1)S(1)}, bf16[2,64,512]{2,1,0:T(8,128)(2,1)S(1)}, u32[]{:S(2)}, u32[]{:S(2)}) collective-permute-start(bf16[2,64,512]{2,1,0:T(8,128)(2,1)S(1)} %get-tuple-element.33), channel_id=1, source_target_pairs={{0,2},{1,3},{2,0},{3,1},{4,6},{5,7},{6,4},{7,5},{8,10},{9,11},{10,... | collective-permute-start | bytes 393224 | tf_op jit(solution)/shard_map/ppermute | solution.py:68
  28.9 18.2 %slice-start = ((s8[4718592]{0:T(1024)(128)(4,1)}), s8[524288]{0:T(1024)(128)(4,1)S(1)}, s32[]{:S(2)}) async-start(s8[4718592]{0:T(1024)(128)(4,1)} %bitcast.2), calls=%async_computation | async-start | bytes 1048576
  30.5 2.5 %collective-permute-start.6 = (bf16[64,512]{1,0:T(8,128)(2,1)S(1)}, bf16[64,512]{1,0:T(8,128)(2,1)S(1)}, u32[]{:S(2)}, u32[]{:S(2)}) collective-permute-start(bf16[64,512]{1,0:T(8,128)(2,1)S(1)} %get-tuple-element.37), channel_id=1, source_target_pairs={{0,1},{1,0},{2,3},{3,2},{4,5},{5,4},{6,7},{7,6},{8,9},{9,8},{10,11... | collective-permute-start | bytes 196616 | tf_op jit(solution)/shard_map/ppermute | solution.py:68
  30.6 2.4 %collective-permute-start.7 = (bf16[64,512]{1,0:T(8,128)(2,1)S(1)}, bf16[64,512]{1,0:T(8,128)(2,1)S(1)}, u32[]{:S(2)}, u32[]{:S(2)}) collective-permute-start(bf16[64,512]{1,0:T(8,128)(2,1)S(1)} %get-tuple-element.38), channel_id=1, source_target_pairs={{0,1},{1,0},{2,3},{3,2},{4,5},{5,4},{6,7},{7,6},{8,9},{9,8},{10,11... | collective-permute-start | bytes 196616 | tf_op jit(solution)/shard_map/ppermute | solution.py:68
  31.1 1.9 %collective-permute-start.8 = (bf16[64,512]{1,0:T(8,128)(2,1)S(1)}, bf16[64,512]{1,0:T(8,128)(2,1)S(1)}, u32[]{:S(2)}, u32[]{:S(2)}) collective-permute-start(bf16[64,512]{1,0:T(8,128)(2,1)S(1)} %get-tuple-element.39), channel_id=1, source_target_pairs={{0,1},{1,0},{2,3},{3,2},{4,5},{5,4},{6,7},{7,6},{8,9},{9,8},{10,11... | collective-permute-start | bytes 196616 | tf_op jit(solution)/shard_map/ppermute | solution.py:68
  31.2 1.8 %collective-permute-start.9 = (bf16[64,512]{1,0:T(8,128)(2,1)S(1)}, bf16[64,512]{1,0:T(8,128)(2,1)S(1)}, u32[]{:S(2)}, u32[]{:S(2)}) collective-permute-start(bf16[64,512]{1,0:T(8,128)(2,1)S(1)} %get-tuple-element.40), channel_id=1, source_target_pairs={{0,1},{1,0},{2,3},{3,2},{4,5},{5,4},{6,7},{7,6},{8,9},{9,8},{10,11... | collective-permute-start | bytes 196616 | tf_op jit(solution)/shard_map/ppermute | solution.py:68
  31.6 15.6 %slice-start.1 = ((s8[4718592]{0:T(1024)(128)(4,1)}), s8[4194304]{0:T(1024)(128)(4,1)S(1)}, s32[]{:S(2)}) async-start(s8[4718592]{0:T(1024)(128)(4,1)} %bitcast.2), calls=%async_computation.1 | async-start | bytes 8388608
  33.2 1.6 %collective-permute-start.15 = (bf16[2,64,512]{2,1,0:T(8,128)(2,1)S(1)}, bf16[2,64,512]{2,1,0:T(8,128)(2,1)S(1)}, u32[]{:S(2)}, u32[]{:S(2)}) collective-permute-start(bf16[2,64,512]{2,1,0:T(8,128)(2,1)S(1)} %shard_map.46.own), channel_id=1, source_target_pairs={{0,1},{1,0},{2,3},{3,2},{4,5},{5,4},{6,7},{7,6},{8,9},{9,8},{10,11... | collective-permute-start | bytes 393224 | tf_op jit(solution)/shard_map/ppermute | solution.py:68
  33.3 5.9 %collective-permute-start.10 = (bf16[2,64,512]{2,1,0:T(8,128)(2,1)S(1)}, bf16[2,64,512]{2,1,0:T(8,128)(2,1)S(1)}, u32[]{:S(2)}, u32[]{:S(2)}) collective-permute-start(bf16[2,64,512]{2,1,0:T(8,128)(2,1)S(1)} %get-tuple-element.42), channel_id=1, source_target_pairs={{0,2},{1,3},{2,0},{3,1},{4,6},{5,7},{6,4},{7,5},{8,10},{9,11},{10,... | collective-permute-start | bytes 393224 | tf_op jit(solution)/shard_map/ppermute | solution.py:68
  34.9 12.3 %collective-permute-start.16 = (bf16[2,2,64,512]{3,2,1,0:T(8,128)(2,1)S(1)}, bf16[2,2,64,512]{3,2,1,0:T(8,128)(2,1)S(1)}, u32[]{:S(2)}, u32[]{:S(2)}) collective-permute-start(bf16[2,2,64,512]{3,2,1,0:T(8,128)(2,1)S(1)} %shard_map.47), channel_id=1, source_target_pairs={{0,0},{6,1},{8,2},{14,3},{2,4},{4,5},{10,6},{12,7},{1,8},{7,9},{9,... | collective-permute-start | bytes 786440 | tf_op jit(solution)/shard_map/ppermute | solution.py:59
  35.6 11.6 %collective-permute-start.17 = (bf16[2,2,64,512]{3,2,1,0:T(8,128)(2,1)S(1)}, bf16[2,2,64,512]{3,2,1,0:T(8,128)(2,1)S(1)}, u32[]{:S(2)}, u32[]{:S(2)}) collective-permute-start(bf16[2,2,64,512]{3,2,1,0:T(8,128)(2,1)S(1)} %shard_map.47), channel_id=1, source_target_pairs={{2,0},{4,1},{10,2},{12,3},{0,4},{6,5},{8,6},{14,7},{3,8},{5,9},{11... | collective-permute-start | bytes 786440 | tf_op jit(solution)/shard_map/ppermute | solution.py:59
  39.3 3.8 %collective-permute-start.11 = (bf16[2,64,512]{2,1,0:T(8,128)(2,1)S(1)}, bf16[2,64,512]{2,1,0:T(8,128)(2,1)S(1)}, u32[]{:S(2)}, u32[]{:S(2)}) collective-permute-start(bf16[2,64,512]{2,1,0:T(8,128)(2,1)S(1)} %shard_map.44.own), channel_id=1, source_target_pairs={{0,1},{1,0},{2,3},{3,2},{4,5},{5,4},{6,7},{7,6},{8,9},{9,8},{10,11... | collective-permute-start | bytes 393224 | tf_op jit(solution)/shard_map/ppermute | solution.py:68
  43.2 11.7 %collective-permute-start.12 = (bf16[2,2,64,512]{3,2,1,0:T(8,128)(2,1)S(1)}, bf16[2,2,64,512]{3,2,1,0:T(8,128)(2,1)S(1)}, u32[]{:S(2)}, u32[]{:S(2)}) collective-permute-start(bf16[2,2,64,512]{3,2,1,0:T(8,128)(2,1)S(1)} %shard_map.45), channel_id=1, source_target_pairs={{0,0},{6,1},{8,2},{14,3},{2,4},{4,5},{10,6},{12,7},{1,8},{7,9},{9,... | collective-permute-start | bytes 786440 | tf_op jit(solution)/shard_map/ppermute | solution.py:59
  43.9 19.7 %collective-permute-start.13 = (bf16[2,2,64,512]{3,2,1,0:T(8,128)(2,1)S(1)}, bf16[2,2,64,512]{3,2,1,0:T(8,128)(2,1)S(1)}, u32[]{:S(2)}, u32[]{:S(2)}) collective-permute-start(bf16[2,2,64,512]{3,2,1,0:T(8,128)(2,1)S(1)} %shard_map.45), channel_id=1, source_target_pairs={{2,0},{4,1},{10,2},{12,3},{0,4},{6,5},{8,6},{14,7},{3,8},{5,9},{11... | collective-permute-start | bytes 786440 | tf_op jit(solution)/shard_map/ppermute | solution.py:59
  48.7 6.3 %collective-permute-start.18 = (bf16[128,512]{1,0:T(8,128)(2,1)S(1)}, bf16[128,512]{1,0:T(8,128)(2,1)S(1)}, u32[]{:S(2)}, u32[]{:S(2)}) collective-permute-start(bf16[128,512]{1,0:T(8,128)(2,1)S(1)} %get-tuple-element.48), channel_id=1, source_target_pairs={{0,1},{1,0},{2,3},{3,2},{4,5},{5,4},{6,7},{7,6},{8,9},{9,8},{10,11... | collective-permute-start | bytes 393224 | tf_op jit(solution)/shard_map/ppermute | solution.py:68
  52.9 2.0 %collective-permute-start.19 = (bf16[128,512]{1,0:T(8,128)(2,1)S(1)}, bf16[128,512]{1,0:T(8,128)(2,1)S(1)}, u32[]{:S(2)}, u32[]{:S(2)}) collective-permute-start(bf16[128,512]{1,0:T(8,128)(2,1)S(1)} %get-tuple-element.49), channel_id=1, source_target_pairs={{0,1},{1,0},{2,3},{3,2},{4,5},{5,4},{6,7},{7,6},{8,9},{9,8},{10,11... | collective-permute-start | bytes 393224 | tf_op jit(solution)/shard_map/ppermute | solution.py:68
  54.4 12.7 %collective-permute-start.21 = (bf16[256,512]{1,0:T(8,128)(2,1)S(1)}, bf16[256,512]{1,0:T(8,128)(2,1)S(1)}, u32[]{:S(2)}, u32[]{:S(2)}) collective-permute-start(bf16[256,512]{1,0:T(8,128)(2,1)S(1)} %shard_map.48), channel_id=1, source_target_pairs={{0,1},{1,0},{2,3},{3,2},{4,5},{5,4},{6,7},{7,6},{8,9},{9,8},{10,11... | collective-permute-start | bytes 786440 | tf_op jit(solution)/shard_map/ppermute | solution.py:68
  55.7 11.4 %collective-permute-start.20 = (bf16[112,512]{1,0:T(8,128)(2,1)S(1)}, bf16[112,512]{1,0:T(8,128)(2,1)S(1)}, u32[]{:S(2)}, u32[]{:S(2)}) collective-permute-start(bf16[112,512]{1,0:T(8,128)(2,1)S(1)} %shard_map.50), channel_id=1, source_target_pairs={{0,2},{1,3},{2,0},{3,1},{4,6},{5,7},{6,4},{7,5},{8,10},{9,11},{10,... | collective-permute-start | bytes 344072 | tf_op jit(solution)/shard_map/ppermute | solution.py:68
  64.5 5.3 %collective-permute-start.22 = (bf16[144,512]{1,0:T(8,128)(2,1)S(1)}, bf16[144,512]{1,0:T(8,128)(2,1)S(1)}, u32[]{:S(2)}, u32[]{:S(2)}) collective-permute-start(bf16[144,512]{1,0:T(8,128)(2,1)S(1)} %shard_map.51), channel_id=1, source_target_pairs={{0,2},{1,3},{2,0},{3,1},{4,6},{5,7},{6,4},{7,5},{8,10},{9,11},{10,... | collective-permute-start | bytes 442376 | tf_op jit(solution)/shard_map/ppermute | solution.py:68

commit v8 on v7

--- a/solution.py
+++ b/solution.py
@@ -45,7 +45,10 @@
             taken.append(lax.ppermute(x, ("chan", "img"), moves))
         return taken
 
-    def spread(self, x, turn):
+    def pair_of(self, half, level, col, turn):
+        return (level // self.ratio + turn + (col if half else 1)) % self.pairs
+
+    def spread(self, x, half, turn):
         taken = []
         for e in range(self.ratio):
             moves = []
@@ -53,7 +56,7 @@
                 v, u = level // self.ratio, level % self.ratio
                 core = v // self.pairs
                 for col in range(self.cols):
-                    pair = (v + col + turn) % self.pairs
+                    pair = self.pair_of(half, level, col, turn)
                     source = col * self.ratio + (u + e) % self.ratio
                     moves.append((source * self.cols + 2 * pair + core, level * self.cols + col))
             taken.append(lax.ppermute(x, ("chan", "img"), moves))
@@ -209,13 +212,13 @@
     return plan.call(silu_body, [keep, came], [(keep.shape, BF16)])[0]
 
 
-def conv_two_body(plan, chosen, *refs):
+def conv_two_body(plan, half, chosen, *refs):
     pieces, (kernel, out, wide) = refs[:-3], refs[-3:]
     level, col = where_am_i()
     clear_edges(plan, wide)
     for n, piece in enumerate(pieces):
         turn, e = n // plan.ratio, n % plan.ratio
-        pair = (level // plan.ratio + col + turn) % plan.pairs
+        pair = plan.pair_of(half, level, col, turn)
         for core in range(2):
             row_at = pl.multiple_of(plan.width + (2 * pair + core) * plan.share, 16)
             for f, at in enumerate(chosen):
@@ -224,10 +227,10 @@
     out[...] = times(plan, rows, kernel).astype(out.dtype).reshape(out.shape)
 
 
-def conv_two(plan, pieces, chosen, kernel, dtype):
+def conv_two(plan, half, pieces, chosen, kernel, dtype):
     frames = len(chosen)
     return plan.call(
-        functools.partial(conv_two_body, plan, chosen),
+        functools.partial(conv_two_body, plan, half, chosen),
         [*pieces, kernel],
         [((frames, plan.pixels, plan.c_out), dtype)],
         18 * frames * plan.pixels * plan.c_in * plan.c_out,
@@ -252,7 +255,7 @@
     clear_edges(plan, wide)
     for n, piece in enumerate(pieces):
         turn, e = n // plan.ratio, n % plan.ratio
-        pair = (level // plan.ratio + col + turn) % plan.pairs
+        pair = plan.pair_of(0, level, col, turn)
         for core in range(2):
             row_at = pl.multiple_of(plan.width + (2 * pair + core) * plan.share, 16)
             place(plan, piece[core, (col + first) % 2], 0, row_at, plan.lanes(level, e), wide)
@@ -296,7 +299,7 @@
 
 def part_of(plan, part):
     level, col = where_am_i()
-    first = (level // plan.ratio + col) % plan.pairs == 0
+    first = plan.pair_of(1, level, col, 0) == 0
     size = plan.pixels // 2 - plan.width
     if part == 0:
         return jnp.where(first, 0, plan.pixels - size), size
@@ -312,7 +315,7 @@
     clear_edges(plan, wide)
     for n, piece in enumerate(pieces):
         turn, e = n // plan.ratio, n % plan.ratio
-        pair = (level // plan.ratio + col + turn) % plan.pairs
+        pair = plan.pair_of(1, level, col, turn)
         for core in range(2):
             row_at = pl.multiple_of(plan.width + (2 * pair + core) * plan.share, 16)
             place(plan, piece[core, frame], 0, row_at, plan.lanes(level, e), wide)
@@ -347,11 +350,11 @@
     odds = after(odds, hidden)
     frames = len(odds[0][0])
     if plan.pairs != 2:
-        sums = conv_two(plan, odds, range(frames), kernel, BF16)
+        sums = conv_two(plan, 0, odds, range(frames), kernel, BF16)
         came = plan.swap(after(sums, evens), 0)
-        here = conv_two(plan, evens, range(frames // 2), kernel, F32)
+        here = conv_two(plan, 1, evens, range(frames // 2), kernel, F32)
         send = merge(plan, 0, here, came, range(1, frames, 2), BF16)
-        here = conv_two(plan, evens, range(frames // 2, frames), kernel, F32)
+        here = conv_two(plan, 1, evens, range(frames // 2, frames), kernel, F32)
         return sum_rest(plan, here, came, send)
     cames = [plan.swap(part, 0) for part in conv_for_other(plan, odds, 1, kernel, 2)]
     own = conv_for_other(plan, odds, 0, kernel, 1)[0]
@@ -379,9 +382,9 @@
     kept, cames = conv_one_in_two(plan, after(late, ahead), kernel_one, 2)
     kept, behind = sum_one(plan, kept, cames)
     hidden = join(plan, add_silu(plan, keep, after(plan.swap(ahead, last), behind)))
-    odds = [p for t in range(plan.pairs) for p in plan.spread(hidden, t)]
+    odds = [p for t in range(plan.pairs) for p in plan.spread(hidden, 0, t)]
     hidden = join(plan, add_silu(plan, kept, plan.swap(behind, last)))
-    evens = [p for t in range(plan.pairs) for p in plan.spread(hidden, t)]
+    evens = [p for t in range(plan.pairs) for p in plan.spread(hidden, 1, t)]
     return sum_in_parts(plan, odds, evens, hidden, kernel_two).reshape(features.shape)
 
 

time: 70.8 us -> 69.1 us (0.976)
  starting transfers between devices: 44.2 us -> 40.3 us
  waiting for transfers between devices: 10.4 us -> 12.7 us
    ppermute x15, starting transfers between devices: 27.7 us -> 25.1 us  [swap(): return lax.ppermute(x, 'img', [(i, i ^ 1 << bit) for i in range(self.cols)])]
    ppermute x15, waiting for transfers between devices: 4.44 us -> 6.69 us  [swap(): return lax.ppermute(x, 'img', [(i, i ^ 1 << bit) for i in range(self.cols)])]
    ppermute x4, starting transfers between devices: 8.3 us -> 7.03 us  [spread(): taken.append(lax.ppermute(x, ('chan', 'img'), moves))]
  transfers between devices with their start and end apart: 23 -> 23, of which waited for: 5 -> 6; matrix products, arithmetic and copies ran while one was open for 0% -> 0% of each run, Pallas kernels for 18% -> 18%
where the time goes in v8:
time: 69.1 us; the launch traced here: 68.9 us
  starting transfers between devices  40.3 us (58%)
  Pallas kernels  13.3 us (19%)
  waiting for transfers between devices  12.7 us (18%)
  local copies, waits for them, and re-layouts  2.34 us (3%)
    ppermute x15, starting transfers between devices, swap(): return lax.ppermute(x, 'img', [(i, i ^ 1 << bit) for i in range(self.cols)])  25.1 us
    pallas_call x16, Pallas kernels, call(): pl.pallas_call(body, in_specs=[VMEM] * len(inputs), out_specs=[VMEM] * le...  13 us
    ppermute x4, starting transfers between devices, spread_frame(): taken.append(lax.ppermute(x, ('chan', 'img'), moves))  8.17 us
    ppermute x4, starting transfers between devices, spread(): taken.append(lax.ppermute(x, ('chan', 'img'), moves))  7.03 us
    ppermute x15, waiting for transfers between devices, swap(): return lax.ppermute(x, 'img', [(i, i ^ 1 << bit) for i in range(self.cols)])  6.69 us
    ppermute x4, waiting for transfers between devices, spread_frame(): taken.append(lax.ppermute(x, ('chan', 'img'), moves))  5.99 us
    unnamed x6, local copies, waits for them, and re-layouts  2.34 us
  transfers between devices with their start and end apart: 23, of which 6 were waited for; matrix products, arithmetic and copies ran while one was open for 0% of the time, Pallas kernels for 18%

profile of v8, /device:TPU:0, one launch (start us, length us, event | category | flops | bytes accessed | tf_op | source)
XLA Modules:
  0.0 68.9 jit_solution(13871483895773072472)
XLA Ops:
  0.0 5.0 %collective-permute-start.2 = (bf16[256,512]{1,0:T(8,128)(2,1)}, bf16[256,512]{1,0:T(8,128)(2,1)S(1)}, u32[]{:S(2)}, u32[]{:S(2)}) collective-permute-start(bf16[256,512]{1,0:T(8,128)(2,1)} %bitcast.4), channel_id=1, source_target_pairs={{0,12},{1,0},{2,4},{3,8},{4,13},{5,1},{6,5},{7,9},{8,14},{9,2},{10... | collective-permute-start | bytes 786440 | tf_op jit(solution)/shard_map/ppermute | solution.py:45
  5.0 0.0 collective-permute-start.3
  5.1 1.5 %collective-permute-start = (bf16[256,512]{1,0:T(8,128)(2,1)}, bf16[256,512]{1,0:T(8,128)(2,1)S(1)}, u32[]{:S(2)}, u32[]{:S(2)}) collective-permute-start(bf16[256,512]{1,0:T(8,128)(2,1)} %bitcast.6), channel_id=1, source_target_pairs={{0,8},{1,12},{2,0},{3,4},{4,9},{5,13},{6,1},{7,5},{8,10},{9,14},{1... | collective-permute-start | bytes 786440 | tf_op jit(solution)/shard_map/ppermute | solution.py:45
  6.6 1.6 %collective-permute-start.1 = (bf16[256,512]{1,0:T(8,128)(2,1)}, bf16[256,512]{1,0:T(8,128)(2,1)S(1)}, u32[]{:S(2)}, u32[]{:S(2)}) collective-permute-start(bf16[256,512]{1,0:T(8,128)(2,1)} %bitcast.7), channel_id=1, source_target_pairs={{0,0},{1,4},{2,8},{3,12},{4,1},{5,5},{6,9},{7,13},{8,2},{9,6},{10,... | collective-permute-start | bytes 786440 | tf_op jit(solution)/shard_map/ppermute | solution.py:45
  8.2 2.3 %copy-done = bf16[3,3,512,512]{3,2,1,0:T(8,128)(2,1)S(1)} copy-done((bf16[3,3,512,512]{3,2,1,0:T(8,128)(2,1)S(1)}, bf16[3,3,512,512]{3,2,1,0:T(8,128)(2,1)}, u32[]{:S(2)}) %copy-start) | copy-done | bytes 4718616
  10.5 0.3 shard_map.37.refs_2_.kernel
  10.8 0.4 collective-permute-done.2.refs_0_
  11.2 5.6 %collective-permute-done.3.refs_1_ = bf16[256,512]{1,0:T(8,128)(2,1)S(1)} collective-permute-done((bf16[256,512]{1,0:T(8,128)(2,1)}, bf16[256,512]{1,0:T(8,128)(2,1)S(1)}, u32[]{:S(2)}, u32[]{:S(2)}) %collective-permute-start.3) | collective-permute-done | bytes 262176 | tf_op jit(solution)/shard_map/ppermute | solution.py:45
  16.8 1.6 %shard_map.38 = (bf16[128,512]{1,0:T(8,128)(2,1)S(1)}, bf16[128,512]{1,0:T(8,128)(2,1)S(1)}, bf16[2,288,1536]{2,1,0:T(8,128)(2,1)S(1)}) custom-call(bf16[256,512]{1,0:T(8,128)(2,1)S(1)} %collective-permute-done.2.refs_0_, bf16[256,512]{1,0:T(8,128)(2,1)S(1)} %collective-permute-done.3.refs_1_, bf16[3,3,512,512]{3,2,1,0:T(8,128)(2,1)S(1)} %shard_map.37.refs_2_.kernel), custom_call_target="tpu_custom_call" | custom-call | flops 1207959552 | bytes 5242880 | tf_op jit(solution)/shard_map/pallas_call | solution.py:75
  18.4 0.1 collective-permute-start.4
  18.5 0.5 collective-permute-start.5
  19.0 1.4 %shard_map.39.kept = f32[2,128,512]{2,1,0:T(8,128)S(1)} custom-call(bf16[2,288,1536]{2,1,0:T(8,128)(2,1)S(1)} %get-tuple-element.30.wide, bf16[3,3,512,512]{3,2,1,0:T(8,128)(2,1)S(1)} %shard_map.37.refs_2_.kernel), custom_call_target="tpu_custom_call" | custom-call | flops 1207959552 | bytes 6488064 | tf_op jit(solution)/shard_map/pallas_call | solution.py:75
  20.3 0.0 collective-permute-done.4.refs_0_
  20.3 0.0 collective-permute-done.5.refs_1_
  20.4 0.1 shard_map.40
  20.4 8.5 %collective-permute-start.14 = (bf16[2,64,512]{2,1,0:T(8,128)(2,1)S(1)}, bf16[2,64,512]{2,1,0:T(8,128)(2,1)S(1)}, u32[]{:S(2)}, u32[]{:S(2)}) collective-permute-start(bf16[2,64,512]{2,1,0:T(8,128)(2,1)S(1)} %get-tuple-element.33), channel_id=1, source_target_pairs={{0,2},{1,3},{2,0},{3,1},{4,6},{5,7},{6,4},{7,5},{8,10},{9,11},{10,... | collective-permute-start | bytes 393224 | tf_op jit(solution)/shard_map/ppermute | solution.py:71
  28.9 0.0 collective-permute-done.refs_0_
  28.9 0.0 collective-permute-done.1.refs_1_
  29.0 1.5 %shard_map.41 = (bf16[64,512]{1,0:T(8,128)(2,1)S(1)}, bf16[64,512]{1,0:T(8,128)(2,1)S(1)}, bf16[64,512]{1,0:T(8,128)(2,1)S(1)}, bf16[64,512]{1,0:T(8,128)(2,1)S(1)}, bf16[2,288,1536]{2,1,0:T(8,128)(2,1)S(1)}) custom-call(bf16[256,512]{1,0:T(8,128)(2,1)S(1)} %collective-permute-done.refs_0_, bf16[256,512]{1,0:T(8,128)(2,1)S(1)} %collective-permute-done.1.refs_1_, ...), custom_call_target="tpu_custom_call" | custom-call | flops 1207959552 | bytes 5242880 | tf_op jit(solution)/shard_map/pallas_call | solution.py:75
  30.5 0.1 collective-permute-start.6
  30.6 0.5 collective-permute-start.7
  31.1 0.1 collective-permute-start.8
  31.2 0.4 collective-permute-start.9
  31.6 1.4 %shard_map.42.kept = f32[2,128,512]{2,1,0:T(8,128)S(1)} custom-call(bf16[2,288,1536]{2,1,0:T(8,128)(2,1)S(1)} %get-tuple-element.36.wide, bf16[3,3,512,512]{3,2,1,0:T(8,128)(2,1)S(1)} %shard_map.37.refs_2_.kernel), custom_call_target="tpu_custom_call" | custom-call | flops 1207959552 | bytes 6488064 | tf_op jit(solution)/shard_map/pallas_call | solution.py:75
  33.0 0.0 collective-permute-done.6.refs_0_
  33.0 0.0 collective-permute-done.7.refs_1_
  33.0 0.0 collective-permute-done.8.refs_2_
  33.0 0.0 collective-permute-done.9.refs_3_
  33.0 0.1 shard_map.43
  33.1 0.0 collective-permute-done.14.came
  33.1 0.1 shard_map.46.own
  33.2 0.1 collective-permute-start.15
  33.3 1.5 %collective-permute-start.10 = (bf16[2,64,512]{2,1,0:T(8,128)(2,1)S(1)}, bf16[2,64,512]{2,1,0:T(8,128)(2,1)S(1)}, u32[]{:S(2)}, u32[]{:S(2)}) collective-permute-start(bf16[2,64,512]{2,1,0:T(8,128)(2,1)S(1)} %get-tuple-element.42), channel_id=1, source_target_pairs={{0,2},{1,3},{2,0},{3,1},{4,6},{5,7},{6,4},{7,5},{8,10},{9,11},{10,... | collective-permute-start | bytes 393224 | tf_op jit(solution)/shard_map/ppermute | solution.py:71
  34.8 0.0 collective-permute-done.15.came
  34.9 0.4 collective-permute-start.16
  35.3 0.7 collective-permute-start.17
  36.0 3.2 %collective-permute-done.10.came = bf16[2,64,512]{2,1,0:T(8,128)(2,1)S(1)} collective-permute-done((bf16[2,64,512]{2,1,0:T(8,128)(2,1)S(1)}, bf16[2,64,512]{2,1,0:T(8,128)(2,1)S(1)}, u32[]{:S(2)}, u32[]{:S(2)}) %collective-permute-start.10) | collective-permute-done | bytes 131104 | tf_op jit(solution)/shard_map/ppermute | solution.py:71
  39.2 0.1 shard_map.44.own
  39.3 0.5 collective-permute-start.11
  39.8 1.0 %collective-permute-done.11.came = bf16[2,64,512]{2,1,0:T(8,128)(2,1)S(1)} collective-permute-done((bf16[2,64,512]{2,1,0:T(8,128)(2,1)S(1)}, bf16[2,64,512]{2,1,0:T(8,128)(2,1)S(1)}, u32[]{:S(2)}, u32[]{:S(2)}) %collective-permute-start.11) | collective-permute-done | bytes 131104 | tf_op jit(solution)/shard_map/ppermute | solution.py:71
  40.8 0.7 collective-permute-start.12
  41.5 5.3 %collective-permute-start.13 = (bf16[2,2,64,512]{3,2,1,0:T(8,128)(2,1)S(1)}, bf16[2,2,64,512]{3,2,1,0:T(8,128)(2,1)S(1)}, u32[]{:S(2)}, u32[]{:S(2)}) collective-permute-start(bf16[2,2,64,512]{3,2,1,0:T(8,128)(2,1)S(1)} %shard_map.45), channel_id=1, source_target_pairs={{2,0},{4,1},{10,2},{12,3},{0,4},{6,5},{8,6},{14,7},{3,8},{5,9},{11... | collective-permute-start | bytes 786440 | tf_op jit(solution)/shard_map/ppermute | solution.py:62
  46.7 0.0 collective-permute-done.16.refs_0_
  46.8 0.0 collective-permute-done.17.refs_1_
  46.8 0.0 slice-done
  46.8 0.0 slice-done.1
  46.8 1.4 %shard_map.49 = (bf16[128,512]{1,0:T(8,128)(2,1)S(1)}, bf16[128,512]{1,0:T(8,128)(2,1)S(1)}) custom-call(bf16[2,2,64,512]{3,2,1,0:T(8,128)(2,1)S(1)} %collective-permute-done.16.refs_0_, bf16[2,2,64,512]{3,2,1,0:T(8,128)(2,1)S(1)} %collective-permute-done.17.refs_1_, bf16[3,3,512,512]{3,2,1,0:T(8,128)(2,1)S(1)} %bitcast.3), custom_call_target="tpu_custom_call" | custom-call | flops 1207959552 | bytes 5242880 | tf_op jit(solution)/shard_map/pallas_call | solution.py:75
  48.2 4.7 %collective-permute-start.18 = (bf16[128,512]{1,0:T(8,128)(2,1)S(1)}, bf16[128,512]{1,0:T(8,128)(2,1)S(1)}, u32[]{:S(2)}, u32[]{:S(2)}) collective-permute-start(bf16[128,512]{1,0:T(8,128)(2,1)S(1)} %get-tuple-element.48), channel_id=1, source_target_pairs={{0,1},{1,0},{2,3},{3,2},{4,5},{5,4},{6,7},{7,6},{8,9},{9,8},{10,11... | collective-permute-start | bytes 393224 | tf_op jit(solution)/shard_map/ppermute | solution.py:71
  52.9 0.1 collective-permute-start.19
  53.0 1.4 %shard_map.48 = bf16[256,512]{1,0:T(8,128)(2,1)S(1)} custom-call(bf16[2,2,64,512]{3,2,1,0:T(8,128)(2,1)S(1)} %collective-permute-done.16.refs_0_, bf16[2,2,64,512]{3,2,1,0:T(8,128)(2,1)S(1)} %collective-permute-done.17.refs_1_, bf16[3,3,512,512]{3,2,1,0:T(8,128)(2,1)S(1)} %bitcast.3), custom_call_target="tpu_custom_call" | custom-call | flops 1207959552 | bytes 5242880 | tf_op jit(solution)/shard_map/pallas_call | solution.py:75
  54.4 0.5 collective-permute-start.21
  54.9 0.0 collective-permute-done.12.refs_0_
  54.9 0.0 collective-permute-done.18.refs_2_.refs_3_
  54.9 0.0 collective-permute-done.19.refs_3_.refs_4_
  54.9 0.8 %shard_map.50 = bf16[112,512]{1,0:T(8,128)(2,1)S(1)} custom-call(bf16[2,2,64,512]{3,2,1,0:T(8,128)(2,1)S(1)} %collective-permute-done.12.refs_0_, bf16[3,3,512,512]{3,2,1,0:T(8,128)(2,1)S(1)} %bitcast.3, bf16[128,512]{1,0:T(8,128)(2,1)S(1)} %collective-permute-done.18.refs_2_.refs_3_, bf16[128,512]{1,0:T(8,128)(2,1)S(1)} %collective-permute-done.19.refs_3_.refs_4_), custom_call_target="tpu_custom_call" | custom-call | flops 528482304 | bytes 5242880 | tf_op jit(solution)/shard_map/pallas_call | solution.py:75
  55.7 5.5 %collective-permute-start.20 = (bf16[112,512]{1,0:T(8,128)(2,1)S(1)}, bf16[112,512]{1,0:T(8,128)(2,1)S(1)}, u32[]{:S(2)}, u32[]{:S(2)}) collective-permute-start(bf16[112,512]{1,0:T(8,128)(2,1)S(1)} %shard_map.50), channel_id=1, source_target_pairs={{0,2},{1,3},{2,0},{3,1},{4,6},{5,7},{6,4},{7,5},{8,10},{9,11},{10,... | collective-permute-start | bytes 344072 | tf_op jit(solution)/shard_map/ppermute | solution.py:71
  61.2 0.0 collective-permute-done.13.refs_1_
  61.2 1.0 %shard_map.51 = bf16[144,512]{1,0:T(8,128)(2,1)S(1)} custom-call(bf16[2,2,64,512]{3,2,1,0:T(8,128)(2,1)S(1)} %collective-permute-done.12.refs_0_, bf16[2,2,64,512]{3,2,1,0:T(8,128)(2,1)S(1)} %collective-permute-done.13.refs_1_, bf16[3,3,512,512]{3,2,1,0:T(8,128)(2,1)S(1)} %bitcast.3, bf16[128,512]{1,0:T(8,128)(2,1)S(1)} %collective-permute-done.18.refs_2_.refs_3_, ...), custom_call_target="tpu_custom_call" | custom-call | flops 679477248 | bytes 5505024 | tf_op jit(solution)/shard_map/pallas_call | solution.py:75
  62.2 2.1 %collective-permute-start.22 = (bf16[144,512]{1,0:T(8,128)(2,1)S(1)}, bf16[144,512]{1,0:T(8,128)(2,1)S(1)}, u32[]{:S(2)}, u32[]{:S(2)}) collective-permute-start(bf16[144,512]{1,0:T(8,128)(2,1)S(1)} %shard_map.51), channel_id=1, source_target_pairs={{0,2},{1,3},{2,0},{3,1},{4,6},{5,7},{6,4},{7,5},{8,10},{9,11},{10,... | collective-permute-start | bytes 442376 | tf_op jit(solution)/shard_map/ppermute | solution.py:71
  64.3 0.1 collective-permute-done.20.refs_0_
  64.3 0.0 collective-permute-done.21.refs_3_
  64.3 1.4 %shard_map.52.kept = f32[256,512]{1,0:T(8,128)S(1)} custom-call(bf16[2,2,64,512]{3,2,1,0:T(8,128)(2,1)S(1)} %collective-permute-done.12.refs_0_, bf16[2,2,64,512]{3,2,1,0:T(8,128)(2,1)S(1)} %collective-permute-done.13.refs_1_, bf16[3,3,512,512]{3,2,1,0:T(8,128)(2,1)S(1)} %bitcast.3, bf16[256,512]{1,0:T(8,128)(2,1)S(1)} %collective-permute-done.21.refs_3_), custom_call_target="tpu_custom_call" | custom-call | flops 1207959552 | bytes 5505024 | tf_op jit(solution)/shard_map/pallas_call | solution.py:75
  65.8 2.4 %collective-permute-done.22.refs_1_ = bf16[144,512]{1,0:T(8,128)(2,1)S(1)} collective-permute-done((bf16[144,512]{1,0:T(8,128)(2,1)S(1)}, bf16[144,512]{1,0:T(8,128)(2,1)S(1)}, u32[]{:S(2)}, u32[]{:S(2)}) %collective-permute-start.22) | collective-permute-done | bytes 147488 | tf_op jit(solution)/shard_map/ppermute | solution.py:71
  68.1 0.8 %shard_map.53 = bf16[256,512]{1,0:T(8,128)(2,1)} custom-call(f32[256,512]{1,0:T(8,128)S(1)} %shard_map.52.kept, bf16[112,512]{1,0:T(8,128)(2,1)S(1)} %collective-permute-done.20.refs_0_, bf16[144,512]{1,0:T(8,128)(2,1)S(1)} %collective-permute-done.22.refs_1_), custom_call_target="tpu_custom_call" | custom-call | bytes 786432 | tf_op jit(solution)/shard_map/pallas_call | solution.py:75
  (6 shorter events, 0.1 us)
Async XLA Ops:
  0.0 11.2 %collective-permute-start.2 = (bf16[256,512]{1,0:T(8,128)(2,1)}, bf16[256,512]{1,0:T(8,128)(2,1)S(1)}, u32[]{:S(2)}, u32[]{:S(2)}) collective-permute-start(bf16[256,512]{1,0:T(8,128)(2,1)} %bitcast.4), channel_id=1, source_target_pairs={{0,12},{1,0},{2,4},{3,8},{4,13},{5,1},{6,5},{7,9},{8,14},{9,2},{10... | collective-permute-start | bytes 786440 | tf_op jit(solution)/shard_map/ppermute | solution.py:45
  5.0 11.8 %collective-permute-start.3 = (bf16[256,512]{1,0:T(8,128)(2,1)}, bf16[256,512]{1,0:T(8,128)(2,1)S(1)}, u32[]{:S(2)}, u32[]{:S(2)}) collective-permute-start(bf16[256,512]{1,0:T(8,128)(2,1)} %bitcast.5), channel_id=1, source_target_pairs={{0,4},{1,8},{2,12},{3,0},{4,5},{5,9},{6,13},{7,1},{8,6},{9,10},{10... | collective-permute-start | bytes 786440 | tf_op jit(solution)/shard_map/ppermute | solution.py:45
  5.1 23.9 %collective-permute-start = (bf16[256,512]{1,0:T(8,128)(2,1)}, bf16[256,512]{1,0:T(8,128)(2,1)S(1)}, u32[]{:S(2)}, u32[]{:S(2)}) collective-permute-start(bf16[256,512]{1,0:T(8,128)(2,1)} %bitcast.6), channel_id=1, source_target_pairs={{0,8},{1,12},{2,0},{3,4},{4,9},{5,13},{6,1},{7,5},{8,10},{9,14},{1... | collective-permute-start | bytes 786440 | tf_op jit(solution)/shard_map/ppermute | solution.py:45
  6.6 22.4 %collective-permute-start.1 = (bf16[256,512]{1,0:T(8,128)(2,1)}, bf16[256,512]{1,0:T(8,128)(2,1)S(1)}, u32[]{:S(2)}, u32[]{:S(2)}) collective-permute-start(bf16[256,512]{1,0:T(8,128)(2,1)} %bitcast.7), channel_id=1, source_target_pairs={{0,0},{1,4},{2,8},{3,12},{4,1},{5,5},{6,9},{7,13},{8,2},{9,6},{10,... | collective-permute-start | bytes 786440 | tf_op jit(solution)/shard_map/ppermute | solution.py:45
  8.2 2.3 %copy-start = (bf16[3,3,512,512]{3,2,1,0:T(8,128)(2,1)S(1)}, bf16[3,3,512,512]{3,2,1,0:T(8,128)(2,1)}, u32[]{:S(2)}) copy-start(bf16[3,3,512,512]{3,2,1,0:T(8,128)(2,1)} %source.1) | copy-start | bytes 14155780
  18.4 2.0 %collective-permute-start.4 = (bf16[128,512]{1,0:T(8,128)(2,1)S(1)}, bf16[128,512]{1,0:T(8,128)(2,1)S(1)}, u32[]{:S(2)}, u32[]{:S(2)}) collective-permute-start(bf16[128,512]{1,0:T(8,128)(2,1)S(1)} %get-tuple-element.31), channel_id=1, source_target_pairs={{0,1},{1,0},{2,3},{3,2},{4,5},{5,4},{6,7},{7,6},{8,9},{9,8},{10,11... | collective-permute-start | bytes 393224 | tf_op jit(solution)/shard_map/ppermute | solution.py:71
  18.5 1.9 %collective-permute-start.5 = (bf16[128,512]{1,0:T(8,128)(2,1)S(1)}, bf16[128,512]{1,0:T(8,128)(2,1)S(1)}, u32[]{:S(2)}, u32[]{:S(2)}) collective-permute-start(bf16[128,512]{1,0:T(8,128)(2,1)S(1)} %get-tuple-element.32), channel_id=1, source_target_pairs={{0,1},{1,0},{2,3},{3,2},{4,5},{5,4},{6,7},{7,6},{8,9},{9,8},{10,11... | collective-permute-start | bytes 393224 | tf_op jit(solution)/shard_map/ppermute | solution.py:71
  20.4 12.7 %collective-permute-start.14 = (bf16[2,64,512]{2,1,0:T(8,128)(2,1)S(1)}, bf16[2,64,512]{2,1,0:T(8,128)(2,1)S(1)}, u32[]{:S(2)}, u32[]{:S(2)}) collective-permute-start(bf16[2,64,512]{2,1,0:T(8,128)(2,1)S(1)} %get-tuple-element.33), channel_id=1, source_target_pairs={{0,2},{1,3},{2,0},{3,1},{4,6},{5,7},{6,4},{7,5},{8,10},{9,11},{10,... | collective-permute-start | bytes 393224 | tf_op jit(solution)/shard_map/ppermute | solution.py:71
  28.9 17.8 %slice-start = ((s8[4718592]{0:T(1024)(128)(4,1)}), s8[524288]{0:T(1024)(128)(4,1)S(1)}, s32[]{:S(2)}) async-start(s8[4718592]{0:T(1024)(128)(4,1)} %bitcast.2), calls=%async_computation | async-start | bytes 1048576
  30.5 2.5 %collective-permute-start.6 = (bf16[64,512]{1,0:T(8,128)(2,1)S(1)}, bf16[64,512]{1,0:T(8,128)(2,1)S(1)}, u32[]{:S(2)}, u32[]{:S(2)}) collective-permute-start(bf16[64,512]{1,0:T(8,128)(2,1)S(1)} %get-tuple-element.37), channel_id=1, source_target_pairs={{0,1},{1,0},{2,3},{3,2},{4,5},{5,4},{6,7},{7,6},{8,9},{9,8},{10,11... | collective-permute-start | bytes 196616 | tf_op jit(solution)/shard_map/ppermute | solution.py:71
  30.6 2.4 %collective-permute-start.7 = (bf16[64,512]{1,0:T(8,128)(2,1)S(1)}, bf16[64,512]{1,0:T(8,128)(2,1)S(1)}, u32[]{:S(2)}, u32[]{:S(2)}) collective-permute-start(bf16[64,512]{1,0:T(8,128)(2,1)S(1)} %get-tuple-element.38), channel_id=1, source_target_pairs={{0,1},{1,0},{2,3},{3,2},{4,5},{5,4},{6,7},{7,6},{8,9},{9,8},{10,11... | collective-permute-start | bytes 196616 | tf_op jit(solution)/shard_map/ppermute | solution.py:71
  31.1 1.9 %collective-permute-start.8 = (bf16[64,512]{1,0:T(8,128)(2,1)S(1)}, bf16[64,512]{1,0:T(8,128)(2,1)S(1)}, u32[]{:S(2)}, u32[]{:S(2)}) collective-permute-start(bf16[64,512]{1,0:T(8,128)(2,1)S(1)} %get-tuple-element.39), channel_id=1, source_target_pairs={{0,1},{1,0},{2,3},{3,2},{4,5},{5,4},{6,7},{7,6},{8,9},{9,8},{10,11... | collective-permute-start | bytes 196616 | tf_op jit(solution)/shard_map/ppermute | solution.py:71
  31.2 1.8 %collective-permute-start.9 = (bf16[64,512]{1,0:T(8,128)(2,1)S(1)}, bf16[64,512]{1,0:T(8,128)(2,1)S(1)}, u32[]{:S(2)}, u32[]{:S(2)}) collective-permute-start(bf16[64,512]{1,0:T(8,128)(2,1)S(1)} %get-tuple-element.40), channel_id=1, source_target_pairs={{0,1},{1,0},{2,3},{3,2},{4,5},{5,4},{6,7},{7,6},{8,9},{9,8},{10,11... | collective-permute-start | bytes 196616 | tf_op jit(solution)/shard_map/ppermute | solution.py:71
  31.6 15.2 %slice-start.1 = ((s8[4718592]{0:T(1024)(128)(4,1)}), s8[4194304]{0:T(1024)(128)(4,1)S(1)}, s32[]{:S(2)}) async-start(s8[4718592]{0:T(1024)(128)(4,1)} %bitcast.2), calls=%async_computation.1 | async-start | bytes 8388608
  33.2 1.6 %collective-permute-start.15 = (bf16[2,64,512]{2,1,0:T(8,128)(2,1)S(1)}, bf16[2,64,512]{2,1,0:T(8,128)(2,1)S(1)}, u32[]{:S(2)}, u32[]{:S(2)}) collective-permute-start(bf16[2,64,512]{2,1,0:T(8,128)(2,1)S(1)} %shard_map.46.own), channel_id=1, source_target_pairs={{0,1},{1,0},{2,3},{3,2},{4,5},{5,4},{6,7},{7,6},{8,9},{9,8},{10,11... | collective-permute-start | bytes 393224 | tf_op jit(solution)/shard_map/ppermute | solution.py:71
  33.3 5.9 %collective-permute-start.10 = (bf16[2,64,512]{2,1,0:T(8,128)(2,1)S(1)}, bf16[2,64,512]{2,1,0:T(8,128)(2,1)S(1)}, u32[]{:S(2)}, u32[]{:S(2)}) collective-permute-start(bf16[2,64,512]{2,1,0:T(8,128)(2,1)S(1)} %get-tuple-element.42), channel_id=1, source_target_pairs={{0,2},{1,3},{2,0},{3,1},{4,6},{5,7},{6,4},{7,5},{8,10},{9,11},{10,... | collective-permute-start | bytes 393224 | tf_op jit(solution)/shard_map/ppermute | solution.py:71
  34.9 11.9 %collective-permute-start.16 = (bf16[2,2,64,512]{3,2,1,0:T(8,128)(2,1)S(1)}, bf16[2,2,64,512]{3,2,1,0:T(8,128)(2,1)S(1)}, u32[]{:S(2)}, u32[]{:S(2)}) collective-permute-start(bf16[2,2,64,512]{3,2,1,0:T(8,128)(2,1)S(1)} %shard_map.47), channel_id=1, source_target_pairs={{2,0},{6,1},{10,2},{14,3},{0,4},{4,5},{8,6},{12,7},{3,8},{7,9},{11... | collective-permute-start | bytes 786440 | tf_op jit(solution)/shard_map/ppermute | solution.py:62
  35.3 11.5 %collective-permute-start.17 = (bf16[2,2,64,512]{3,2,1,0:T(8,128)(2,1)S(1)}, bf16[2,2,64,512]{3,2,1,0:T(8,128)(2,1)S(1)}, u32[]{:S(2)}, u32[]{:S(2)}) collective-permute-start(bf16[2,2,64,512]{3,2,1,0:T(8,128)(2,1)S(1)} %shard_map.47), channel_id=1, source_target_pairs={{0,0},{4,1},{8,2},{12,3},{2,4},{6,5},{10,6},{14,7},{1,8},{5,9},{9,... | collective-permute-start | bytes 786440 | tf_op jit(solution)/shard_map/ppermute | solution.py:62
  39.3 1.5 %collective-permute-start.11 = (bf16[2,64,512]{2,1,0:T(8,128)(2,1)S(1)}, bf16[2,64,512]{2,1,0:T(8,128)(2,1)S(1)}, u32[]{:S(2)}, u32[]{:S(2)}) collective-permute-start(bf16[2,64,512]{2,1,0:T(8,128)(2,1)S(1)} %shard_map.44.own), channel_id=1, source_target_pairs={{0,1},{1,0},{2,3},{3,2},{4,5},{5,4},{6,7},{7,6},{8,9},{9,8},{10,11... | collective-permute-start | bytes 393224 | tf_op jit(solution)/shard_map/ppermute | solution.py:71
  40.8 14.1 %collective-permute-start.12 = (bf16[2,2,64,512]{3,2,1,0:T(8,128)(2,1)S(1)}, bf16[2,2,64,512]{3,2,1,0:T(8,128)(2,1)S(1)}, u32[]{:S(2)}, u32[]{:S(2)}) collective-permute-start(bf16[2,2,64,512]{3,2,1,0:T(8,128)(2,1)S(1)} %shard_map.45), channel_id=1, source_target_pairs={{0,0},{6,1},{8,2},{14,3},{2,4},{4,5},{10,6},{12,7},{1,8},{7,9},{9,... | collective-permute-start | bytes 786440 | tf_op jit(solution)/shard_map/ppermute | solution.py:62
  41.5 19.7 %collective-permute-start.13 = (bf16[2,2,64,512]{3,2,1,0:T(8,128)(2,1)S(1)}, bf16[2,2,64,512]{3,2,1,0:T(8,128)(2,1)S(1)}, u32[]{:S(2)}, u32[]{:S(2)}) collective-permute-start(bf16[2,2,64,512]{3,2,1,0:T(8,128)(2,1)S(1)} %shard_map.45), channel_id=1, source_target_pairs={{2,0},{4,1},{10,2},{12,3},{0,4},{6,5},{8,6},{14,7},{3,8},{5,9},{11... | collective-permute-start | bytes 786440 | tf_op jit(solution)/shard_map/ppermute | solution.py:62
  48.2 6.7 %collective-permute-start.18 = (bf16[128,512]{1,0:T(8,128)(2,1)S(1)}, bf16[128,512]{1,0:T(8,128)(2,1)S(1)}, u32[]{:S(2)}, u32[]{:S(2)}) collective-permute-start(bf16[128,512]{1,0:T(8,128)(2,1)S(1)} %get-tuple-element.48), channel_id=1, source_target_pairs={{0,1},{1,0},{2,3},{3,2},{4,5},{5,4},{6,7},{7,6},{8,9},{9,8},{10,11... | collective-permute-start | bytes 393224 | tf_op jit(solution)/shard_map/ppermute | solution.py:71
  52.9 2.0 %collective-permute-start.19 = (bf16[128,512]{1,0:T(8,128)(2,1)S(1)}, bf16[128,512]{1,0:T(8,128)(2,1)S(1)}, u32[]{:S(2)}, u32[]{:S(2)}) collective-permute-start(bf16[128,512]{1,0:T(8,128)(2,1)S(1)} %get-tuple-element.49), channel_id=1, source_target_pairs={{0,1},{1,0},{2,3},{3,2},{4,5},{5,4},{6,7},{7,6},{8,9},{9,8},{10,11... | collective-permute-start | bytes 393224 | tf_op jit(solution)/shard_map/ppermute | solution.py:71
  54.4 9.9 %collective-permute-start.21 = (bf16[256,512]{1,0:T(8,128)(2,1)S(1)}, bf16[256,512]{1,0:T(8,128)(2,1)S(1)}, u32[]{:S(2)}, u32[]{:S(2)}) collective-permute-start(bf16[256,512]{1,0:T(8,128)(2,1)S(1)} %shard_map.48), channel_id=1, source_target_pairs={{0,1},{1,0},{2,3},{3,2},{4,5},{5,4},{6,7},{7,6},{8,9},{9,8},{10,11... | collective-permute-start | bytes 786440 | tf_op jit(solution)/shard_map/ppermute | solution.py:71
  55.7 8.6 %collective-permute-start.20 = (bf16[112,512]{1,0:T(8,128)(2,1)S(1)}, bf16[112,512]{1,0:T(8,128)(2,1)S(1)}, u32[]{:S(2)}, u32[]{:S(2)}) collective-permute-start(bf16[112,512]{1,0:T(8,128)(2,1)S(1)} %shard_map.50), channel_id=1, source_target_pairs={{0,2},{1,3},{2,0},{3,1},{4,6},{5,7},{6,4},{7,5},{8,10},{9,11},{10,... | collective-permute-start | bytes 344072 | tf_op jit(solution)/shard_map/ppermute | solution.py:71
  62.2 6.0 %collective-permute-start.22 = (bf16[144,512]{1,0:T(8,128)(2,1)S(1)}, bf16[144,512]{1,0:T(8,128)(2,1)S(1)}, u32[]{:S(2)}, u32[]{:S(2)}) collective-permute-start(bf16[144,512]{1,0:T(8,128)(2,1)S(1)} %shard_map.51), channel_id=1, source_target_pairs={{0,2},{1,3},{2,0},{3,1},{4,6},{5,7},{6,4},{7,5},{8,10},{9,11},{10,... | collective-permute-start | bytes 442376 | tf_op jit(solution)/shard_map/ppermute | solution.py:71

commit v9 on v8

--- a/solution.py
+++ b/solution.py
@@ -46,7 +46,7 @@
         return taken
 
     def pair_of(self, half, level, col, turn):
-        return (level // self.ratio + turn + (col if half else 1)) % self.pairs
+        return (level // self.ratio + turn + 1 + (col if half else 0)) % self.pairs
 
     def spread(self, x, half, turn):
         taken = []

time: 69.1 us -> 68.2 us (0.987)
  waiting for transfers between devices: 12.7 us -> 11.9 us
    ppermute x4, starting transfers between devices: 7.03 us -> 5.65 us  [spread(): taken.append(lax.ppermute(x, ('chan', 'img'), moves))]
    ppermute x15, starting transfers between devices: 25.1 us -> 26.2 us  [swap(): return lax.ppermute(x, 'img', [(i, i ^ 1 << bit) for i in range(self.cols)])]
    ppermute x15, waiting for transfers between devices: 6.69 us -> 5.93 us  [swap(): return lax.ppermute(x, 'img', [(i, i ^ 1 << bit) for i in range(self.cols)])]
  transfers between devices with their start and end apart: 23 -> 23, of which waited for: 6 -> 5; matrix products, arithmetic and copies ran while one was open for 0% -> 0% of each run, Pallas kernels for 18% -> 18%
where the time goes in v9:
time: 68.2 us; the launch traced here: 68 us
  starting transfers between devices  40 us (59%)
  Pallas kernels  13.4 us (20%)
  waiting for transfers between devices  11.9 us (17%)
  local copies, waits for them, and re-layouts  2.34 us (3%)
    ppermute x15, starting transfers between devices, swap(): return lax.ppermute(x, 'img', [(i, i ^ 1 << bit) for i in range(self.cols)])  26.2 us
    pallas_call x16, Pallas kernels, call(): pl.pallas_call(body, in_specs=[VMEM] * len(inputs), out_specs=[VMEM] * le...  13.1 us
    ppermute x4, starting transfers between devices, spread_frame(): taken.append(lax.ppermute(x, ('chan', 'img'), moves))  8.17 us
    ppermute x4, waiting for transfers between devices, spread_frame(): taken.append(lax.ppermute(x, ('chan', 'img'), moves))  5.99 us
    ppermute x15, waiting for transfers between devices, swap(): return lax.ppermute(x, 'img', [(i, i ^ 1 << bit) for i in range(self.cols)])  5.93 us
    ppermute x4, starting transfers between devices, spread(): taken.append(lax.ppermute(x, ('chan', 'img'), moves))  5.65 us
    unnamed x6, local copies, waits for them, and re-layouts  2.34 us
  transfers between devices with their start and end apart: 23, of which 5 were waited for; matrix products, arithmetic and copies ran while one was open for 0% of the time, Pallas kernels for 18%

profile of v9, /device:TPU:0, one launch (start us, length us, event | category | flops | bytes accessed | tf_op | source)
XLA Modules:
  0.0 68.0 jit_solution(6576238420755957496)
XLA Ops:
  0.0 5.0 %collective-permute-start.2 = (bf16[256,512]{1,0:T(8,128)(2,1)}, bf16[256,512]{1,0:T(8,128)(2,1)S(1)}, u32[]{:S(2)}, u32[]{:S(2)}) collective-permute-start(bf16[256,512]{1,0:T(8,128)(2,1)} %bitcast.4), channel_id=1, source_target_pairs={{0,12},{1,0},{2,4},{3,8},{4,13},{5,1},{6,5},{7,9},{8,14},{9,2},{10... | collective-permute-start | bytes 786440 | tf_op jit(solution)/shard_map/ppermute | solution.py:45
  5.0 0.0 collective-permute-start.3
  5.1 1.5 %collective-permute-start = (bf16[256,512]{1,0:T(8,128)(2,1)}, bf16[256,512]{1,0:T(8,128)(2,1)S(1)}, u32[]{:S(2)}, u32[]{:S(2)}) collective-permute-start(bf16[256,512]{1,0:T(8,128)(2,1)} %bitcast.6), channel_id=1, source_target_pairs={{0,8},{1,12},{2,0},{3,4},{4,9},{5,13},{6,1},{7,5},{8,10},{9,14},{1... | collective-permute-start | bytes 786440 | tf_op jit(solution)/shard_map/ppermute | solution.py:45
  6.6 1.6 %collective-permute-start.1 = (bf16[256,512]{1,0:T(8,128)(2,1)}, bf16[256,512]{1,0:T(8,128)(2,1)S(1)}, u32[]{:S(2)}, u32[]{:S(2)}) collective-permute-start(bf16[256,512]{1,0:T(8,128)(2,1)} %bitcast.7), channel_id=1, source_target_pairs={{0,0},{1,4},{2,8},{3,12},{4,1},{5,5},{6,9},{7,13},{8,2},{9,6},{10,... | collective-permute-start | bytes 786440 | tf_op jit(solution)/shard_map/ppermute | solution.py:45
  8.2 2.3 %copy-done = bf16[3,3,512,512]{3,2,1,0:T(8,128)(2,1)S(1)} copy-done((bf16[3,3,512,512]{3,2,1,0:T(8,128)(2,1)S(1)}, bf16[3,3,512,512]{3,2,1,0:T(8,128)(2,1)}, u32[]{:S(2)}) %copy-start) | copy-done | bytes 4718616
  10.5 0.3 shard_map.37.refs_2_.kernel
  10.8 0.4 collective-permute-done.2.refs_0_
  11.2 5.6 %collective-permute-done.3.refs_1_ = bf16[256,512]{1,0:T(8,128)(2,1)S(1)} collective-permute-done((bf16[256,512]{1,0:T(8,128)(2,1)}, bf16[256,512]{1,0:T(8,128)(2,1)S(1)}, u32[]{:S(2)}, u32[]{:S(2)}) %collective-permute-start.3) | collective-permute-done | bytes 262176 | tf_op jit(solution)/shard_map/ppermute | solution.py:45
  16.8 1.6 %shard_map.38 = (bf16[128,512]{1,0:T(8,128)(2,1)S(1)}, bf16[128,512]{1,0:T(8,128)(2,1)S(1)}, bf16[2,288,1536]{2,1,0:T(8,128)(2,1)S(1)}) custom-call(bf16[256,512]{1,0:T(8,128)(2,1)S(1)} %collective-permute-done.2.refs_0_, bf16[256,512]{1,0:T(8,128)(2,1)S(1)} %collective-permute-done.3.refs_1_, bf16[3,3,512,512]{3,2,1,0:T(8,128)(2,1)S(1)} %shard_map.37.refs_2_.kernel), custom_call_target="tpu_custom_call" | custom-call | flops 1207959552 | bytes 5242880 | tf_op jit(solution)/shard_map/pallas_call | solution.py:75
  18.4 0.1 collective-permute-start.4
  18.5 0.5 collective-permute-start.5
  19.0 1.4 %shard_map.39.kept = f32[2,128,512]{2,1,0:T(8,128)S(1)} custom-call(bf16[2,288,1536]{2,1,0:T(8,128)(2,1)S(1)} %get-tuple-element.30.wide, bf16[3,3,512,512]{3,2,1,0:T(8,128)(2,1)S(1)} %shard_map.37.refs_2_.kernel), custom_call_target="tpu_custom_call" | custom-call | flops 1207959552 | bytes 6488064 | tf_op jit(solution)/shard_map/pallas_call | solution.py:75
  20.3 0.0 collective-permute-done.4.refs_0_
  20.3 0.0 collective-permute-done.5.refs_1_
  20.4 0.1 shard_map.40
  20.4 8.5 %collective-permute-start.14 = (bf16[2,64,512]{2,1,0:T(8,128)(2,1)S(1)}, bf16[2,64,512]{2,1,0:T(8,128)(2,1)S(1)}, u32[]{:S(2)}, u32[]{:S(2)}) collective-permute-start(bf16[2,64,512]{2,1,0:T(8,128)(2,1)S(1)} %get-tuple-element.33), channel_id=1, source_target_pairs={{0,2},{1,3},{2,0},{3,1},{4,6},{5,7},{6,4},{7,5},{8,10},{9,11},{10,... | collective-permute-start | bytes 393224 | tf_op jit(solution)/shard_map/ppermute | solution.py:71
  28.9 0.0 collective-permute-done.refs_0_
  28.9 0.0 collective-permute-done.1.refs_1_
  29.0 1.5 %shard_map.41 = (bf16[64,512]{1,0:T(8,128)(2,1)S(1)}, bf16[64,512]{1,0:T(8,128)(2,1)S(1)}, bf16[64,512]{1,0:T(8,128)(2,1)S(1)}, bf16[64,512]{1,0:T(8,128)(2,1)S(1)}, bf16[2,288,1536]{2,1,0:T(8,128)(2,1)S(1)}) custom-call(bf16[256,512]{1,0:T(8,128)(2,1)S(1)} %collective-permute-done.refs_0_, bf16[256,512]{1,0:T(8,128)(2,1)S(1)} %collective-permute-done.1.refs_1_, ...), custom_call_target="tpu_custom_call" | custom-call | flops 1207959552 | bytes 5242880 | tf_op jit(solution)/shard_map/pallas_call | solution.py:75
  30.5 0.1 collective-permute-start.6
  30.6 0.5 collective-permute-start.7
  31.1 0.1 collective-permute-start.8
  31.2 0.4 collective-permute-start.9
  31.6 1.4 %shard_map.42.kept = f32[2,128,512]{2,1,0:T(8,128)S(1)} custom-call(bf16[2,288,1536]{2,1,0:T(8,128)(2,1)S(1)} %get-tuple-element.36.wide, bf16[3,3,512,512]{3,2,1,0:T(8,128)(2,1)S(1)} %shard_map.37.refs_2_.kernel), custom_call_target="tpu_custom_call" | custom-call | flops 1207959552 | bytes 6488064 | tf_op jit(solution)/shard_map/pallas_call | solution.py:75
  33.0 0.0 collective-permute-done.6.refs_0_
  33.0 0.0 collective-permute-done.7.refs_1_
  33.0 0.0 collective-permute-done.8.refs_2_
  33.0 0.0 collective-permute-done.9.refs_3_
  33.0 0.1 shard_map.43
  33.1 0.0 collective-permute-done.14.came
  33.1 0.1 shard_map.46.own
  33.2 0.1 collective-permute-start.15
  33.3 1.5 %collective-permute-start.10 = (bf16[2,64,512]{2,1,0:T(8,128)(2,1)S(1)}, bf16[2,64,512]{2,1,0:T(8,128)(2,1)S(1)}, u32[]{:S(2)}, u32[]{:S(2)}) collective-permute-start(bf16[2,64,512]{2,1,0:T(8,128)(2,1)S(1)} %get-tuple-element.42), channel_id=1, source_target_pairs={{0,2},{1,3},{2,0},{3,1},{4,6},{5,7},{6,4},{7,5},{8,10},{9,11},{10,... | collective-permute-start | bytes 393224 | tf_op jit(solution)/shard_map/ppermute | solution.py:71
  34.8 0.0 collective-permute-done.15.came
  34.9 0.4 collective-permute-start.16
  35.3 0.7 collective-permute-start.17
  36.0 3.2 %collective-permute-done.10.came = bf16[2,64,512]{2,1,0:T(8,128)(2,1)S(1)} collective-permute-done((bf16[2,64,512]{2,1,0:T(8,128)(2,1)S(1)}, bf16[2,64,512]{2,1,0:T(8,128)(2,1)S(1)}, u32[]{:S(2)}, u32[]{:S(2)}) %collective-permute-start.10) | collective-permute-done | bytes 131104 | tf_op jit(solution)/shard_map/ppermute | solution.py:71
  39.2 0.1 shard_map.44.own
  39.3 0.5 collective-permute-start.11
  39.8 1.0 %collective-permute-done.11.came = bf16[2,64,512]{2,1,0:T(8,128)(2,1)S(1)} collective-permute-done((bf16[2,64,512]{2,1,0:T(8,128)(2,1)S(1)}, bf16[2,64,512]{2,1,0:T(8,128)(2,1)S(1)}, u32[]{:S(2)}, u32[]{:S(2)}) %collective-permute-start.11) | collective-permute-done | bytes 131104 | tf_op jit(solution)/shard_map/ppermute | solution.py:71
  40.8 3.9 %collective-permute-start.12 = (bf16[2,2,64,512]{3,2,1,0:T(8,128)(2,1)S(1)}, bf16[2,2,64,512]{3,2,1,0:T(8,128)(2,1)S(1)}, u32[]{:S(2)}, u32[]{:S(2)}) collective-permute-start(bf16[2,2,64,512]{3,2,1,0:T(8,128)(2,1)S(1)} %shard_map.45), channel_id=1, source_target_pairs={{2,0},{4,1},{10,2},{12,3},{0,4},{6,5},{8,6},{14,7},{3,8},{5,9},{11... | collective-permute-start | bytes 786440 | tf_op jit(solution)/shard_map/ppermute | solution.py:62
  44.7 0.7 collective-permute-start.13
  45.4 0.0 collective-permute-done.16.refs_0_
  45.4 0.0 collective-permute-done.17.refs_1_
  45.4 0.0 slice-done
  45.4 0.0 slice-done.1
  45.4 1.4 %shard_map.49 = (bf16[128,512]{1,0:T(8,128)(2,1)S(1)}, bf16[128,512]{1,0:T(8,128)(2,1)S(1)}) custom-call(bf16[2,2,64,512]{3,2,1,0:T(8,128)(2,1)S(1)} %collective-permute-done.16.refs_0_, bf16[2,2,64,512]{3,2,1,0:T(8,128)(2,1)S(1)} %collective-permute-done.17.refs_1_, bf16[3,3,512,512]{3,2,1,0:T(8,128)(2,1)S(1)} %bitcast.3), custom_call_target="tpu_custom_call" | custom-call | flops 1207959552 | bytes 5242880 | tf_op jit(solution)/shard_map/pallas_call | solution.py:75
  46.9 8.2 %collective-permute-start.18 = (bf16[128,512]{1,0:T(8,128)(2,1)S(1)}, bf16[128,512]{1,0:T(8,128)(2,1)S(1)}, u32[]{:S(2)}, u32[]{:S(2)}) collective-permute-start(bf16[128,512]{1,0:T(8,128)(2,1)S(1)} %get-tuple-element.48), channel_id=1, source_target_pairs={{0,1},{1,0},{2,3},{3,2},{4,5},{5,4},{6,7},{7,6},{8,9},{9,8},{10,11... | collective-permute-start | bytes 393224 | tf_op jit(solution)/shard_map/ppermute | solution.py:71
  55.0 0.1 collective-permute-start.19
  55.1 1.4 %shard_map.48 = bf16[256,512]{1,0:T(8,128)(2,1)S(1)} custom-call(bf16[2,2,64,512]{3,2,1,0:T(8,128)(2,1)S(1)} %collective-permute-done.16.refs_0_, bf16[2,2,64,512]{3,2,1,0:T(8,128)(2,1)S(1)} %collective-permute-done.17.refs_1_, bf16[3,3,512,512]{3,2,1,0:T(8,128)(2,1)S(1)} %bitcast.3), custom_call_target="tpu_custom_call" | custom-call | flops 1207959552 | bytes 5242880 | tf_op jit(solution)/shard_map/pallas_call | solution.py:75
  56.5 0.5 collective-permute-start.21
  57.0 0.0 collective-permute-done.12.refs_0_
  57.0 0.0 collective-permute-done.18.refs_2_.refs_3_
  57.0 0.0 collective-permute-done.19.refs_3_.refs_4_
  57.1 0.9 %shard_map.50 = bf16[112,512]{1,0:T(8,128)(2,1)S(1)} custom-call(bf16[2,2,64,512]{3,2,1,0:T(8,128)(2,1)S(1)} %collective-permute-done.12.refs_0_, bf16[3,3,512,512]{3,2,1,0:T(8,128)(2,1)S(1)} %bitcast.3, bf16[128,512]{1,0:T(8,128)(2,1)S(1)} %collective-permute-done.18.refs_2_.refs_3_, bf16[128,512]{1,0:T(8,128)(2,1)S(1)} %collective-permute-done.19.refs_3_.refs_4_), custom_call_target="tpu_custom_call" | custom-call | flops 528482304 | bytes 5242880 | tf_op jit(solution)/shard_map/pallas_call | solution.py:75
  57.9 0.7 collective-permute-start.20
  58.6 0.0 collective-permute-done.13.refs_1_
  58.6 1.0 %shard_map.51 = bf16[144,512]{1,0:T(8,128)(2,1)S(1)} custom-call(bf16[2,2,64,512]{3,2,1,0:T(8,128)(2,1)S(1)} %collective-permute-done.12.refs_0_, bf16[2,2,64,512]{3,2,1,0:T(8,128)(2,1)S(1)} %collective-permute-done.13.refs_1_, bf16[3,3,512,512]{3,2,1,0:T(8,128)(2,1)S(1)} %bitcast.3, bf16[128,512]{1,0:T(8,128)(2,1)S(1)} %collective-permute-done.18.refs_2_.refs_3_, ...), custom_call_target="tpu_custom_call" | custom-call | flops 679477248 | bytes 5505024 | tf_op jit(solution)/shard_map/pallas_call | solution.py:75
  59.6 4.6 %collective-permute-start.22 = (bf16[144,512]{1,0:T(8,128)(2,1)S(1)}, bf16[144,512]{1,0:T(8,128)(2,1)S(1)}, u32[]{:S(2)}, u32[]{:S(2)}) collective-permute-start(bf16[144,512]{1,0:T(8,128)(2,1)S(1)} %shard_map.51), channel_id=1, source_target_pairs={{0,2},{1,3},{2,0},{3,1},{4,6},{5,7},{6,4},{7,5},{8,10},{9,11},{10,... | collective-permute-start | bytes 442376 | tf_op jit(solution)/shard_map/ppermute | solution.py:71
  64.1 0.0 collective-permute-done.20.refs_0_
  64.1 0.0 collective-permute-done.21.refs_3_
  64.1 1.4 %shard_map.52.kept = f32[256,512]{1,0:T(8,128)S(1)} custom-call(bf16[2,2,64,512]{3,2,1,0:T(8,128)(2,1)S(1)} %collective-permute-done.12.refs_0_, bf16[2,2,64,512]{3,2,1,0:T(8,128)(2,1)S(1)} %collective-permute-done.13.refs_1_, bf16[3,3,512,512]{3,2,1,0:T(8,128)(2,1)S(1)} %bitcast.3, bf16[256,512]{1,0:T(8,128)(2,1)S(1)} %collective-permute-done.21.refs_3_), custom_call_target="tpu_custom_call" | custom-call | flops 1207959552 | bytes 5505024 | tf_op jit(solution)/shard_map/pallas_call | solution.py:75
  65.6 1.7 %collective-permute-done.22.refs_1_ = bf16[144,512]{1,0:T(8,128)(2,1)S(1)} collective-permute-done((bf16[144,512]{1,0:T(8,128)(2,1)S(1)}, bf16[144,512]{1,0:T(8,128)(2,1)S(1)}, u32[]{:S(2)}, u32[]{:S(2)}) %collective-permute-start.22) | collective-permute-done | bytes 147488 | tf_op jit(solution)/shard_map/ppermute | solution.py:71
  67.2 0.8 %shard_map.53 = bf16[256,512]{1,0:T(8,128)(2,1)} custom-call(f32[256,512]{1,0:T(8,128)S(1)} %shard_map.52.kept, bf16[112,512]{1,0:T(8,128)(2,1)S(1)} %collective-permute-done.20.refs_0_, bf16[144,512]{1,0:T(8,128)(2,1)S(1)} %collective-permute-done.22.refs_1_), custom_call_target="tpu_custom_call" | custom-call | bytes 786432 | tf_op jit(solution)/shard_map/pallas_call | solution.py:75
  (6 shorter events, 0.1 us)
Async XLA Ops:
  0.0 11.2 %collective-permute-start.2 = (bf16[256,512]{1,0:T(8,128)(2,1)}, bf16[256,512]{1,0:T(8,128)(2,1)S(1)}, u32[]{:S(2)}, u32[]{:S(2)}) collective-permute-start(bf16[256,512]{1,0:T(8,128)(2,1)} %bitcast.4), channel_id=1, source_target_pairs={{0,12},{1,0},{2,4},{3,8},{4,13},{5,1},{6,5},{7,9},{8,14},{9,2},{10... | collective-permute-start | bytes 786440 | tf_op jit(solution)/shard_map/ppermute | solution.py:45
  5.0 11.8 %collective-permute-start.3 = (bf16[256,512]{1,0:T(8,128)(2,1)}, bf16[256,512]{1,0:T(8,128)(2,1)S(1)}, u32[]{:S(2)}, u32[]{:S(2)}) collective-permute-start(bf16[256,512]{1,0:T(8,128)(2,1)} %bitcast.5), channel_id=1, source_target_pairs={{0,4},{1,8},{2,12},{3,0},{4,5},{5,9},{6,13},{7,1},{8,6},{9,10},{10... | collective-permute-start | bytes 786440 | tf_op jit(solution)/shard_map/ppermute | solution.py:45
  5.1 23.9 %collective-permute-start = (bf16[256,512]{1,0:T(8,128)(2,1)}, bf16[256,512]{1,0:T(8,128)(2,1)S(1)}, u32[]{:S(2)}, u32[]{:S(2)}) collective-permute-start(bf16[256,512]{1,0:T(8,128)(2,1)} %bitcast.6), channel_id=1, source_target_pairs={{0,8},{1,12},{2,0},{3,4},{4,9},{5,13},{6,1},{7,5},{8,10},{9,14},{1... | collective-permute-start | bytes 786440 | tf_op jit(solution)/shard_map/ppermute | solution.py:45
  6.6 22.4 %collective-permute-start.1 = (bf16[256,512]{1,0:T(8,128)(2,1)}, bf16[256,512]{1,0:T(8,128)(2,1)S(1)}, u32[]{:S(2)}, u32[]{:S(2)}) collective-permute-start(bf16[256,512]{1,0:T(8,128)(2,1)} %bitcast.7), channel_id=1, source_target_pairs={{0,0},{1,4},{2,8},{3,12},{4,1},{5,5},{6,9},{7,13},{8,2},{9,6},{10,... | collective-permute-start | bytes 786440 | tf_op jit(solution)/shard_map/ppermute | solution.py:45
  8.2 2.3 %copy-start = (bf16[3,3,512,512]{3,2,1,0:T(8,128)(2,1)S(1)}, bf16[3,3,512,512]{3,2,1,0:T(8,128)(2,1)}, u32[]{:S(2)}) copy-start(bf16[3,3,512,512]{3,2,1,0:T(8,128)(2,1)} %source.1) | copy-start | bytes 14155780
  18.4 2.0 %collective-permute-start.4 = (bf16[128,512]{1,0:T(8,128)(2,1)S(1)}, bf16[128,512]{1,0:T(8,128)(2,1)S(1)}, u32[]{:S(2)}, u32[]{:S(2)}) collective-permute-start(bf16[128,512]{1,0:T(8,128)(2,1)S(1)} %get-tuple-element.31), channel_id=1, source_target_pairs={{0,1},{1,0},{2,3},{3,2},{4,5},{5,4},{6,7},{7,6},{8,9},{9,8},{10,11... | collective-permute-start | bytes 393224 | tf_op jit(solution)/shard_map/ppermute | solution.py:71
  18.5 1.9 %collective-permute-start.5 = (bf16[128,512]{1,0:T(8,128)(2,1)S(1)}, bf16[128,512]{1,0:T(8,128)(2,1)S(1)}, u32[]{:S(2)}, u32[]{:S(2)}) collective-permute-start(bf16[128,512]{1,0:T(8,128)(2,1)S(1)} %get-tuple-element.32), channel_id=1, source_target_pairs={{0,1},{1,0},{2,3},{3,2},{4,5},{5,4},{6,7},{7,6},{8,9},{9,8},{10,11... | collective-permute-start | bytes 393224 | tf_op jit(solution)/shard_map/ppermute | solution.py:71
  20.4 12.7 %collective-permute-start.14 = (bf16[2,64,512]{2,1,0:T(8,128)(2,1)S(1)}, bf16[2,64,512]{2,1,0:T(8,128)(2,1)S(1)}, u32[]{:S(2)}, u32[]{:S(2)}) collective-permute-start(bf16[2,64,512]{2,1,0:T(8,128)(2,1)S(1)} %get-tuple-element.33), channel_id=1, source_target_pairs={{0,2},{1,3},{2,0},{3,1},{4,6},{5,7},{6,4},{7,5},{8,10},{9,11},{10,... | collective-permute-start | bytes 393224 | tf_op jit(solution)/shard_map/ppermute | solution.py:71
  28.9 16.4 %slice-start = ((s8[4718592]{0:T(1024)(128)(4,1)}), s8[524288]{0:T(1024)(128)(4,1)S(1)}, s32[]{:S(2)}) async-start(s8[4718592]{0:T(1024)(128)(4,1)} %bitcast.2), calls=%async_computation | async-start | bytes 1048576
  30.5 2.5 %collective-permute-start.6 = (bf16[64,512]{1,0:T(8,128)(2,1)S(1)}, bf16[64,512]{1,0:T(8,128)(2,1)S(1)}, u32[]{:S(2)}, u32[]{:S(2)}) collective-permute-start(bf16[64,512]{1,0:T(8,128)(2,1)S(1)} %get-tuple-element.37), channel_id=1, source_target_pairs={{0,1},{1,0},{2,3},{3,2},{4,5},{5,4},{6,7},{7,6},{8,9},{9,8},{10,11... | collective-permute-start | bytes 196616 | tf_op jit(solution)/shard_map/ppermute | solution.py:71
  30.6 2.4 %collective-permute-start.7 = (bf16[64,512]{1,0:T(8,128)(2,1)S(1)}, bf16[64,512]{1,0:T(8,128)(2,1)S(1)}, u32[]{:S(2)}, u32[]{:S(2)}) collective-permute-start(bf16[64,512]{1,0:T(8,128)(2,1)S(1)} %get-tuple-element.38), channel_id=1, source_target_pairs={{0,1},{1,0},{2,3},{3,2},{4,5},{5,4},{6,7},{7,6},{8,9},{9,8},{10,11... | collective-permute-start | bytes 196616 | tf_op jit(solution)/shard_map/ppermute | solution.py:71
  31.1 1.9 %collective-permute-start.8 = (bf16[64,512]{1,0:T(8,128)(2,1)S(1)}, bf16[64,512]{1,0:T(8,128)(2,1)S(1)}, u32[]{:S(2)}, u32[]{:S(2)}) collective-permute-start(bf16[64,512]{1,0:T(8,128)(2,1)S(1)} %get-tuple-element.39), channel_id=1, source_target_pairs={{0,1},{1,0},{2,3},{3,2},{4,5},{5,4},{6,7},{7,6},{8,9},{9,8},{10,11... | collective-permute-start | bytes 196616 | tf_op jit(solution)/shard_map/ppermute | solution.py:71
  31.2 1.8 %collective-permute-start.9 = (bf16[64,512]{1,0:T(8,128)(2,1)S(1)}, bf16[64,512]{1,0:T(8,128)(2,1)S(1)}, u32[]{:S(2)}, u32[]{:S(2)}) collective-permute-start(bf16[64,512]{1,0:T(8,128)(2,1)S(1)} %get-tuple-element.40), channel_id=1, source_target_pairs={{0,1},{1,0},{2,3},{3,2},{4,5},{5,4},{6,7},{7,6},{8,9},{9,8},{10,11... | collective-permute-start | bytes 196616 | tf_op jit(solution)/shard_map/ppermute | solution.py:71
  31.6 13.8 %slice-start.1 = ((s8[4718592]{0:T(1024)(128)(4,1)}), s8[4194304]{0:T(1024)(128)(4,1)S(1)}, s32[]{:S(2)}) async-start(s8[4718592]{0:T(1024)(128)(4,1)} %bitcast.2), calls=%async_computation.1 | async-start | bytes 8388608
  33.2 1.6 %collective-permute-start.15 = (bf16[2,64,512]{2,1,0:T(8,128)(2,1)S(1)}, bf16[2,64,512]{2,1,0:T(8,128)(2,1)S(1)}, u32[]{:S(2)}, u32[]{:S(2)}) collective-permute-start(bf16[2,64,512]{2,1,0:T(8,128)(2,1)S(1)} %shard_map.46.own), channel_id=1, source_target_pairs={{0,1},{1,0},{2,3},{3,2},{4,5},{5,4},{6,7},{7,6},{8,9},{9,8},{10,11... | collective-permute-start | bytes 393224 | tf_op jit(solution)/shard_map/ppermute | solution.py:71
  33.3 5.9 %collective-permute-start.10 = (bf16[2,64,512]{2,1,0:T(8,128)(2,1)S(1)}, bf16[2,64,512]{2,1,0:T(8,128)(2,1)S(1)}, u32[]{:S(2)}, u32[]{:S(2)}) collective-permute-start(bf16[2,64,512]{2,1,0:T(8,128)(2,1)S(1)} %get-tuple-element.42), channel_id=1, source_target_pairs={{0,2},{1,3},{2,0},{3,1},{4,6},{5,7},{6,4},{7,5},{8,10},{9,11},{10,... | collective-permute-start | bytes 393224 | tf_op jit(solution)/shard_map/ppermute | solution.py:71
  34.9 10.5 %collective-permute-start.16 = (bf16[2,2,64,512]{3,2,1,0:T(8,128)(2,1)S(1)}, bf16[2,2,64,512]{3,2,1,0:T(8,128)(2,1)S(1)}, u32[]{:S(2)}, u32[]{:S(2)}) collective-permute-start(bf16[2,2,64,512]{3,2,1,0:T(8,128)(2,1)S(1)} %shard_map.47), channel_id=1, source_target_pairs={{2,0},{6,1},{10,2},{14,3},{0,4},{4,5},{8,6},{12,7},{3,8},{7,9},{11... | collective-permute-start | bytes 786440 | tf_op jit(solution)/shard_map/ppermute | solution.py:62
  35.3 10.1 %collective-permute-start.17 = (bf16[2,2,64,512]{3,2,1,0:T(8,128)(2,1)S(1)}, bf16[2,2,64,512]{3,2,1,0:T(8,128)(2,1)S(1)}, u32[]{:S(2)}, u32[]{:S(2)}) collective-permute-start(bf16[2,2,64,512]{3,2,1,0:T(8,128)(2,1)S(1)} %shard_map.47), channel_id=1, source_target_pairs={{0,0},{4,1},{8,2},{12,3},{2,4},{6,5},{10,6},{14,7},{1,8},{5,9},{9,... | collective-permute-start | bytes 786440 | tf_op jit(solution)/shard_map/ppermute | solution.py:62
  39.3 1.5 %collective-permute-start.11 = (bf16[2,64,512]{2,1,0:T(8,128)(2,1)S(1)}, bf16[2,64,512]{2,1,0:T(8,128)(2,1)S(1)}, u32[]{:S(2)}, u32[]{:S(2)}) collective-permute-start(bf16[2,64,512]{2,1,0:T(8,128)(2,1)S(1)} %shard_map.44.own), channel_id=1, source_target_pairs={{0,1},{1,0},{2,3},{3,2},{4,5},{5,4},{6,7},{7,6},{8,9},{9,8},{10,11... | collective-permute-start | bytes 393224 | tf_op jit(solution)/shard_map/ppermute | solution.py:71
  40.8 16.3 %collective-permute-start.12 = (bf16[2,2,64,512]{3,2,1,0:T(8,128)(2,1)S(1)}, bf16[2,2,64,512]{3,2,1,0:T(8,128)(2,1)S(1)}, u32[]{:S(2)}, u32[]{:S(2)}) collective-permute-start(bf16[2,2,64,512]{3,2,1,0:T(8,128)(2,1)S(1)} %shard_map.45), channel_id=1, source_target_pairs={{2,0},{4,1},{10,2},{12,3},{0,4},{6,5},{8,6},{14,7},{3,8},{5,9},{11... | collective-permute-start | bytes 786440 | tf_op jit(solution)/shard_map/ppermute | solution.py:62
  44.7 13.9 %collective-permute-start.13 = (bf16[2,2,64,512]{3,2,1,0:T(8,128)(2,1)S(1)}, bf16[2,2,64,512]{3,2,1,0:T(8,128)(2,1)S(1)}, u32[]{:S(2)}, u32[]{:S(2)}) collective-permute-start(bf16[2,2,64,512]{3,2,1,0:T(8,128)(2,1)S(1)} %shard_map.45), channel_id=1, source_target_pairs={{0,0},{6,1},{8,2},{14,3},{2,4},{4,5},{10,6},{12,7},{1,8},{7,9},{9,... | collective-permute-start | bytes 786440 | tf_op jit(solution)/shard_map/ppermute | solution.py:62
  46.9 10.2 %collective-permute-start.18 = (bf16[128,512]{1,0:T(8,128)(2,1)S(1)}, bf16[128,512]{1,0:T(8,128)(2,1)S(1)}, u32[]{:S(2)}, u32[]{:S(2)}) collective-permute-start(bf16[128,512]{1,0:T(8,128)(2,1)S(1)} %get-tuple-element.48), channel_id=1, source_target_pairs={{0,1},{1,0},{2,3},{3,2},{4,5},{5,4},{6,7},{7,6},{8,9},{9,8},{10,11... | collective-permute-start | bytes 393224 | tf_op jit(solution)/shard_map/ppermute | solution.py:71
  55.0 2.0 %collective-permute-start.19 = (bf16[128,512]{1,0:T(8,128)(2,1)S(1)}, bf16[128,512]{1,0:T(8,128)(2,1)S(1)}, u32[]{:S(2)}, u32[]{:S(2)}) collective-permute-start(bf16[128,512]{1,0:T(8,128)(2,1)S(1)} %get-tuple-element.49), channel_id=1, source_target_pairs={{0,1},{1,0},{2,3},{3,2},{4,5},{5,4},{6,7},{7,6},{8,9},{9,8},{10,11... | collective-permute-start | bytes 393224 | tf_op jit(solution)/shard_map/ppermute | solution.py:71
  56.5 7.6 %collective-permute-start.21 = (bf16[256,512]{1,0:T(8,128)(2,1)S(1)}, bf16[256,512]{1,0:T(8,128)(2,1)S(1)}, u32[]{:S(2)}, u32[]{:S(2)}) collective-permute-start(bf16[256,512]{1,0:T(8,128)(2,1)S(1)} %shard_map.48), channel_id=1, source_target_pairs={{0,1},{1,0},{2,3},{3,2},{4,5},{5,4},{6,7},{7,6},{8,9},{9,8},{10,11... | collective-permute-start | bytes 786440 | tf_op jit(solution)/shard_map/ppermute | solution.py:71
  57.9 6.2 %collective-permute-start.20 = (bf16[112,512]{1,0:T(8,128)(2,1)S(1)}, bf16[112,512]{1,0:T(8,128)(2,1)S(1)}, u32[]{:S(2)}, u32[]{:S(2)}) collective-permute-start(bf16[112,512]{1,0:T(8,128)(2,1)S(1)} %shard_map.50), channel_id=1, source_target_pairs={{0,2},{1,3},{2,0},{3,1},{4,6},{5,7},{6,4},{7,5},{8,10},{9,11},{10,... | collective-permute-start | bytes 344072 | tf_op jit(solution)/shard_map/ppermute | solution.py:71
  59.6 7.7 %collective-permute-start.22 = (bf16[144,512]{1,0:T(8,128)(2,1)S(1)}, bf16[144,512]{1,0:T(8,128)(2,1)S(1)}, u32[]{:S(2)}, u32[]{:S(2)}) collective-permute-start(bf16[144,512]{1,0:T(8,128)(2,1)S(1)} %shard_map.51), channel_id=1, source_target_pairs={{0,2},{1,3},{2,0},{3,1},{4,6},{5,7},{6,4},{7,5},{8,10},{9,11},{10,... | collective-permute-start | bytes 442376 | tf_op jit(solution)/shard_map/ppermute | solution.py:71
